TPU v7x, 32 devices: a whole 2x2x4 slice. The times are simulated.
32 devices in a mesh: batch: 8 (over z, x), section: 4 (over y, core).
Axes of the slice: x: 2, y: 2, z: 4, core: 2. Of those that a mesh axis runs over, the one named last changes fastest.
Arguments:
- stem_input: float32 [64, 576, 1024], P(('batch', 'section')), may hold values from -6 to 6
- image_class: int32 [64], P(('batch', 'section')), may hold values 0 or 1
- owner: int32 [64], P('batch'), may hold values from 0 to 3, as said below
- conv_in_weight: bfloat16 [1024, 256], replicated, may hold values from -0.1875 to 0.1875
- first_gain: float32 [256], replicated, may hold values from 0.5 to 1.5
- first_bias: float32 [256], replicated, may hold values from -1.75 to 1.75
- conv_mid_weight: bfloat16 [9, 256, 256], replicated, may hold values from -0.125 to 0.125
- second_gain: float32 [256], replicated, may hold values from 0.5 to 1.5
- second_bias: float32 [256], replicated, may hold values from -1.75 to 1.75
- conv_out_weight: bfloat16 [256, 1024], replicated, may hold values from -0.375 to 0.375
- third_gain: float32 [1024], replicated, may hold values from 0.5 to 1.5
- third_bias: float32 [1024], replicated, may hold values from -1.75 to 1.75
- embed_weight: bfloat16 [1024, 768], replicated, may hold values from -0.1875 to 0.1875
- embed_bias: float32 [768], replicated, may hold values from -3 to 3
- position_table: bfloat16 [576, 768], replicated, may hold values from -3 to 3
- attn_gain: float32 [768], replicated, may hold values from 0.5 to 1.5
- attn_bias: float32 [768], replicated, may hold values from -1.75 to 1.75
- joint_weight: bfloat16 [768, 2304], replicated, may hold values from -0.21875 to 0.21875
- query_bias: float32 [768], replicated, may hold values from -3 to 3
- value_bias: float32 [768], replicated, may hold values from -3 to 3
- mix_weight: bfloat16 [768, 768], replicated, may hold values from -0.875 to 0.875
- mix_bias: float32 [768], replicated, may hold values from -1.75 to 1.75
- mlp_gain: float32 [768], replicated, may hold values from 0.5 to 1.5
- mlp_bias: float32 [768], replicated, may hold values from -1.75 to 1.75
- expand_weight: bfloat16 [768, 3072], replicated, may hold values from -0.21875 to 0.21875
- expand_bias: float32 [3072], replicated, may hold values from -3 to 3
- shrink_weight: bfloat16 [3072, 768], replicated, may hold values from -0.109375 to 0.109375
- shrink_bias: float32 [768], replicated, may hold values from -1.75 to 1.75
- cotangent: bfloat16 [32, 4, 576, 768], P(('batch', 'section')), may hold values from -6 to 6
Outputs:
- block_output: bfloat16 [32, 4, 576, 768], P(('batch', 'section'))
- input_grad: float32 [64, 576, 1024], P(('batch', 'section'))
- grad_conv_in: float32 [262144], P(('batch', 'section'))
- grad_first_gain: float32 [256], replicated
- grad_first_bias: float32 [256], replicated
- grad_conv_mid: float32 [589824], P(('batch', 'section'))
- grad_second_gain: float32 [256], replicated
- grad_second_bias: float32 [256], replicated
- grad_conv_out: float32 [262144], P(('batch', 'section'))
- grad_third_gain: float32 [1024], replicated
- grad_third_bias: float32 [1024], replicated
- grad_embed_weight: float32 [786432], P(('batch', 'section'))
- grad_embed_bias: float32 [768], replicated
- grad_position_table: float32 [442368], P(('batch', 'section'))
- grad_attn_gain: float32 [768], replicated
- grad_attn_bias: float32 [768], replicated
- grad_joint_weight: float32 [1769472], P(('batch', 'section'))
- grad_query_bias: float32 [768], replicated
- grad_value_bias: float32 [768], replicated
- grad_mix_weight: float32 [589824], P(('batch', 'section'))
- grad_mix_bias: float32 [768], replicated
- grad_mlp_gain: float32 [768], replicated
- grad_mlp_bias: float32 [768], replicated
- grad_expand_weight: float32 [2359296], P(('batch', 'section'))
- grad_expand_bias: float32 [3072], replicated
- grad_shrink_weight: float32 [2359296], P(('batch', 'section'))
- grad_shrink_bias: float32 [768], replicated
Inputs may be any that keep to these rules, and one draw needn't show every extreme that they name: `image_class`: 1 marks an image of 24 x 24 patches, 0 one of 14 x 14 patches in the grid's top-left corner; the other cells are padding. `owner`: entry b * 4 * 2 + s * 2 + j is the section index that runs the block of image j of section index s at batch index b. Within one batch index every section index is named exactly 2 times, and one section index names the same section index at most 1 times, exactly 1 times for some pair.
All inputs are finite; a program needn't handle non-finite values. No bound on the sum of `image_class` on one device may be relied on, other than what follows from the above.
Results may differ from a plain program's by a relative error of at most 0.017.
The roundings to bfloat16 on the way count: a program that leaves them out, or rounds other values in their place, can miss the bound.
Values may be sent and summed in bfloat16 or wider, within the bound.
No kernel may reach another device: no remote copies, remote signals or barrier semaphores. Data moves between devices by JAX's collectives and lax.ppermute only.
A program may use at most 320 MiB of HBM per device.

v0:
```python
import jax
import jax.numpy as jnp
from jax import lax
from jax.sharding import PartitionSpec as P

HEADS = 12
GROUPS = 32
SIDE = 24
SIDE_SMALL = 14


def cell_validity(image_class):
    grid_cells = jnp.arange(SIDE * SIDE, dtype=jnp.int32)
    corner = (grid_cells // SIDE < SIDE_SMALL) & (grid_cells % SIDE < SIDE_SMALL)
    return jnp.where((image_class[:, None] == 1) | corner[None, :], 1.0, 0.0).astype(jnp.float32)


def standardize(weight):
    lead_axes = tuple(range(weight.ndim - 1))
    centred = weight - jnp.mean(weight, axis=lead_axes, keepdims=True)
    spread = jnp.mean(centred * centred, axis=lead_axes, keepdims=True)
    return centred * lax.rsqrt(spread + 1e-05)


def group_norm(values, gain, bias, validity):
    images, grid_cells, channels = values.shape
    per_group = channels // GROUPS
    grouped = values.reshape(images, grid_cells, GROUPS, per_group)
    weights = validity[:, :, None, None]
    total = jnp.sum(weights, axis=(1, 3), keepdims=True) * per_group
    centre = jnp.sum(grouped * weights, axis=(1, 3), keepdims=True) / total
    centred = (grouped - centre) * weights
    spread = jnp.sum(centred * centred, axis=(1, 3), keepdims=True) / total
    normed = ((grouped - centre) * lax.rsqrt(spread + 1e-05)).reshape(images, grid_cells, channels)
    return normed * gain + bias


def layer_norm(values, gain, bias):
    centre = jnp.mean(values, axis=-1, keepdims=True)
    centred = values - centre
    spread = jnp.mean(centred * centred, axis=-1, keepdims=True)
    return centred * lax.rsqrt(spread + 1e-06) * gain + bias


def neighbours(values):
    images, grid_cells, channels = values.shape
    grid = values.reshape(images, SIDE, SIDE, channels)
    padded = jnp.pad(grid, ((0, 0), (1, 1), (1, 1), (0, 0)))
    pieces = [
        padded[:, row_shift : row_shift + SIDE, col_shift : col_shift + SIDE, :]
        for row_shift in range(3)
        for col_shift in range(3)
    ]
    return jnp.concatenate(pieces, axis=-1).reshape(images, grid_cells, 9 * channels)


def gelu_exact(values):
    return jax.nn.gelu(values, approximate=False)


def product(left, right):
    return jnp.dot(left, right, preferred_element_type=jnp.float32)


def left_product(left, right):
    return lax.dot_general(
        left, right, (((0,), (0,)), ((), ())), preferred_element_type=jnp.float32
    )


def right_product(left, right):
    return lax.dot_general(
        left, right, (((1,), (1,)), ((), ())), preferred_element_type=jnp.float32
    )


def split_heads(rows):
    grid_cells, model_width = rows.shape
    return rows.reshape(grid_cells, HEADS, model_width // HEADS)


def masked_scores(query_heads, key_heads, validity):
    head_size = query_heads.shape[2]
    scores = jnp.einsum(
        "qhd,khd->hqk", query_heads, key_heads, preferred_element_type=jnp.float32
    ) * head_size ** (-0.5)
    return jnp.where(validity[None, None, :] > 0, scores, -1000000000.0)


def attend_forward(packed):
    query, key_rows, value_rows, validity = packed
    grid_cells, model_width = query.shape
    scores = masked_scores(split_heads(query), split_heads(key_rows), validity)
    top = jnp.max(scores, axis=-1, keepdims=True)
    weights = jnp.exp(scores - top)
    total = jnp.sum(weights, axis=-1, keepdims=True)
    probs = (weights / total).astype(jnp.bfloat16)
    mixed = jnp.einsum(
        "hqk,khd->qhd", probs, split_heads(value_rows), preferred_element_type=jnp.float32
    )
    return (mixed.reshape(grid_cells, model_width), (top + jnp.log(total))[:, :, 0])


def attend_backward(packed):
    query, key_rows, value_rows, validity, log_total, grad_mixed = packed
    grid_cells, model_width = query.shape
    query_heads = split_heads(query)
    key_heads = split_heads(key_rows)
    value_heads = split_heads(value_rows)
    grad_heads = split_heads(grad_mixed)
    scale = (model_width // HEADS) ** (-0.5)
    probs = jnp.exp(masked_scores(query_heads, key_heads, validity) - log_total[:, :, None])
    probs_low = probs.astype(jnp.bfloat16)
    grad_probs = jnp.einsum(
        "qhd,khd->hqk", grad_heads, value_heads, preferred_element_type=jnp.float32
    )
    inner = jnp.sum(probs * grad_probs, axis=-1, keepdims=True)
    grad_scores = (probs * (grad_probs - inner)).astype(jnp.bfloat16)
    grad_value = jnp.einsum(
        "hqk,qhd->khd", probs_low, grad_heads, preferred_element_type=jnp.float32
    )
    grad_query = (
        jnp.einsum("hqk,khd->qhd", grad_scores, key_heads, preferred_element_type=jnp.float32)
        * scale
    )
    grad_key = (
        jnp.einsum("hqk,qhd->khd", grad_scores, query_heads, preferred_element_type=jnp.float32)
        * scale
    )
    return jnp.concatenate(
        [
            grad_query.reshape(grid_cells, model_width),
            grad_key.reshape(grid_cells, model_width),
            grad_value.reshape(grid_cells, model_width),
        ],
        axis=-1,
    )


def block_sums(block_terms):
    attention_part = (
        lax.psum_scatter(
            block_terms[0].reshape(-1), ("batch", "section"), scatter_dimension=0, tiled=True
        ),
        lax.psum_scatter(
            block_terms[1].reshape(-1), ("batch", "section"), scatter_dimension=0, tiled=True
        ),
    )
    feed_part = (
        lax.psum_scatter(
            block_terms[2].reshape(-1), ("batch", "section"), scatter_dimension=0, tiled=True
        ),
        lax.psum_scatter(
            block_terms[3].reshape(-1), ("batch", "section"), scatter_dimension=0, tiled=True
        ),
    )
    return (attention_part[0], attention_part[1], feed_part[0], feed_part[1])


def shards(
    stem_input,
    image_class,
    owner,
    conv_in_weight,
    first_gain,
    first_bias,
    conv_mid_weight,
    second_gain,
    second_bias,
    conv_out_weight,
    third_gain,
    third_bias,
    embed_weight,
    embed_bias,
    position_table,
    attn_gain,
    attn_bias,
    joint_weight,
    query_bias,
    value_bias,
    mix_weight,
    mix_bias,
    mlp_gain,
    mlp_bias,
    expand_weight,
    expand_bias,
    shrink_weight,
    shrink_bias,
    cotangent,
):
    sections = lax.axis_size("section")
    images, grid_cells, channels = stem_input.shape
    middle = conv_in_weight.shape[1]
    model_width = embed_weight.shape[1]
    slot_count = cotangent.shape[1]
    capacity = slot_count // sections
    flat_rows = images * grid_cells
    validity = cell_validity(image_class)
    keep_cells = validity[:, :, None]
    keep_rows = validity.reshape(flat_rows, 1)
    inputs = stem_input * keep_cells
    inputs_low = inputs.astype(jnp.bfloat16).reshape(flat_rows, channels)
    std_in, back_std_in = jax.vjp(standardize, conv_in_weight.astype(jnp.float32))
    std_mid, back_std_mid = jax.vjp(standardize, conv_mid_weight.astype(jnp.float32))
    std_out, back_std_out = jax.vjp(standardize, conv_out_weight.astype(jnp.float32))
    in_low = std_in.astype(jnp.bfloat16)
    mid_low = std_mid.astype(jnp.bfloat16).reshape(9 * middle, middle)
    out_low = std_out.astype(jnp.bfloat16)

    def norm_gelu(values, gain, bias):
        return gelu_exact(group_norm(values, gain, bias, validity)) * keep_cells

    def norm_residual(residual, values, gain, bias):
        return gelu_exact(residual + group_norm(values, gain, bias, validity)) * keep_cells

    first = product(inputs_low, in_low).reshape(images, grid_cells, middle)
    act_one, back_first = jax.vjp(norm_gelu, first, first_gain, first_bias)
    columns = neighbours(act_one.astype(jnp.bfloat16)).reshape(flat_rows, 9 * middle)
    second = product(columns, mid_low).reshape(images, grid_cells, middle)
    act_two, back_second = jax.vjp(norm_gelu, second, second_gain, second_bias)
    act_two_low = act_two.astype(jnp.bfloat16).reshape(flat_rows, middle)
    third = product(act_two_low, out_low).reshape(images, grid_cells, channels)
    stem, back_third = jax.vjp(norm_residual, inputs, third, third_gain, third_bias)
    stem_low = stem.astype(jnp.bfloat16).reshape(flat_rows, channels)
    tokens = (
        product(stem_low, embed_weight).reshape(images, grid_cells, model_width)
        + embed_bias
        + position_table.astype(jnp.float32)[None]
    ) * keep_cells
    tokens_low = tokens.astype(jnp.bfloat16)
    group_owner = owner.reshape(sections, images)
    section_index = lax.axis_index("section")
    mine = lax.dynamic_index_in_dim(group_owner, section_index, 0, keepdims=False)
    local_index = jnp.arange(images, dtype=jnp.int32)
    rank = jnp.sum(
        (mine[None, :] == mine[:, None]) & (local_index[None, :] < local_index[:, None]), axis=1
    )
    send_slot = mine * capacity + rank
    slot_ids = jnp.arange(slot_count, dtype=jnp.int32)
    hits = send_slot[None, :] == slot_ids[:, None]
    filled = jnp.any(hits, axis=1)
    source_of = jnp.sum(jnp.where(hits, local_index[None, :], 0), axis=1)
    outgoing = jnp.where(filled[:, None, None], tokens_low[source_of], jnp.zeros((), jnp.bfloat16))
    out_flags = jnp.where(filled, image_class[source_of] + 1, 0).astype(jnp.bfloat16)
    incoming, in_flags = (
        lax.all_to_all(outgoing, "section", split_axis=0, concat_axis=0, tiled=True),
        lax.all_to_all(out_flags, "section", split_axis=0, concat_axis=0, tiled=True),
    )
    per_source = jnp.sum(group_owner == section_index, axis=1)
    arrived = slot_ids % capacity < per_source[slot_ids // capacity]
    order = jnp.nonzero(arrived, size=images)[0].astype(jnp.int32)
    block_class = (in_flags[order].astype(jnp.float32) > 1.5).astype(jnp.int32)
    block_valid = cell_validity(block_class)
    block_keep = block_valid.reshape(flat_rows, 1)
    resid_zero = incoming[order].astype(jnp.float32).reshape(flat_rows, model_width)
    normed, back_norm_one = jax.vjp(layer_norm, resid_zero, attn_gain, attn_bias)
    normed_low = normed.astype(jnp.bfloat16)
    joint = product(normed_low, joint_weight)
    query = (
        (joint[:, :model_width] + query_bias)
        .astype(jnp.bfloat16)
        .reshape(images, grid_cells, model_width)
    )
    key_rows = (
        joint[:, model_width : 2 * model_width]
        .astype(jnp.bfloat16)
        .reshape(images, grid_cells, model_width)
    )
    value_rows = (
        (joint[:, 2 * model_width :] + value_bias)
        .astype(jnp.bfloat16)
        .reshape(images, grid_cells, model_width)
    )
    mixed, log_total = lax.map(attend_forward, (query, key_rows, value_rows, block_valid))
    mixed_low = mixed.reshape(flat_rows, model_width).astype(jnp.bfloat16)
    resid_one = resid_zero + product(mixed_low, mix_weight) + mix_bias
    normed_two, back_norm_two = jax.vjp(layer_norm, resid_one, mlp_gain, mlp_bias)
    normed_two_low = normed_two.astype(jnp.bfloat16)
    hidden, back_gelu = jax.vjp(gelu_exact, product(normed_two_low, expand_weight) + expand_bias)
    hidden_low = hidden.astype(jnp.bfloat16)
    final = (resid_one + product(hidden_low, shrink_weight) + shrink_bias) * block_keep
    block_rows = final.astype(jnp.bfloat16).reshape(images, grid_cells, model_width)
    block_output = (
        jnp.zeros((slot_count, grid_cells, model_width), jnp.bfloat16)
        .at[order]
        .set(block_rows)[None]
    )
    grad_final = (
        cotangent[0][order].astype(jnp.float32).reshape(flat_rows, model_width) * block_keep
    )
    grad_shrink_bias = jnp.sum(grad_final, axis=0)
    grad_final_low = grad_final.astype(jnp.bfloat16)
    grad_shrink = left_product(hidden_low, grad_final_low)
    (grad_pre,) = back_gelu(right_product(grad_final_low, shrink_weight))
    grad_expand_bias = jnp.sum(grad_pre, axis=0)
    grad_pre_low = grad_pre.astype(jnp.bfloat16)
    grad_expand = left_product(normed_two_low, grad_pre_low)
    grad_resid_norm, grad_mlp_gain, grad_mlp_bias = back_norm_two(
        right_product(grad_pre_low, expand_weight)
    )
    grad_resid = grad_final + grad_resid_norm
    grad_mix_bias = jnp.sum(grad_resid, axis=0)
    grad_resid_low = grad_resid.astype(jnp.bfloat16)
    grad_mix = left_product(mixed_low, grad_resid_low)
    grad_mixed_low = (
        right_product(grad_resid_low, mix_weight)
        .astype(jnp.bfloat16)
        .reshape(images, grid_cells, model_width)
    )
    grad_joint = lax.map(
        attend_backward, (query, key_rows, value_rows, block_valid, log_total, grad_mixed_low)
    ).reshape(flat_rows, 3 * model_width)
    grad_query_bias = jnp.sum(grad_joint[:, :model_width], axis=0)
    grad_value_bias = jnp.sum(grad_joint[:, 2 * model_width :], axis=0)
    grad_joint_low = grad_joint.astype(jnp.bfloat16)
    grad_joint_weight = left_product(normed_low, grad_joint_low)
    grad_zero_norm, grad_attn_gain, grad_attn_bias = back_norm_one(
        right_product(grad_joint_low, joint_weight)
    )
    grad_tokens = (
        (grad_resid + grad_zero_norm).astype(jnp.bfloat16).reshape(images, grid_cells, model_width)
    )
    block_terms = (grad_joint_weight, grad_mix, grad_expand, grad_shrink)
    block_summed = block_terms
    returning = (
        jnp.zeros((slot_count, grid_cells, model_width), jnp.bfloat16).at[order].set(grad_tokens)
    )
    came_back = lax.all_to_all(returning, "section", split_axis=0, concat_axis=0, tiled=True)
    grad_embed_out = (
        came_back[send_slot].astype(jnp.float32).reshape(flat_rows, model_width) * keep_rows
    )
    grad_embed_bias = jnp.sum(grad_embed_out, axis=0)
    grad_position = jnp.sum(grad_embed_out.reshape(images, grid_cells, model_width), axis=0)
    grad_embed_low = grad_embed_out.astype(jnp.bfloat16)
    grad_embed = left_product(stem_low, grad_embed_low)
    grad_stem = right_product(grad_embed_low, embed_weight).reshape(images, grid_cells, channels)
    grad_inputs_res, grad_third, grad_third_gain, grad_third_bias = back_third(grad_stem)
    grad_third_low = grad_third.astype(jnp.bfloat16).reshape(flat_rows, channels)
    grad_std_out = left_product(act_two_low, grad_third_low)
    grad_act_two = right_product(grad_third_low, out_low).reshape(images, grid_cells, middle)
    grad_second, grad_second_gain, grad_second_bias = back_second(grad_act_two)
    grad_second_low = grad_second.astype(jnp.bfloat16).reshape(flat_rows, middle)
    grad_std_mid = left_product(columns, grad_second_low).reshape(9, middle, middle)
    grad_columns = right_product(grad_second_low, mid_low).reshape(images, grid_cells, 9 * middle)
    _, spread_back = jax.vjp(neighbours, jnp.zeros((images, grid_cells, middle), jnp.float32))
    (grad_act_one,) = spread_back(grad_columns)
    grad_first, grad_first_gain, grad_first_bias = back_first(grad_act_one)
    grad_first_low = grad_first.astype(jnp.bfloat16).reshape(flat_rows, middle)
    grad_std_in = left_product(inputs_low, grad_first_low)
    input_grad = (
        grad_inputs_res
        + right_product(grad_first_low, in_low).reshape(images, grid_cells, channels)
    ) * keep_cells
    (grad_conv_in,) = back_std_in(grad_std_in)
    (grad_conv_mid,) = back_std_mid(grad_std_mid)
    (grad_conv_out,) = back_std_out(grad_std_out)
    stem_summed = (
        lax.psum_scatter(
            grad_conv_in.reshape(-1), ("batch", "section"), scatter_dimension=0, tiled=True
        ),
        lax.psum_scatter(
            grad_conv_mid.reshape(-1), ("batch", "section"), scatter_dimension=0, tiled=True
        ),
        lax.psum_scatter(
            grad_conv_out.reshape(-1), ("batch", "section"), scatter_dimension=0, tiled=True
        ),
        lax.psum_scatter(
            grad_embed.reshape(-1), ("batch", "section"), scatter_dimension=0, tiled=True
        ),
        lax.psum_scatter(
            grad_position.reshape(-1), ("batch", "section"), scatter_dimension=0, tiled=True
        ),
    )
    block_summed = block_sums(block_summed)
    small_summed = lax.psum(
        (
            grad_first_gain,
            grad_first_bias,
            grad_second_gain,
            grad_second_bias,
            grad_third_gain,
            grad_third_bias,
            grad_embed_bias,
            grad_attn_gain,
            grad_attn_bias,
            grad_query_bias,
            grad_value_bias,
            grad_mix_bias,
            grad_mlp_gain,
            grad_mlp_bias,
            grad_expand_bias,
            grad_shrink_bias,
        ),
        ("batch", "section"),
    )
    return (
        block_output,
        input_grad,
        stem_summed[0],
        small_summed[0],
        small_summed[1],
        stem_summed[1],
        small_summed[2],
        small_summed[3],
        stem_summed[2],
        small_summed[4],
        small_summed[5],
        stem_summed[3],
        small_summed[6],
        stem_summed[4],
        small_summed[7],
        small_summed[8],
        block_summed[0],
        small_summed[9],
        small_summed[10],
        block_summed[1],
        small_summed[11],
        small_summed[12],
        small_summed[13],
        block_summed[2],
        small_summed[14],
        block_summed[3],
        small_summed[15],
    )


def solution(mesh):
    in_specs = (
        P(("batch", "section"), None, None),
        P(("batch", "section")),
        P("batch"),
        P(),
        P(),
        P(),
        P(),
        P(),
        P(),
        P(),
        P(),
        P(),
        P(),
        P(),
        P(),
        P(),
        P(),
        P(),
        P(),
        P(),
        P(),
        P(),
        P(),
        P(),
        P(),
        P(),
        P(),
        P(),
        P(("batch", "section"), None, None, None),
    )
    out_specs = (
        P(("batch", "section"), None, None, None),
        P(("batch", "section"), None, None),
        P(("batch", "section")),
        P(),
        P(),
        P(("batch", "section")),
        P(),
        P(),
        P(("batch", "section")),
        P(),
        P(),
        P(("batch", "section")),
        P(),
        P(("batch", "section")),
        P(),
        P(),
        P(("batch", "section")),
        P(),
        P(),
        P(("batch", "section")),
        P(),
        P(),
        P(),
        P(("batch", "section")),
        P(),
        P(("batch", "section")),
        P(),
    )
    return jax.shard_map(shards, mesh=mesh, in_specs=in_specs, out_specs=out_specs, check_vma=False)
```

profile of v0, /device:TPU:0, one launch (start us, length us, event | category | flops | bytes accessed | tf_op | source)
XLA Modules:
  0.0 1363.9 jit_solution(14386833629070398058)
XLA Ops:
  13.1 4.2 all-to-all-start.1
  78.0 5.3 reshape.1244
  83.3 5.4 copy.432
  112.2 4.4 multiply_reduce_fusion.17
  117.6 4.2 fusion.81
  128.1 5.7 copy.442
  133.8 14.3 %multiply_convert_fusion.2 = (bf16[2,576,1024]{2,1,0:T(8,128)(2,1)S(1)}, f32[2,576,1024]{2,1,0:T(8,128)}, f32[2,576,1024]{2,1,0:T(8,128)}) fusion(f32[2,576]{1,0:T(2,128)S(1)} %get-tuple-element.347, f32[1024]{0:T(1024)} %param.44, f32[2,576,1024]{2,1,0:T(8,128)} %copy.442, f32[1024]{0:T(1024)} %param.43, f32[2,576,1024]{2,1,0:T(8,128)} %param.33), kind=kLoop, calls=%fused_computation.80 | loop fusion | flops 82575360 | bytes 21246464 | tf_op jit(solution)/shard_map/convert_element_type | solution.py:224
  152.9 4.2 gather_fusion.1
  157.1 4.1 broadcast_select_fusion
  161.2 5.1 all-to-all-start
  198.3 8.6 copy.473
  224.6 4.4 fusion.235
  244.7 74.3 %while.22 = (s32[]{:T(128)}, bf16[2,576,768]{2,1,0:T(8,128)(2,1)}, f32[2,12,576]{2,1,0:T(8,128)}, bf16[2,576,768]{1,2,0:T(8,128)(2,1)}, f32[2,576]{1,0:T(2,128)S...) while((s32[]{:T(128)}, bf16[2,576,768]{2,1,0:T(8,128)(2,1)}, ...), condition=%wide.region_26.27_spmd, body=%wide.region_23.26_spmd.sunk | while | flops 1066985280 | bytes 60650136 | solution.py:274
  246.6 8.7 fusion.295
  255.2 10.3 fusion.296
  268.4 9.2 fusion.297
  283.7 8.7 fusion.295
  292.4 10.3 fusion.296
  305.5 9.2 fusion.297
  319.1 4.2 fusion.232
  325.1 40.0 %multiply_convert_fusion.1 = (bf16[1152,3072]{1,0:T(8,128)(2,1)}, f32[1152,3072]{1,0:T(8,128)}, f32[1152,3072]{1,0:T(8,128)}) fusion(f32[3072]{0:T(1024)S(1)} %copy-done.154, bf16[768,3072]{1,0:T(8,128)(2,1)S(1)} %copy-done.149, f32[1152,768]{1,0:T(8,128)S(1)} %get-tuple-element.357, f32[768]{0:T(1024)S(1)} %copy-done.157, f32[768]{0:T(1024)S(1)} %copy-done.132, ...), kind=kOutput, calls=%fused_computation.45 | convolution fusion | flops 5673811968 | bytes 43674624 | tf_op jit(solution)/shard_map/dot_general | solution.py:62
  365.2 20.4 %fusion.233 = (f32[3072]{0:T(1024)}, bf16[1152,3072]{1,0:T(8,128)(2,1)}) fusion(f32[1152,3072]{1,0:T(8,128)} %get-tuple-element.299, f32[1152,3072]{1,0:T(8,128)} %get-tuple-element.358, bf16[1152,768]{1,0:T(8,128)(2,1)} %fusion.50, bf16[3072,768]{1,0:T(8,128)(2,1)} %param.59), kind=kOutput, calls=%fused_computation.512 | convolution fusion | flops 5488899072 | bytes 41889792 | tf_op jit(solution)/shard_map/dot_general | solution.py:72
  385.6 13.0 fusion.46
  398.7 7.2 multiply_reduce_fusion.7
  411.4 122.0 %while.23 = (s32[]{:T(128)}, f32[2,576,2304]{1,2,0:T(8,128)}, bf16[2,576,768]{1,2,0:T(8,128)(2,1)}, f32[2,576]{1,0:T(2,128)S(1)}, bf16[2,576,768]{1,2,0:T(8,128)...) while((s32[]{:T(128)}, f32[2,576,2304]{1,2,0:T(8,128)}, ...), condition=%wide.region_34.35_spmd, body=%wide.region_32.34_spmd.sunk | while | flops 2611291904 | bytes 183376240 | solution.py:310
  414.5 7.4 fusion.308
  425.8 18.2 %multiply_reduce_fusion.24 = (f32[12,576]{1,0:T(8,128)S(1)}, f32[12,576,576]{1,2,0:T(8,128)}) fusion(f32[12,576,576]{1,2,0:T(8,128)} %fusion.308, f32[12,576]{1,0:T(8,128)} %dynamic-slice_bitcast_fusion.2, pred[576]{0:T(1024)(128)(4,1)S(1)} %compare_reduce_fusion.5, bf16[576,12,64]{0,2,1:T(8,128)(2,1)} %bitcast.330, bf16[576,12,64]{0,2,1:T(8,128)(2,1)} %bitcast.332), kind=kOutput, calls=%fused_computation.25.clone.1 | convolution fusion | flops 529507584 | bytes 33675840 | tf_op jit(solution)/shard_map/while/body/eval_jaxpr/qhd,khd->hqk/dot_general | solution.py:114
  444.1 12.7 multiply_convert_fusion.8
  461.2 8.2 fusion.309
  475.2 7.4 fusion.308
  486.5 18.2 %multiply_reduce_fusion.24 = (f32[12,576]{1,0:T(8,128)S(1)}, f32[12,576,576]{1,2,0:T(8,128)}) fusion(f32[12,576,576]{1,2,0:T(8,128)} %fusion.308, f32[12,576]{1,0:T(8,128)} %dynamic-slice_bitcast_fusion.2, pred[576]{0:T(1024)(128)(4,1)S(1)} %compare_reduce_fusion.5, bf16[576,12,64]{0,2,1:T(8,128)(2,1)} %bitcast.330, bf16[576,12,64]{0,2,1:T(8,128)(2,1)} %bitcast.332), kind=kOutput, calls=%fused_computation.25.clone.1 | convolution fusion | flops 529507584 | bytes 33675840 | tf_op jit(solution)/shard_map/while/body/eval_jaxpr/qhd,khd->hqk/dot_general | solution.py:114
  504.8 12.7 multiply_convert_fusion.8
  521.9 8.2 fusion.309
  533.4 12.2 copy.452
  545.7 10.0 fusion.221
  562.3 5.5 scatter_fusion.1
  567.8 4.9 all-to-all-start.2
  572.7 13.2 fusion.20
  586.0 9.5 copy.570
  595.4 8.1 reshape.1265
  603.5 5.7 fusion.155
  612.5 11.3 fusion.236
  623.8 10.8 reshape.1268
  634.6 4.0 gather_fusion.6
  638.7 6.5 convolution_bitcast_fusion
  645.2 10.5 fusion.220
  655.7 6.2 copy.457
  661.9 5.0 multiply_reduce_fusion.1
  672.2 5.1 add_convert_fusion
  679.9 5.3 fusion.222
  706.0 4.9 fusion.59
  714.7 4.4 reshape.1263
  719.1 4.9 convert_element_type.273
  724.0 9.7 fusion.51
  733.7 4.1 fusion.231
  744.7 5.1 copy.464
  749.8 5.3 reshape.1258
  755.1 6.7 multiply_reduce_fusion.20
  775.0 10.7 fusion.49
  787.7 5.4 scatter_fusion
  793.1 4.1 slice_reduce_fusion
  802.7 45.4 %all-reduce.19 = (f32[256]{0:T(256)}, f32[256]{0:T(256)}, f32[256]{0:T(256)}, f32[256]{0:T(256)}, f32[1024]{0:T(1024)}, /*index=5*/f32[1024]{0:T(1024)}, f32[768...) all-reduce(f32[256]{0:T(256)} %reduce_sum.711, ...), channel_id=1, replica_groups=mesh['batch'=8,'section'=4] {'batch','section'}, use_global_device_ids=true, to_apply=%region_53.54 | all-reduce | flops 13056 | bytes 104448 | tf_op jit(solution)/shard_map/psum | solution.py:375
  848.2 6.4 add_multiply_fusion
  854.6 488.4 %all-reduce.23.cloned.1.call-done = (f32[262144]{0:T(1024)}, f32[589824]{0:T(1024)}, f32[262144]{0:T(1024)}, f32[786432]{0:T(1024)}, f32[442368]{0:T(1024)}, /*i...) async-done(((f32[262144]{0:T(1024)}, f32[589824]{0:T(1024)}, f32[262144]{0:T(1024)}, f32[786432]{0:T(1024)}, f32[442368]{0:T(1024)}, ...) | async-done | bytes 37683216
  (582 shorter events, 303.9 us)
Async XLA Ops:
  7.2 217.4 %copy-start = (bf16[768,2304]{1,0:T(8,128)(2,1)S(1)}, bf16[768,2304]{1,0:T(8,128)(2,1)}, u32[]{:S(2)}) copy-start(bf16[768,2304]{1,0:T(8,128)(2,1)} %param.50) | copy-start | bytes 10616836
  8.5 11.3 copy-start.147
  13.1 53.0 %all-to-all-start.1 = ((bf16[4,1,1]{2,1,0:T(2,128)(2,1)}), bf16[4,1,1]{2,1,0:T(2,128)(2,1)}, u32[]{:S(2)}, u32[]{:S(2)}) async-start(bf16[4,1,1]{2,1,0:T(2,128)(2,1)} %copy.443), calls=%async_computation.1 | async-start | bytes 4096 | tf_op jit(solution)/shard_map/all_to_all | solution.py:247
  21.8 17.0 %copy-start.121 = (pred[2]{0:T(512)(128)(4,1)}, pred[2]{0:T(512)(128)(4,1)S(1)}, u32[]{:S(2)}) copy-start(pred[2]{0:T(512)(128)(4,1)S(1)} %broadcast_compare_fusion) | copy-start | bytes 10
  21.8 17.0 %copy-start.119 = (pred[576]{0:T(1024)(128)(4,1)}, pred[576]{0:T(1024)(128)(4,1)S(1)}, u32[]{:S(2)}) copy-start(pred[576]{0:T(1024)(128)(4,1)S(1)} %fusion.200) | copy-start | bytes 1732
  27.6 11.2 copy-start.129
  52.0 5.2 copy-start.122
  52.0 5.9 copy-start.120
  68.4 79.7 %copy-start.53 = (f32[2,576]{1,0:T(2,128)}, f32[2,576]{1,0:T(2,128)S(1)}, u32[]{:S(2)}) copy-start(f32[2,576]{1,0:T(2,128)S(1)} %get-tuple-element.347) | copy-start | bytes 13828
  104.6 5.8 copy-start.32
  112.2 5.5 copy-start.107
  112.2 5.5 copy-start.108
  116.5 5.3 copy-start.10
  116.6 5.2 copy-start.86
  117.6 5.3 copy-start.109
  133.8 15.8 %copy-start.55 = (f32[576,768]{1,0:T(8,128)S(1)}, f32[576,768]{1,0:T(8,128)}, u32[]{:S(2)}) copy-start(f32[576,768]{1,0:T(8,128)} %convert_element_type.243) | copy-start | bytes 5308420
  133.8 15.8 %copy-start.151 = (bf16[1024,768]{1,0:T(8,128)(2,1)S(1)}, bf16[1024,768]{1,0:T(8,128)(2,1)}, u32[]{:S(2)}) copy-start(bf16[1024,768]{1,0:T(8,128)(2,1)} %param.45) | copy-start | bytes 4718596
  133.8 15.8 %copy-start.155 = (f32[768]{0:T(1024)S(1)}, f32[768]{0:T(1024)}, u32[]{:S(2)}) copy-start(f32[768]{0:T(1024)} %param.46) | copy-start | bytes 9220
  161.2 48.7 %all-to-all-start = ((bf16[4,576,768]{2,1,0:T(8,128)(2,1)}), bf16[4,576,768]{2,1,0:T(8,128)(2,1)}, u32[]{:S(2)}, u32[]{:S(2)}) async-start(bf16[4,576,768]{2,1,0:T(8,128)(2,1)} %broadcast_select_fusion), calls=%async_computation | async-start | bytes 7077888 | tf_op jit(solution)/shard_map/all_to_all | solution.py:246
  166.4 40.5 %copy-start.69 = (f32[1152]{0:T(1024)}, f32[1152]{0:T(1024)S(1)}, u32[]{:S(2)}) copy-start(f32[1152]{0:T(1024)S(1)} %select_n.225) | copy-start | bytes 13828
  190.5 6.0 copy-start.33
  218.5 6.2 copy-start.62
  244.7 74.3 %copy-start.156 = (f32[768]{0:T(1024)S(1)}, f32[768]{0:T(1024)}, u32[]{:S(2)}) copy-start(f32[768]{0:T(1024)} %param.54) | copy-start | bytes 9220
  319.1 6.0 copy-start.149
  325.1 40.1 %copy-start.90 = (f32[1152]{0:T(1024)}, f32[1152]{0:T(1024)S(1)}, u32[]{:S(2)}) copy-start(f32[1152]{0:T(1024)S(1)} %fusion.193) | copy-start | bytes 13828
  385.6 13.0 copy-start.19
  385.6 13.1 copy-start.91
  385.6 13.1 copy-start.133
  385.6 13.1 copy-start.150
  385.6 13.1 copy-start.158
  414.4 7.6 copy-start.3
  414.5 7.5 copy-start.1
  414.5 7.5 copy-start.58
  414.5 8.1 copy-start.24
  425.8 18.3 %copy-start.25 = (f32[12,576]{1,0:T(8,128)S(1)}, f32[12,576]{1,0:T(8,128)}, u32[]{:S(2)}) copy-start(f32[12,576]{1,0:T(8,128)} %dynamic-slice_bitcast_fusion.2) | copy-start | bytes 82948 | tf_op jit(solution)/shard_map/while
  444.1 12.7 copy-start.2
  475.1 7.6 copy-start.3
  475.1 7.5 copy-start.1
  475.2 7.5 copy-start.58
  475.2 8.1 copy-start.24
  486.5 18.2 %copy-start.25 = (f32[12,576]{1,0:T(8,128)S(1)}, f32[12,576]{1,0:T(8,128)}, u32[]{:S(2)}) copy-start(f32[12,576]{1,0:T(8,128)} %dynamic-slice_bitcast_fusion.2) | copy-start | bytes 82948 | tf_op jit(solution)/shard_map/while
  504.8 12.7 copy-start.2
  533.4 12.2 copy-start.63
  533.4 12.2 copy-start.79
  545.7 10.0 copy-start.68
  545.7 10.0 copy-start.9
  545.7 10.0 copy-start.65
  567.8 66.8 %all-to-all-start.2 = ((bf16[4,576,768]{2,1,0:T(8,128)(2,1)}), bf16[4,576,768]{2,1,0:T(8,128)(2,1)}, u32[]{:S(2)}, u32[]{:S(2)}) async-start(bf16[4,576,768]{2,1,0:T(8,128)(2,1)} %scatter_fusion.1), calls=%async_computation.2 | async-start | bytes 7077888 | tf_op jit(solution)/shard_map/all_to_all | solution.py:328
  572.7 770.3 %all-reduce.23.cloned.1.call-start = ((), (), s32[]{:S(2)}) async-start(), calls=%async_computation.3 | async-start | bytes 75366400
  638.6 6.5 copy-start.27
  638.6 6.5 copy-start.123
  638.6 6.5 copy-start.141
  638.7 6.5 copy-start.152
  655.7 6.2 copy-start.81
  661.8 5.3 slice-start
  661.9 5.5 slice-start.1
  749.7 5.3 copy-start.85
  749.8 5.3 copy-start.88
  755.1 6.7 copy-start.95
  755.1 6.7 copy-start.138
  755.1 6.8 copy-start.13
  755.1 7.3 copy-start.106
  793.1 55.1 %copy-start.76 = (f32[256]{0:T(256)S(1)}, f32[256]{0:T(256)}, u32[]{:S(2)}) copy-start(f32[256]{0:T(256)} %copy-done.74) | copy-start | bytes 3076
  793.1 55.1 %copy-start.98 = (f32[256]{0:T(256)S(1)}, f32[256]{0:T(256)}, u32[]{:S(2)}) copy-start(f32[256]{0:T(256)} %copy-done.96) | copy-start | bytes 3076
  (112 other events, 316.0 us)
Sparse Core Ops, SparseCore 0:
  771.9 570.9 all-reduce.22
where the time goes:
time: 1370 us; the launch traced here: 1360 us
  waiting for transfers between devices  488 us (36%)
  matrix products  317 us (23%)
  local copies, waits for them, and re-layouts  290 us (21%)
  other arithmetic  192 us (14%)
  blocking collectives  45.4 us (3%)
  between operations  15.5 us (1%)
  starting transfers between devices  14.3 us (1%)
    unnamed x2, waiting for transfers between devices  488 us
    dot_general x8, matrix products, right_product(): lax.dot_general(left, right, (((1,), (1,)), ((), ())), preferred_element_...  72.3 us
    dot_general x8, matrix products, product(): return jnp.dot(left, right, preferred_element_type=jnp.float32)  71.8 us
    dot_general x8, matrix products, left_product(): lax.dot_general(left, right, (((0,), (0,)), ((), ())), preferred_element_...  61 us
    unnamed x327, local copies, waits for them, and re-layouts  58.5 us
    psum x1, blocking collectives, shards(): lax.psum((grad_first_gain, grad_first_bias, grad_second_gain, grad_second...  45.4 us
    dot_general x2, matrix products, attend_backward(): jnp.einsum('qhd,khd->hqk', grad_heads, value_heads, preferred_element_typ...  36.5 us
    dot_general x4, matrix products, masked_scores(): jnp.einsum('qhd,khd->hqk', query_heads, key_heads, preferred_element_type...  32.2 us
  transfers between devices with their start and end apart: 4, of which 1 were waited for; matrix products, arithmetic and copies ran while one was open for 14% of the time, Pallas kernels for 0%

commit v1 on v0

v1 whole, which is shorter than its diff:
```python
import jax
import jax.numpy as jnp
from jax import lax
from jax.experimental import pallas as pl
from jax.experimental.pallas import tpu as pltpu
from jax.sharding import PartitionSpec as P

HEADS = 12
GROUPS = 32
SIDE = 24
SIDE_SMALL = 14
LANES = 128
MIB = 1024 * 1024
BOTH = ("batch", "section")

f32 = jnp.float32
bf16 = jnp.bfloat16


def dot_nn(left, right):
    return jnp.dot(left, right, preferred_element_type=f32)


def dot_tn(left, right):
    return lax.dot_general(left, right, (((0,), (0,)), ((), ())), preferred_element_type=f32)


def dot_nt(left, right):
    return lax.dot_general(left, right, (((1,), (1,)), ((), ())), preferred_element_type=f32)


def fold(values):
    rows, columns = values.shape
    return jnp.sum(values.reshape(rows // 8, 8, columns), axis=0)


def total(values):
    return jnp.sum(values, axis=0, keepdims=True)


def spread_lanes(mask, columns):
    return jnp.concatenate([mask] * (columns // LANES), axis=1)


def cdf_pdf(values):
    bell = jnp.exp(-0.5 * (values * values))
    t = 1.0 / (1.0 + 0.23164189 * jnp.abs(values))
    tail = (
        ((((0.5307027145 * t - 0.7265760135) * t + 0.7107068705) * t - 0.142248368) * t + 0.127414796)
        * t
        * bell
    )
    return jnp.where(values < 0.0, tail, 1.0 - tail), bell * 0.3989422804014327


def group_total(row, per_group):
    channels = row.shape[1]
    rows = jnp.broadcast_to(row, (8, channels))
    lane = lax.broadcasted_iota(jnp.int32, (8, LANES), 1)
    parts = []
    for k in range(channels // LANES):
        part = rows[:, k * LANES : (k + 1) * LANES]
        step = 1
        while step < per_group:
            up = pltpu.roll(part, LANES - step, 1)
            down = pltpu.roll(part, step, 1)
            part = part + jnp.where((lane & step) == 0, up, down)
            step *= 2
        parts.append(part)
    return jnp.concatenate(parts, axis=1)[0:1]


def cell_grid(cells):
    cell = lax.broadcasted_iota(jnp.int32, (cells, LANES), 0).astype(f32)
    row = jnp.floor((cell + 0.5) * (1.0 / SIDE))
    return row, cell - row * SIDE


def validity_mask(image_class, cells):
    row, column = cell_grid(cells)
    corner = jnp.where((row < SIDE_SMALL) & (column < SIDE_SMALL), 1.0, 0.0)
    return jnp.where(image_class == 1, 1.0, corner)


def valid_count(image_class):
    return jnp.where(image_class == 1, float(SIDE * SIDE), float(SIDE_SMALL * SIDE_SMALL))


def rows_at(index, size):
    return pl.ds(pl.multiple_of(index * size, size), size)


def fill_columns(grid_value, padded, columns, sign):
    cells, channels = grid_value.shape
    _, column = cell_grid(cells)
    has_left = spread_lanes(jnp.where(column > 0.5, 1.0, 0.0), channels)
    has_right = spread_lanes(jnp.where(column < SIDE - 1.5, 1.0, 0.0), channels)
    zeros = jnp.zeros((SIDE, channels), f32)
    shifted = (
        pltpu.roll(grid_value, 1, 0) * has_left,
        grid_value,
        pltpu.roll(grid_value, cells - 1, 0) * has_right,
    )
    for k in range(3):
        padded[k, 0:SIDE, :] = zeros
        padded[k, SIDE + cells : 2 * SIDE + cells, :] = zeros
        padded[k, SIDE : SIDE + cells, :] = shifted[k]
    for row_shift in range(3):
        for column_shift in range(3):
            tap = row_shift * 3 + column_shift
            down = row_shift if sign > 0 else 2 - row_shift
            across = column_shift if sign > 0 else 2 - column_shift
            columns[:, tap * channels : (tap + 1) * channels] = padded[
                across, down * SIDE : down * SIDE + cells, :
            ].astype(bf16)


def standardized(weight):
    rows = weight.shape[0]
    centred = weight - total(weight) * (1.0 / rows)
    spread = total(centred * centred) * (1.0 / rows)
    scale = lax.rsqrt(spread + 1e-05)
    return centred * scale, scale


def standardize_back(weight, grad):
    rows = weight.shape[0]
    normal, scale = standardized(weight)
    grad_mean = total(grad) * (1.0 / rows)
    inner = total(grad * normal) * (1.0 / rows)
    return scale * (grad - grad_mean - normal * inner)


def stem_forward_kernel(
    class_ref,
    x_ref,
    w_in_ref,
    w_mid_ref,
    w_out_ref,
    gain1_ref,
    bias1_ref,
    gain2_ref,
    bias2_ref,
    gain3_ref,
    bias3_ref,
    embed_ref,
    embed_bias_ref,
    position_ref,
    std_in_ref,
    std_mid_ref,
    std_out_ref,
    first_ref,
    second_ref,
    third_ref,
    stat1_ref,
    stat2_ref,
    stat3_ref,
    stem_ref,
    tokens_ref,
    mask,
    padded,
    columns,
    act_two,
):
    image = pl.program_id(0)
    cells = x_ref.shape[1]
    channels = x_ref.shape[2]
    middle = w_in_ref.shape[1]

    @pl.when(image == 0)
    def _():
        std_in_ref[...] = standardized(w_in_ref[...].astype(f32))[0].astype(bf16)
        std_mid_ref[...] = standardized(w_mid_ref[...].astype(f32))[0].astype(bf16)
        std_out_ref[...] = standardized(w_out_ref[...].astype(f32))[0].astype(bf16)

    image_class = class_ref[image]
    mask[...] = validity_mask(image_class, cells)
    count = valid_count(image_class)
    chunk = 96
    steps = cells // chunk

    def stats(values_ref, stat_ref, sums):
        width = values_ref.shape[2]
        per_group = width // GROUPS
        inverse = 1.0 / (count * per_group)
        centre = group_total(total(sums), per_group) * inverse

        def one(step, carry):
            rows = rows_at(step, chunk)
            centred = (values_ref[0, rows, :] - centre) * spread_lanes(mask[rows, :], width)
            return carry + fold(centred * centred)

        squares = lax.fori_loop(0, steps, one, jnp.zeros((8, width), f32))
        scale = lax.rsqrt(group_total(total(squares), per_group) * inverse + 1e-05)
        stat_ref[0, 0:1, :] = centre
        stat_ref[0, 1:2, :] = scale
        return centre, scale

    def first_step(step, carry):
        rows = rows_at(step, chunk)
        low = (x_ref[0, rows, :] * spread_lanes(mask[rows, :], channels)).astype(bf16)
        values = dot_nn(low, std_in_ref[...])
        first_ref[0, rows, :] = values
        return carry + fold(values)

    sums = lax.fori_loop(0, steps, first_step, jnp.zeros((8, middle), f32))
    centre, scale = stats(first_ref, stat1_ref, sums)
    gain = scale * gain1_ref[...]
    normed = (first_ref[0] - centre) * gain + bias1_ref[...]
    act = normed * cdf_pdf(normed)[0] * spread_lanes(mask[...], middle)
    fill_columns(act, padded, columns, 1)

    def second_step(step, carry):
        rows = rows_at(step, chunk)
        values = dot_nn(columns[rows, :], std_mid_ref[...])
        second_ref[0, rows, :] = values
        return carry + fold(values * spread_lanes(mask[rows, :], middle))

    sums = lax.fori_loop(0, steps, second_step, jnp.zeros((8, middle), f32))
    centre, scale = stats(second_ref, stat2_ref, sums)
    gain = scale * gain2_ref[...]
    normed = (second_ref[0] - centre) * gain + bias2_ref[...]
    act_two[...] = (normed * cdf_pdf(normed)[0] * spread_lanes(mask[...], middle)).astype(bf16)

    def third_step(step, carry):
        rows = rows_at(step, chunk)
        values = dot_nn(act_two[rows, :], std_out_ref[...])
        third_ref[0, rows, :] = values
        return carry + fold(values)

    sums = lax.fori_loop(0, steps, third_step, jnp.zeros((8, channels), f32))
    centre, scale = stats(third_ref, stat3_ref, sums)
    gain = scale * gain3_ref[...]

    @pl.loop(0, steps)
    def _(step):
        rows = rows_at(step, chunk)
        keep = mask[rows, :]
        keep_wide = spread_lanes(keep, channels)
        argument = (
            x_ref[0, rows, :] * keep_wide + (third_ref[0, rows, :] - centre) * gain + bias3_ref[...]
        )
        stem = (argument * cdf_pdf(argument)[0] * keep_wide).astype(bf16)
        stem_ref[0, rows, :] = stem
        values = dot_nn(stem, embed_ref[...]) + embed_bias_ref[...] + position_ref[rows, :].astype(f32)
        tokens_ref[0, rows, :] = (values * spread_lanes(keep, values.shape[1])).astype(bf16)


def whole(shape):
    return pl.BlockSpec(shape, lambda *_: (0,) * len(shape))


def per_image(shape):
    return pl.BlockSpec((1,) + shape, lambda image, *_: (image,) + (0,) * len(shape))


def stem_forward(image_class, x, w_in, w_mid, w_out, norms, embed, embed_bias, position):
    images, cells, channels = x.shape
    middle = w_in.shape[1]
    width = embed.shape[1]
    row = lambda size: whole((1, size))
    return pl.pallas_call(
        stem_forward_kernel,
        out_shape=(
            jax.ShapeDtypeStruct((channels, middle), bf16),
            jax.ShapeDtypeStruct((9 * middle, middle), bf16),
            jax.ShapeDtypeStruct((middle, channels), bf16),
            jax.ShapeDtypeStruct((images, cells, middle), f32),
            jax.ShapeDtypeStruct((images, cells, middle), f32),
            jax.ShapeDtypeStruct((images, cells, channels), f32),
            jax.ShapeDtypeStruct((images, 8, middle), f32),
            jax.ShapeDtypeStruct((images, 8, middle), f32),
            jax.ShapeDtypeStruct((images, 8, channels), f32),
            jax.ShapeDtypeStruct((images, cells, channels), bf16),
            jax.ShapeDtypeStruct((images, cells, width), bf16),
        ),
        grid_spec=pltpu.PrefetchScalarGridSpec(
            num_scalar_prefetch=1,
            grid=(images,),
            in_specs=[
                per_image((cells, channels)),
                whole((channels, middle)),
                whole((9 * middle, middle)),
                whole((middle, channels)),
                row(middle),
                row(middle),
                row(middle),
                row(middle),
                row(channels),
                row(channels),
                whole((channels, width)),
                row(width),
                whole((cells, width)),
            ],
            out_specs=[
                whole((channels, middle)),
                whole((9 * middle, middle)),
                whole((middle, channels)),
                per_image((cells, middle)),
                per_image((cells, middle)),
                per_image((cells, channels)),
                per_image((8, middle)),
                per_image((8, middle)),
                per_image((8, channels)),
                per_image((cells, channels)),
                per_image((cells, width)),
            ],
            scratch_shapes=[
                pltpu.VMEM((cells, LANES), f32),
                pltpu.VMEM((3, cells + 2 * SIDE, middle), f32),
                pltpu.VMEM((cells, 9 * middle), bf16),
                pltpu.VMEM((cells, middle), bf16),
            ],
        ),
        compiler_params=pltpu.CompilerParams(vmem_limit_bytes=58 * MIB),
        name="stem_forward",
    )(image_class, x, w_in, w_mid, w_out, *norms, embed, embed_bias, position)


def row_norm(values):
    centre = jnp.mean(values, axis=-1, keepdims=True)
    centred = values - centre
    scale = lax.rsqrt(jnp.mean(centred * centred, axis=-1, keepdims=True) + 1e-06)
    return centred * scale, scale


def attend_forward_kernel(
    class_ref,
    tokens_ref,
    gain1_ref,
    bias1_ref,
    joint_ref,
    query_bias_ref,
    value_bias_ref,
    mix_ref,
    mix_bias_ref,
    gain2_ref,
    bias2_ref,
    normed_ref,
    query_ref,
    key_ref,
    value_ref,
    log_total_ref,
    mixed_ref,
    resid_ref,
    normed_two_ref,
):
    image = pl.program_id(0)
    cells, width = tokens_ref.shape[1:]
    chunk = 96
    steps = cells // chunk
    scale = (width // HEADS) ** -0.5

    @pl.loop(0, steps)
    def _(step):
        rows = rows_at(step, chunk)
        normal, _ = row_norm(tokens_ref[0, rows, :].astype(f32))
        normed_ref[0, rows, :] = (normal * gain1_ref[...] + bias1_ref[...]).astype(bf16)

    block = 256
    blocks = width // block

    @pl.loop(0, blocks)
    def _(step):
        here = rows_at(step, block)
        later = pl.ds(pl.multiple_of(width + step * block, block), block)
        last = pl.ds(pl.multiple_of(2 * width + step * block, block), block)
        normed = normed_ref[0]
        query = dot_nn(normed, joint_ref[:, here]) + query_bias_ref[:, here]
        query_ref[0, :, here] = query.astype(bf16)
        key_ref[0, :, here] = dot_nn(normed, joint_ref[:, later]).astype(bf16)
        value = dot_nn(normed, joint_ref[:, last]) + value_bias_ref[:, here]
        value_ref[0, :, here] = value.astype(bf16)

    _, column = cell_grid(cells)
    image_class = class_ref[image]
    cell = lax.broadcasted_iota(jnp.int32, (8, cells), 1).astype(f32)
    cell_row = jnp.floor((cell + 0.5) * (1.0 / SIDE))
    cell_column = cell - cell_row * SIDE
    outside = jnp.where((cell_row < SIDE_SMALL) & (cell_column < SIDE_SMALL), 0.0, -1000000000.0)
    key_bias = jnp.where(image_class == 1, 0.0, outside)[0:1]
    upper = lax.broadcasted_iota(jnp.int32, (cells, LANES), 1) >= LANES // 2

    @pl.loop(0, width // LANES)
    def _(pair):
        lanes = rows_at(pair, LANES)
        query = query_ref[0, :, lanes] * bf16(scale)
        key = key_ref[0, :, lanes]
        value = value_ref[0, :, lanes]
        outs = []
        for half in range(2):
            mine = upper if half else jnp.logical_not(upper)
            scores = dot_nt(jnp.where(mine, query, bf16(0)), key) + key_bias
            top = jnp.max(scores, axis=-1, keepdims=True)
            weights = jnp.exp(scores - top)
            weight_sum = jnp.sum(weights, axis=-1, keepdims=True)
            probs = (weights * (1.0 / weight_sum)).astype(bf16)
            outs.append(dot_nn(probs, value))
            log_total = jnp.broadcast_to(top + jnp.log(weight_sum), (cells, LANES))
            log_total_ref[0, 2 * pair + half] = log_total.T[0:8]
        mixed_ref[0, :, lanes] = jnp.where(upper, outs[1], outs[0]).astype(bf16)

    @pl.loop(0, steps)
    def _(step):
        rows = rows_at(step, chunk)
        resid = (
            tokens_ref[0, rows, :].astype(f32)
            + dot_nn(mixed_ref[0, rows, :], mix_ref[...])
            + mix_bias_ref[...]
        )
        resid_ref[0, rows, :] = resid
        normal, _ = row_norm(resid)
        normed_two_ref[0, rows, :] = (normal * gain2_ref[...] + bias2_ref[...]).astype(bf16)


def attend_forward(
    image_class, tokens, gain1, bias1, joint, query_bias, value_bias, mix, mix_bias, gain2, bias2
):
    images, cells, width = tokens.shape
    row = whole((1, width))
    low = jax.ShapeDtypeStruct((images, cells, width), bf16)
    low_spec = per_image((cells, width))
    return pl.pallas_call(
        attend_forward_kernel,
        out_shape=(
            low,
            low,
            low,
            low,
            jax.ShapeDtypeStruct((images, HEADS, 8, cells), f32),
            low,
            jax.ShapeDtypeStruct((images, cells, width), f32),
            low,
        ),
        grid_spec=pltpu.PrefetchScalarGridSpec(
            num_scalar_prefetch=1,
            grid=(images,),
            in_specs=[
                low_spec,
                row,
                row,
                whole((width, 3 * width)),
                row,
                row,
                whole((width, width)),
                row,
                row,
                row,
            ],
            out_specs=[
                low_spec,
                low_spec,
                low_spec,
                low_spec,
                per_image((HEADS, 8, cells)),
                low_spec,
                low_spec,
                low_spec,
            ],
        ),
        compiler_params=pltpu.CompilerParams(vmem_limit_bytes=58 * MIB),
        name="attend_forward",
    )(image_class, tokens, gain1, bias1, joint, query_bias, value_bias, mix, mix_bias, gain2, bias2)


def feed_kernel(
    class_ref,
    mine_ref,
    normed_ref,
    resid_ref,
    cotangent_ref,
    expand_ref,
    expand_bias_ref,
    shrink_ref,
    shrink_bias_ref,
    output_ref,
    grad_normed_ref,
    grad_shrink_ref,
    grad_expand_ref,
    grad_expand_bias_ref,
    grad_shrink_bias_ref,
    sent,
    result,
    hidden,
    grad_pre,
    normed_turned,
):
    step = pl.program_id(0)
    images, cells, width = normed_ref.shape
    part = cells // 2

    @pl.when(step == 0)
    def _():
        sums = jnp.zeros((8, width), f32)
        for image in range(images):
            keep = spread_lanes(validity_mask(class_ref[image], cells), width)
            grad = cotangent_ref[mine_ref[image]].astype(f32) * keep
            sent[image * cells : (image + 1) * cells, :] = grad.astype(bf16)
            sums = sums + fold(grad)
            result[image * cells : (image + 1) * cells, :] = resid_ref[image] + shrink_bias_ref[...]
            normed_turned[:, image * cells : (image + 1) * cells] = normed_ref[image].T
        grad_shrink_bias_ref[...] = sums
        grad_normed_ref[...] = jnp.zeros_like(grad_normed_ref)

    bias_sums = jnp.zeros((8, expand_ref.shape[1]), f32)
    for image in range(images):
        for piece in range(cells // part):
            local = slice(piece * part, (piece + 1) * part)
            rows = slice(image * cells + piece * part, image * cells + (piece + 1) * part)
            pre = dot_nn(normed_ref[image, local, :], expand_ref[...]) + expand_bias_ref[...]
            back = dot_nt(sent[rows, :], shrink_ref[...])
            cdf, pdf = cdf_pdf(pre)
            low = (pre * cdf).astype(bf16)
            hidden[rows, :] = low
            grad = back * (cdf + pre * pdf)
            bias_sums = bias_sums + fold(grad)
            grad_low = grad.astype(bf16)
            grad_pre[rows, :] = grad_low
            result[rows, :] += dot_nn(low, shrink_ref[...])
            grad_normed_ref[image, local, :] += dot_nt(grad_low, expand_ref[...])
    grad_expand_bias_ref[...] = bias_sums
    grad_shrink_ref[...] = dot_tn(hidden[...], sent[...]).astype(bf16)
    grad_expand_ref[...] = dot_nn(normed_turned[...], grad_pre[...]).astype(bf16)

    @pl.when(step == pl.num_programs(0) - 1)
    def _():
        output_ref[...] = jnp.zeros_like(output_ref)
        for image in range(images):
            keep = spread_lanes(validity_mask(class_ref[image], cells), width)
            rows = result[image * cells : (image + 1) * cells, :] * keep
            output_ref[mine_ref[image]] = rows.astype(bf16)


def feed(image_class, mine, normed, resid, cotangent, expand, expand_bias, shrink, shrink_bias):
    images, cells, width = normed.shape
    inner = expand.shape[1]
    slots = cotangent.shape[0]
    block = 512
    return pl.pallas_call(
        feed_kernel,
        out_shape=(
            jax.ShapeDtypeStruct((slots, cells, width), bf16),
            jax.ShapeDtypeStruct((images, cells, width), f32),
            jax.ShapeDtypeStruct((inner, width), bf16),
            jax.ShapeDtypeStruct((width, inner), bf16),
            jax.ShapeDtypeStruct((8, inner), f32),
            jax.ShapeDtypeStruct((8, width), f32),
        ),
        grid_spec=pltpu.PrefetchScalarGridSpec(
            num_scalar_prefetch=2,
            grid=(inner // block,),
            in_specs=[
                whole((images, cells, width)),
                whole((images, cells, width)),
                whole((slots, cells, width)),
                pl.BlockSpec((width, block), lambda step, *_: (0, step)),
                pl.BlockSpec((1, block), lambda step, *_: (0, step)),
                pl.BlockSpec((block, width), lambda step, *_: (step, 0)),
                whole((1, width)),
            ],
            out_specs=[
                whole((slots, cells, width)),
                whole((images, cells, width)),
                pl.BlockSpec((block, width), lambda step, *_: (step, 0)),
                pl.BlockSpec((width, block), lambda step, *_: (0, step)),
                pl.BlockSpec((8, block), lambda step, *_: (0, step)),
                whole((8, width)),
            ],
            scratch_shapes=[
                pltpu.VMEM((images * cells, width), bf16),
                pltpu.VMEM((images * cells, width), f32),
                pltpu.VMEM((images * cells, block), bf16),
                pltpu.VMEM((images * cells, block), bf16),
                pltpu.VMEM((width, images * cells), bf16),
            ],
        ),
        compiler_params=pltpu.CompilerParams(vmem_limit_bytes=60 * MIB),
        name="feed",
    )(image_class, mine, normed, resid, cotangent, expand, expand_bias, shrink, shrink_bias)


def row_norm_back(grad, normal, scale, gain):
    inner = grad * gain
    mean = jnp.mean(inner, axis=-1, keepdims=True)
    cross = jnp.mean(inner * normal, axis=-1, keepdims=True)
    return scale * (inner - mean - normal * cross)


def attend_backward_kernel(
    class_ref,
    mine_ref,
    tokens_ref,
    normed_ref,
    query_ref,
    key_ref,
    value_ref,
    log_total_ref,
    mixed_ref,
    resid_ref,
    cotangent_ref,
    grad_normed_two_ref,
    gain1_ref,
    joint_ref,
    mix_ref,
    gain2_ref,
    grad_tokens_ref,
    grad_joint_weight_ref,
    grad_mix_ref,
    sums_ref,
    mask,
    grad_resid,
    resid_low,
    grad_mixed,
    grad_joint,
    joint_total,
    mix_total,
):
    image = pl.program_id(0)
    last = pl.num_programs(0) - 1
    cells, width = tokens_ref.shape[1:]
    chunk = 96
    steps = cells // chunk
    scale = (width // HEADS) ** -0.5
    mask[...] = validity_mask(class_ref[image], cells)

    @pl.when(image == 0)
    def _():
        sums_ref[...] = jnp.zeros_like(sums_ref)
        joint_total[...] = jnp.zeros_like(joint_total)
        mix_total[...] = jnp.zeros_like(mix_total)

    @pl.loop(0, steps)
    def _(step):
        rows = rows_at(step, chunk)
        normal, row_scale = row_norm(resid_ref[0, rows, :])
        grad = grad_normed_two_ref[0, rows, :]
        sums_ref[0] += fold(grad * normal)
        sums_ref[1] += fold(grad)
        keep = spread_lanes(mask[rows, :], width)
        whole_grad = cotangent_ref[0, rows, :].astype(f32) * keep + row_norm_back(
            grad, normal, row_scale, gain2_ref[...]
        )
        sums_ref[2] += fold(whole_grad)
        grad_resid[rows, :] = whole_grad
        low = whole_grad.astype(bf16)
        resid_low[rows, :] = low
        grad_mixed[rows, :] = dot_nt(low, mix_ref[...]).astype(bf16)

    mix_total[...] += dot_tn(mixed_ref[0], resid_low[...])

    upper = lax.broadcasted_iota(jnp.int32, (cells, LANES), 1) >= LANES // 2
    key_bias = (mask[...] - 1.0) * 1000000000.0
    bias_wide = jnp.concatenate([key_bias] * 5, axis=1)[:, :cells]

    @pl.loop(0, width // LANES)
    def _(pair):
        lanes = rows_at(pair, LANES)
        query = query_ref[0, :, lanes] * bf16(scale)
        key = key_ref[0, :, lanes]
        value = value_ref[0, :, lanes]
        grad_out = grad_mixed[:, lanes]
        grads = []
        for half in range(2):
            mine = upper if half else jnp.logical_not(upper)
            scores = dot_nt(jnp.where(mine, key, bf16(0)), query)
            log_total = log_total_ref[0, 2 * pair + half, 0:1, :]
            probs = jnp.exp(scores + bias_wide - log_total)
            grad_probs = dot_nt(jnp.where(mine, value, bf16(0)), grad_out)
            weighted = probs * grad_probs
            grad_scores = (weighted - probs * total(weighted)).astype(bf16)
            grad_value = dot_nn(probs.astype(bf16), grad_out)
            grad_key = dot_nn(grad_scores, query)
            grad_query = dot_tn(grad_scores, key) * scale
            grads.append((grad_query, grad_key, grad_value))
        for k in range(3):
            grad = jnp.where(upper, grads[1][k], grads[0][k])
            if k != 1:
                sums_ref[3 + k // 2, :, lanes] += fold(grad)
            where = pl.ds(pl.multiple_of(k * width + pair * LANES, LANES), LANES)
            grad_joint[:, where] = grad.astype(bf16)

    block = 256

    @pl.loop(0, 3 * width // block)
    def _(step):
        here = rows_at(step, block)
        joint_total[:, here] += dot_tn(normed_ref[0], grad_joint[:, here])

    @pl.loop(0, steps)
    def _(step):
        rows = rows_at(step, chunk)
        normal, row_scale = row_norm(tokens_ref[0, rows, :].astype(f32))
        grad = dot_nt(grad_joint[rows, :], joint_ref[...])
        sums_ref[5] += fold(grad * normal)
        sums_ref[6] += fold(grad)
        back = row_norm_back(grad, normal, row_scale, gain1_ref[...])
        grad_tokens_ref[0, rows, :] = (grad_resid[rows, :] + back).astype(bf16)

    @pl.when(image == last)
    def _():
        grad_joint_weight_ref[...] = joint_total[...].astype(bf16)
        grad_mix_ref[...] = mix_total[...].astype(bf16)


def attend_backward(
    image_class,
    mine,
    tokens,
    normed,
    query,
    key,
    value,
    log_total,
    mixed,
    resid,
    cotangent,
    grad_normed_two,
    gain1,
    joint,
    mix,
    gain2,
):
    images, cells, width = tokens.shape
    row = whole((1, width))
    rows = per_image((cells, width))
    return pl.pallas_call(
        attend_backward_kernel,
        out_shape=(
            jax.ShapeDtypeStruct((images, cells, width), bf16),
            jax.ShapeDtypeStruct((width, 3 * width), bf16),
            jax.ShapeDtypeStruct((width, width), bf16),
            jax.ShapeDtypeStruct((7, 8, width), f32),
        ),
        grid_spec=pltpu.PrefetchScalarGridSpec(
            num_scalar_prefetch=2,
            grid=(images,),
            in_specs=[
                rows,
                rows,
                rows,
                rows,
                rows,
                per_image((HEADS, 8, cells)),
                rows,
                rows,
                pl.BlockSpec((1, cells, width), lambda image, classes, mine: (mine[image], 0, 0)),
                rows,
                row,
                whole((width, 3 * width)),
                whole((width, width)),
                row,
            ],
            out_specs=[
                rows,
                whole((width, 3 * width)),
                whole((width, width)),
                whole((7, 8, width)),
            ],
            scratch_shapes=[
                pltpu.VMEM((cells, LANES), f32),
                pltpu.VMEM((cells, width), f32),
                pltpu.VMEM((cells, width), bf16),
                pltpu.VMEM((cells, width), bf16),
                pltpu.VMEM((cells, 3 * width), bf16),
                pltpu.VMEM((width, 3 * width), f32),
                pltpu.VMEM((width, width), f32),
            ],
        ),
        compiler_params=pltpu.CompilerParams(vmem_limit_bytes=62 * MIB),
        name="attend_backward",
    )(
        image_class,
        mine,
        tokens,
        normed,
        query,
        key,
        value,
        log_total,
        mixed,
        resid,
        cotangent,
        grad_normed_two,
        gain1,
        joint,
        mix,
        gain2,
    )


def stem_backward_kernel(
    class_ref,
    grad_tokens_ref,
    x_ref,
    first_ref,
    second_ref,
    third_ref,
    stat1_ref,
    stat2_ref,
    stat3_ref,
    stem_ref,
    std_in_ref,
    std_mid_ref,
    std_out_ref,
    w_in_ref,
    w_mid_ref,
    w_out_ref,
    gain1_ref,
    bias1_ref,
    gain2_ref,
    bias2_ref,
    gain3_ref,
    bias3_ref,
    embed_ref,
    input_grad_ref,
    grad_embed_ref,
    grad_position_ref,
    grad_in_ref,
    grad_mid_ref,
    grad_out_ref,
    sums_embed_ref,
    sums1_ref,
    sums2_ref,
    sums3_ref,
    mask,
    grad_third,
    act,
    grad_grid,
    grad_first,
    padded,
    columns,
    embed_total,
    in_total,
    mid_total,
    out_total,
):
    image = pl.program_id(0)
    last = pl.num_programs(0) - 1
    cells, channels = x_ref.shape[1:]
    width = embed_ref.shape[1]
    middle = first_ref.shape[2]
    chunk = 96
    steps = cells // chunk
    image_class = class_ref[image]
    mask[...] = validity_mask(image_class, cells)
    count = valid_count(image_class)

    @pl.when(image == 0)
    def _():
        for ref in (
            grad_position_ref,
            sums_embed_ref,
            sums1_ref,
            sums2_ref,
            sums3_ref,
            embed_total,
            in_total,
            mid_total,
            out_total,
        ):
            ref[...] = jnp.zeros_like(ref)

    @pl.loop(0, steps)
    def _(step):
        rows = rows_at(step, chunk)
        grad = grad_tokens_ref[0, rows, :].astype(f32) * spread_lanes(mask[rows, :], width)
        grad_position_ref[rows, :] += grad
        sums_embed_ref[...] += fold(grad)

    embed_total[...] += dot_tn(stem_ref[0], grad_tokens_ref[0])

    def norm_of(stat_ref):
        return stat_ref[0, 0:1, :], stat_ref[0, 1:2, :]

    def means(sums, gain, per_group):
        inverse = 1.0 / (count * per_group)
        return (
            group_total(total(sums[0]) * gain, per_group) * inverse,
            group_total(total(sums[1]) * gain, per_group) * inverse,
        )

    centre, scale = norm_of(stat3_ref)
    gain = gain3_ref[...]

    def third_step(step, carry):
        rows = rows_at(step, chunk)
        keep = spread_lanes(mask[rows, :], channels)
        grad = dot_nt(grad_tokens_ref[0, rows, :], embed_ref[...]) * keep
        normal = (third_ref[0, rows, :] - centre) * scale
        argument = x_ref[0, rows, :] * keep + normal * gain + bias3_ref[...]
        cdf, pdf = cdf_pdf(argument)
        grad = grad * (cdf + argument * pdf)
        input_grad_ref[0, rows, :] = grad
        return carry[0] + fold(grad * normal), carry[1] + fold(grad)

    zeros = jnp.zeros((8, channels), f32)
    with_normal, plain = lax.fori_loop(0, steps, third_step, (zeros, zeros))
    sums3_ref[0] += with_normal
    sums3_ref[1] += plain
    mean, cross = means((plain, with_normal), gain, channels // GROUPS)
    outer = scale * gain
    mean = mean * scale
    cross = cross * scale

    @pl.loop(0, steps)
    def _(step):
        rows = rows_at(step, chunk)
        keep = spread_lanes(mask[rows, :], channels)
        normal = (third_ref[0, rows, :] - centre) * scale
        grad = (input_grad_ref[0, rows, :] * outer - mean - normal * cross) * keep
        grad_third[rows, :] = grad.astype(bf16)

    def middle_norm(values_ref, stat_ref, gain_ref, bias_ref, sums_ref, grad_of):
        centre, scale = norm_of(stat_ref)
        gain = gain_ref[...]
        keep = spread_lanes(mask[...], middle)
        normal = (values_ref[0] - centre) * scale
        argument = normal * gain + bias_ref[...]
        cdf, pdf = cdf_pdf(argument)
        act[...] = (argument * cdf * keep).astype(bf16)
        grad = grad_of() * keep * (cdf + argument * pdf)
        plain, with_normal = fold(grad), fold(grad * normal)
        sums_ref[0] += with_normal
        sums_ref[1] += plain
        mean, cross = means((plain, with_normal), gain, middle // GROUPS)
        return (grad * (scale * gain) - mean * scale - normal * (cross * scale)) * keep

    grad_second = middle_norm(
        second_ref,
        stat2_ref,
        gain2_ref,
        bias2_ref,
        sums2_ref,
        lambda: dot_nt(grad_third[...], std_out_ref[...]),
    )
    out_total[...] += dot_tn(act[...], grad_third[...])
    fill_columns(grad_second, padded, columns, -1)

    def spread_back():
        grad = jnp.zeros((cells, middle), f32)
        for tap in range(9):
            part = slice(tap * middle, (tap + 1) * middle)
            grad = grad + dot_nt(columns[:, part], std_mid_ref[part, :])
        return grad

    grad = middle_norm(first_ref, stat1_ref, gain1_ref, bias1_ref, sums1_ref, spread_back)
    grad_first[...] = grad.astype(bf16)
    mid_total[...] += dot_tn(act[...], columns[...])

    grad_grid[...] = grad_first[...].T

    @pl.loop(0, steps)
    def _(step):
        rows = rows_at(step, chunk)
        keep = spread_lanes(mask[rows, :], channels)
        back = dot_nt(grad_first[rows, :], std_in_ref[...])
        input_grad_ref[0, rows, :] = (input_grad_ref[0, rows, :] + back) * keep

    low = (x_ref[0] * spread_lanes(mask[...], channels)).astype(bf16)
    in_total[...] += dot_nn(grad_grid[...], low)

    @pl.when(image == last)
    def _():
        grad_embed_ref[...] = embed_total[...].astype(bf16)
        grad_out_ref[...] = standardize_back(w_out_ref[...].astype(f32), out_total[...]).astype(bf16)
        grad_in_ref[...] = standardize_back(w_in_ref[...].astype(f32), in_total[...].T).astype(bf16)
        rows = 9 * middle
        normal, scale = standardized(w_mid_ref[...].astype(f32))
        grads = [mid_total[:, tap * middle : (tap + 1) * middle] for tap in range(9)]
        grad_mean = sum(total(g) for g in grads) * (1.0 / rows)
        inner = sum(
            total(g * normal[tap * middle : (tap + 1) * middle]) for tap, g in enumerate(grads)
        ) * (1.0 / rows)
        for tap, g in enumerate(grads):
            part = slice(tap * middle, (tap + 1) * middle)
            grad_mid_ref[part, :] = (scale * (g - grad_mean - normal[part] * inner)).astype(bf16)


def stem_backward(
    image_class, grad_tokens, x, kept, stem, stds, weights, norms, embed
):
    images, cells, channels = x.shape
    middle = weights[0].shape[1]
    width = embed.shape[1]
    row = lambda size: whole((1, size))
    return pl.pallas_call(
        stem_backward_kernel,
        out_shape=(
            jax.ShapeDtypeStruct((images, cells, channels), f32),
            jax.ShapeDtypeStruct((channels, width), bf16),
            jax.ShapeDtypeStruct((cells, width), f32),
            jax.ShapeDtypeStruct((channels, middle), bf16),
            jax.ShapeDtypeStruct((9 * middle, middle), bf16),
            jax.ShapeDtypeStruct((middle, channels), bf16),
            jax.ShapeDtypeStruct((8, width), f32),
            jax.ShapeDtypeStruct((2, 8, middle), f32),
            jax.ShapeDtypeStruct((2, 8, middle), f32),
            jax.ShapeDtypeStruct((2, 8, channels), f32),
        ),
        grid_spec=pltpu.PrefetchScalarGridSpec(
            num_scalar_prefetch=1,
            grid=(images,),
            in_specs=[
                per_image((cells, width)),
                per_image((cells, channels)),
                per_image((cells, middle)),
                per_image((cells, middle)),
                per_image((cells, channels)),
                per_image((8, middle)),
                per_image((8, middle)),
                per_image((8, channels)),
                per_image((cells, channels)),
                whole((channels, middle)),
                whole((9 * middle, middle)),
                whole((middle, channels)),
                whole((channels, middle)),
                whole((9 * middle, middle)),
                whole((middle, channels)),
                row(middle),
                row(middle),
                row(middle),
                row(middle),
                row(channels),
                row(channels),
                whole((channels, width)),
            ],
            out_specs=[
                per_image((cells, channels)),
                whole((channels, width)),
                whole((cells, width)),
                whole((channels, middle)),
                whole((9 * middle, middle)),
                whole((middle, channels)),
                whole((8, width)),
                whole((2, 8, middle)),
                whole((2, 8, middle)),
                whole((2, 8, channels)),
            ],
            scratch_shapes=[
                pltpu.VMEM((cells, LANES), f32),
                pltpu.VMEM((cells, channels), bf16),
                pltpu.VMEM((cells, middle), bf16),
                pltpu.VMEM((middle, cells), bf16),
                pltpu.VMEM((cells, middle), bf16),
                pltpu.VMEM((3, cells + 2 * SIDE, middle), f32),
                pltpu.VMEM((cells, 9 * middle), bf16),
                pltpu.VMEM((channels, width), f32),
                pltpu.VMEM((middle, channels), f32),
                pltpu.VMEM((middle, 9 * middle), f32),
                pltpu.VMEM((middle, channels), f32),
            ],
        ),
        compiler_params=pltpu.CompilerParams(vmem_limit_bytes=62 * MIB),
        name="stem_backward",
    )(image_class, grad_tokens, x, *kept, stem, *stds, *weights, *norms, embed)


def local_step(
    image_class,
    mine,
    stem_input,
    conv_in_weight,
    conv_mid_weight,
    conv_out_weight,
    norms,
    embed_weight,
    embed_bias,
    position_table,
    attn_gain,
    attn_bias,
    joint_weight,
    query_bias,
    value_bias,
    mix_weight,
    mix_bias,
    mlp_gain,
    mlp_bias,
    expand_weight,
    expand_bias,
    shrink_weight,
    shrink_bias,
    received,
    after_feed=lambda *parts: parts,
):
    line = lambda vector: vector.reshape(1, -1)
    norms = tuple(line(item) for item in norms)
    weights = (conv_in_weight, conv_mid_weight.reshape(-1, conv_mid_weight.shape[-1]), conv_out_weight)
    std_in, std_mid, std_out, first, second, third, stat1, stat2, stat3, stem, tokens = stem_forward(
        image_class, stem_input, *weights, norms, embed_weight, line(embed_bias), position_table
    )
    normed, query, key, value, log_total, mixed, resid, normed_two = attend_forward(
        image_class,
        tokens,
        line(attn_gain),
        line(attn_bias),
        joint_weight,
        line(query_bias),
        line(value_bias),
        mix_weight,
        line(mix_bias),
        line(mlp_gain),
        line(mlp_bias),
    )
    outgoing, grad_normed_two, grad_shrink, grad_expand, sum_expand_bias, sum_shrink_bias = feed(
        image_class,
        mine,
        normed_two,
        resid,
        received,
        expand_weight,
        line(expand_bias),
        shrink_weight,
        line(shrink_bias),
    )
    grad_tokens, grad_joint, grad_mix, sums_block = attend_backward(
        image_class,
        mine,
        tokens,
        normed,
        query,
        key,
        value,
        log_total,
        mixed,
        resid,
        received,
        grad_normed_two,
        line(attn_gain),
        joint_weight,
        mix_weight,
        line(mlp_gain),
    )
    (
        input_grad,
        grad_embed,
        grad_position,
        grad_in,
        grad_mid,
        grad_out,
        sums_embed,
        sums1,
        sums2,
        sums3,
    ) = stem_backward(
        image_class,
        grad_tokens,
        stem_input,
        (first, second, third, stat1, stat2, stat3),
        stem,
        (std_in, std_mid, std_out),
        weights,
        norms,
        embed_weight,
    )
    matrices = (
        grad_in,
        grad_mid,
        grad_out,
        grad_embed,
        grad_position,
        grad_joint,
        grad_mix,
        grad_expand,
        grad_shrink,
    )
    vectors = (
        sums1[0],
        sums1[1],
        sums2[0],
        sums2[1],
        sums3[0],
        sums3[1],
        sums_embed,
        sums_block[5],
        sums_block[6],
        sums_block[3],
        sums_block[4],
        sums_block[2],
        sums_block[0],
        sums_block[1],
        sum_expand_bias,
        sum_shrink_bias,
    )
    return outgoing, input_grad, matrices, vectors


def shards(
    stem_input,
    image_class,
    owner,
    conv_in_weight,
    first_gain,
    first_bias,
    conv_mid_weight,
    second_gain,
    second_bias,
    conv_out_weight,
    third_gain,
    third_bias,
    embed_weight,
    embed_bias,
    position_table,
    attn_gain,
    attn_bias,
    joint_weight,
    query_bias,
    value_bias,
    mix_weight,
    mix_bias,
    mlp_gain,
    mlp_bias,
    expand_weight,
    expand_bias,
    shrink_weight,
    shrink_bias,
    cotangent,
):
    sections = lax.axis_size("section")
    devices = sections * lax.axis_size("batch")
    images = stem_input.shape[0]
    section_index = lax.axis_index("section")
    mine = lax.dynamic_index_in_dim(owner.reshape(sections, images), section_index, 0, keepdims=False)
    received = lax.all_to_all(cotangent[0], "section", split_axis=0, concat_axis=0, tiled=True)
    outgoing, input_grad, matrices, vectors = local_step(
        image_class,
        mine,
        stem_input,
        conv_in_weight,
        conv_mid_weight,
        conv_out_weight,
        (first_gain, first_bias, second_gain, second_bias, third_gain, third_bias),
        embed_weight,
        embed_bias,
        position_table,
        attn_gain,
        attn_bias,
        joint_weight,
        query_bias,
        value_bias,
        mix_weight,
        mix_bias,
        mlp_gain,
        mlp_bias,
        expand_weight,
        expand_bias,
        shrink_weight,
        shrink_bias,
        received,
    )
    block_output = lax.all_to_all(outgoing, "section", split_axis=0, concat_axis=0, tiled=True)[None]

    def scatter(matrix):
        parts = matrix.astype(bf16).reshape(devices, -1)
        size = parts.shape[1]
        padded = -(-size // LANES) * LANES
        if padded != size:
            parts = jnp.pad(parts, ((0, 0), (0, padded - size)))
        parts = parts.reshape(devices, -1, LANES)
        own = lax.psum_scatter(parts, BOTH, scatter_dimension=0, tiled=True)
        return own.astype(f32).reshape(-1)[:size]

    matrices = tuple(scatter(matrix) for matrix in matrices)
    sizes = [vector.shape[1] for vector in vectors]
    packed = lax.psum(jnp.concatenate([jnp.sum(vector, axis=0) for vector in vectors]), BOTH)
    small = []
    start = 0
    for size in sizes:
        small.append(packed[start : start + size])
        start += size
    return (
        block_output,
        input_grad,
        matrices[0],
        small[0],
        small[1],
        matrices[1],
        small[2],
        small[3],
        matrices[2],
        small[4],
        small[5],
        matrices[3],
        small[6],
        matrices[4],
        small[7],
        small[8],
        matrices[5],
        small[9],
        small[10],
        matrices[6],
        small[11],
        small[12],
        small[13],
        matrices[7],
        small[14],
        matrices[8],
        small[15],
    )


def solution(mesh):
    split = P(BOTH)
    images = P(BOTH, None, None)
    slots = P(BOTH, None, None, None)
    full = P()
    in_specs = (images, split, P("batch")) + (full,) * 25 + (slots,)
    out_specs = (
        slots,
        images,
        split,
        full,
        full,
        split,
        full,
        full,
        split,
        full,
        full,
        split,
        full,
        split,
        full,
        full,
        split,
        full,
        full,
        split,
        full,
        full,
        full,
        split,
        full,
        split,
        full,
    )
    return jax.shard_map(shards, mesh=mesh, in_specs=in_specs, out_specs=out_specs, check_vma=False)
```

time: 1370 us -> 1330 us (0.971)
  waiting for transfers between devices: 488 us -> 935 us
  matrix products: 317 us -> 0 us
  Pallas kernels: 0 us -> 254 us
  local copies, waits for them, and re-layouts: 290 us -> 57.2 us
  other arithmetic: 192 us -> 13.4 us
    reduce_scatter x0 -> x9, waiting for transfers between devices: none -> 935 us  [scatter(): own = lax.psum_scatter(parts, BOTH, scatter_dimension=0, tiled=True)]
    unnamed x2 -> x9, waiting for transfers between devices: 488 us -> 0.15 us
    dot_general x38 -> x0, matrix products: 317 us -> none  [the longest x8 72.3 us: right_product(): lax.dot_general(left, right, (((1,), (1,)), ((), ())), preferred_element_...]
    pallas_call x0 -> x5, Pallas kernels: none -> 254 us  [the longest x1 77.6 us: attend_backward(): pl.pallas_call(attend_backward_kernel, out_shape=(jax.ShapeDtypeStruct((i...]
    convert_element_type x16 -> x1, other arithmetic: 71.9 us -> 0.09 us  [scatter(): parts = matrix.astype(bf16).reshape(devices, -1)]
    reduce_sum x36 -> x6, other arithmetic: 68.4 us -> 0.15 us  [shards(): jnp.sum(vector, axis=0)]
    reshape x15 -> x10, local copies, waits for them, and re-layouts: 65.2 us -> 9.39 us  [the longest x9 8.66 us: local_step(): line = lambda vector: vector.reshape(1, -1)]
    unnamed x327 -> x48, local copies, waits for them, and re-layouts: 58.5 us -> 4.54 us
  transfers between devices with their start and end apart: 4 -> 11, of which waited for: 1 -> 9; matrix products, arithmetic and copies ran while one was open for 14% -> 5% of each run, Pallas kernels for 0% -> 6%
where the time goes in v1:
time: 1330 us
  waiting for transfers between devices  935 us (70%)
  Pallas kernels  254 us (19%)
  local copies, waits for them, and re-layouts  57.2 us (4%)
  blocking collectives  42.5 us (3%)
  between operations  14.5 us (1%)
  other arithmetic  13.4 us (1%)
    reduce_scatter x9, waiting for transfers between devices, scatter(): own = lax.psum_scatter(parts, BOTH, scatter_dimension=0, tiled=True)  935 us
    pallas_call x1, Pallas kernels, attend_backward(): pl.pallas_call(attend_backward_kernel, out_shape=(jax.ShapeDtypeStruct((i...  77.6 us
    pallas_call x1, Pallas kernels, feed(): pl.pallas_call(feed_kernel, out_shape=(jax.ShapeDtypeStruct((slots, cells...  54.4 us
    pallas_call x1, Pallas kernels, attend_forward(): pl.pallas_call(attend_forward_kernel, out_shape=(low, low, low, low, jax....  44.1 us
    pallas_call x1, Pallas kernels, stem_backward(): pl.pallas_call(stem_backward_kernel, out_shape=(jax.ShapeDtypeStruct((ima...  43.1 us
    psum x1, blocking collectives, shards(): lax.psum(jnp.concatenate([jnp.sum(vector, axis=0) for vector in vectors])...  42.5 us
    another operation x9, local copies, waits for them, and re-layouts, scatter(): parts = parts.reshape(devices, -1, LANES)  37.9 us
    pallas_call x1, Pallas kernels, stem_forward(): pl.pallas_call(stem_forward_kernel, out_shape=(jax.ShapeDtypeStruct((chan...  35.3 us
  transfers between devices with their start and end apart: 11, of which 9 were waited for; matrix products, arithmetic and copies ran while one was open for 5% of the time, Pallas kernels for 6%

profile of v1, /device:TPU:0, one launch (start us, length us, event | category | flops | bytes accessed | tf_op | source)
XLA Modules:
  0.0 1325.6 jit_solution(14961692931705208593)
XLA Ops:
  7.2 4.4 all-to-all-start
  11.6 0.6 reshape.172.embed_bias_ref
  12.2 0.6 reshape.173.gain1_ref
  12.8 0.6 reshape.178.gain2_ref
  13.4 0.6 reshape.174.bias1_ref
  14.0 1.3 reshape.175.query_bias_ref
  15.2 1.3 reshape.176.value_bias_ref
  16.5 1.3 reshape.177.mix_bias_ref
  17.8 1.3 reshape.179.bias2_ref
  19.0 0.7 reshape.164
  19.8 1.3 reshape.181.shrink_bias_ref
  21.0 35.3 %stem_forward.1 = (bf16[1024,256]{1,0:T(8,128)(2,1)}, bf16[2304,256]{1,0:T(8,128)(2,1)}, bf16[256,1024]{1,0:T(8,128)(2,1)}, f32[2,576,256]{2,1,0:T(8,128)}, f32[...) custom-call(s32[2]{0:T(128)} %class_ref.9, ...), custom_call_target="tpu_custom_call" | custom-call | tf_op jit(solution)/shard_map/stem_forward/pallas_call | solution.py:262
  56.4 44.1 %attend_forward.1 = (bf16[2,576,768]{2,1,0:T(8,128)(2,1)}, bf16[2,576,768]{2,1,0:T(8,128)(2,1)}, bf16[2,576,768]{2,1,0:T(8,128)(2,1)}, bf16[2,576,768]{2,1,0:T(8...) custom-call(s32[2]{0:T(128)} %class_ref.9, ...), custom_call_target="tpu_custom_call" | custom-call | tf_op jit(solution)/shard_map/attend_forward/pallas_call | solution.py:423
  100.5 0.5 dynamic-slice_bitcast_fusion.mine_ref
  101.0 1.8 copy-done
  102.8 54.4 %feed.1 = (bf16[4,576,768]{2,1,0:T(8,128)(2,1)}, f32[2,576,768]{2,1,0:T(8,128)}, bf16[3072,768]{1,0:T(8,128)(2,1)}, bf16[768,3072]{1,0:T(8,128)(2,1)}, f32[8,3072]{1,0:T(8,128)}, /*index=5*/f32[8,768]{1,0:T(8,128)}) custom-call(s32[2]{0:T(128)} %class_ref.9, s32[2]{0:T(128)} %dynamic-slice_bitcast_fusion.mine_ref, ...), custom_call_target="tpu_custom_call" | custom-call | tf_op jit(solution)/shard_map/feed/pallas_call | solution.py:539
  157.1 77.6 %attend_backward.1 = (bf16[2,576,768]{2,1,0:T(8,128)(2,1)}, bf16[768,2304]{1,0:T(8,128)(2,1)}, bf16[768,768]{1,0:T(8,128)(2,1)}, f32[7,8,768]{2,1,0:T(8,128)}) custom-call(s32[2]{0:T(128)} %class_ref.9, s32[2]{0:T(128)} %dynamic-slice_bitcast_fusion.mine_ref, bf16[2,576,768]{2,1,0:T(8,128)(2,1)} %get-tuple-element.66.tokens_ref, ...), custom_call_target="tpu_custom_call" | custom-call | tf_op jit(solution)/shard_map/attend_backward/pallas_call | solution.py:726
  234.7 43.1 %stem_backward.1 = (f32[2,576,1024]{2,1,0:T(8,128)}, bf16[1024,768]{1,0:T(8,128)(2,1)}, f32[576,768]{1,0:T(8,128)}, bf16[1024,256]{1,0:T(8,128)(2,1)}, bf16[2304...) custom-call(s32[2]{0:T(128)} %class_ref.9, ...), custom_call_target="tpu_custom_call" | custom-call | tf_op jit(solution)/shard_map/stem_backward/pallas_call | solution.py:986
  277.8 2.2 reshape_reshape.29
  280.0 0.0 reduce-scatter.10.cloned.1.call-start
  280.1 2.0 reshape_reshape.27
  282.1 0.0 reduce-scatter.12.cloned.1.call-start
  282.1 1.3 reshape_reshape.28
  283.4 0.0 reduce-scatter.22.cloned.1.call-start
  283.5 3.7 reshape_reshape.33
  287.2 0.0 reduce-scatter.18.cloned.1.call-start
  287.3 0.1 convert_element_type.2
  287.4 1.8 reshape_reshape.31
  289.2 0.0 reduce-scatter.16.cloned.1.call-start
  289.3 4.2 reshape_reshape.30
  293.5 0.0 reduce-scatter.20.cloned.1.call-start
  293.5 5.3 reshape_reshape.32
  298.8 0.0 reduce-scatter.26.cloned.1.call-start
  298.9 9.2 reshape_reshape.35
  308.1 0.0 reduce-scatter.26.cloned.1.call-update
  308.2 0.7 copy-done.9
  308.8 0.2 copy-done.6
  309.4 42.5 %psum.7 = f32[13056]{0:T(1024)S(1)} all-reduce(f32[13056]{0:T(1024)S(1)} %constant_dynamic-update-slice_fusion), channel_id=1, replica_groups=mesh['batch'=8,'section'=4] {'batch','section'}, use_global_device_ids=true, to_apply=%region_17.18 | all-reduce | flops 13056 | bytes 104448 | tf_op jit(solution)/shard_map/psum | solution.py:1264
  351.9 0.6 slice.130
  352.5 8.3 reshape_reshape.34
  360.9 3.7 all-to-all-start.1
  364.6 0.0 reduce-scatter.24.cloned.1.call-start
  364.6 1.4 fusion.2
  366.1 1.3 fusion.1
  367.4 1.5 fusion
  368.8 48.7 %reduce-scatter.14.cloned.1.call-done = bf16[1,64,128]{2,1,0:T(8,128)(2,1)} async-done(((bf16[32,64,128]{2,1,0:T(8,128)(2,1)}), bf16[1,64,128]{2,1,0:T(8,128)(2,1)}) %reduce-scatter.14.cloned.1.call-update) | async-done | bytes 16400 | tf_op jit(solution)/shard_map/reduce_scatter | solution.py:1259
  417.5 1.3 bitcast_convert_fusion.7
  418.9 131.2 %reduce-scatter.10.cloned.1.call-done = bf16[1,64,128]{2,1,0:T(8,128)(2,1)} async-done(((bf16[32,64,128]{2,1,0:T(8,128)(2,1)}), bf16[1,64,128]{2,1,0:T(8,128)(2,1)}) %reduce-scatter.10.cloned.1.call-update) | async-done | bytes 16400 | tf_op jit(solution)/shard_map/reduce_scatter | solution.py:1259
  550.1 1.3 bitcast_convert_fusion.8
  551.5 96.0 %reduce-scatter.12.cloned.1.call-done = bf16[1,144,128]{2,1,0:T(8,128)(2,1)} async-done(((bf16[32,144,128]{2,1,0:T(8,128)(2,1)}), bf16[1,144,128]{2,1,0:T(8,128)(2,1)}) %reduce-scatter.12.cloned.1.call-update) | async-done | bytes 36880 | tf_op jit(solution)/shard_map/reduce_scatter | solution.py:1259
  647.4 1.4 bitcast_convert_fusion.5
  648.8 98.8 %reduce-scatter.22.cloned.1.call-done = bf16[1,144,128]{2,1,0:T(8,128)(2,1)} async-done(((bf16[32,144,128]{2,1,0:T(8,128)(2,1)}), bf16[1,144,128]{2,1,0:T(8,128)(2,1)}) %reduce-scatter.22.cloned.1.call-update) | async-done | bytes 36880 | tf_op jit(solution)/shard_map/reduce_scatter | solution.py:1259
  747.7 1.4 bitcast_convert_fusion.4
  749.1 134.5 %reduce-scatter.18.cloned.1.call-done = bf16[1,108,128]{2,1,0:T(8,128)(2,1)} async-done(((bf16[32,108,128]{2,1,0:T(8,128)(2,1)}), bf16[1,108,128]{2,1,0:T(8,128)(2,1)}) %reduce-scatter.18.cloned.1.call-update) | async-done | bytes 27664 | tf_op jit(solution)/shard_map/reduce_scatter | solution.py:1259
  883.6 1.4 bitcast_convert_fusion.6
  884.9 97.5 %reduce-scatter.16.cloned.1.call-done = bf16[1,192,128]{2,1,0:T(8,128)(2,1)} async-done(((bf16[32,192,128]{2,1,0:T(8,128)(2,1)}), bf16[1,192,128]{2,1,0:T(8,128)(2,1)}) %reduce-scatter.16.cloned.1.call-update) | async-done | bytes 49168 | tf_op jit(solution)/shard_map/reduce_scatter | solution.py:1259
  982.5 1.4 bitcast_convert_fusion.3
  983.9 107.7 %reduce-scatter.20.cloned.1.call-done = bf16[1,432,128]{2,1,0:T(8,128)(2,1)} async-done(((bf16[32,432,128]{2,1,0:T(8,128)(2,1)}), bf16[1,432,128]{2,1,0:T(8,128)(2,1)}) %reduce-scatter.20.cloned.1.call-update) | async-done | bytes 110608 | tf_op jit(solution)/shard_map/reduce_scatter | solution.py:1259
  1091.6 1.6 bitcast_convert_fusion.2
  1093.2 110.6 %reduce-scatter.26.cloned.1.call-done = bf16[1,576,128]{2,1,0:T(8,128)(2,1)} async-done(((bf16[32,576,128]{2,1,0:T(8,128)(2,1)}), bf16[1,576,128]{2,1,0:T(8,128)(2,1)}) %reduce-scatter.26.cloned.1.call-update) | async-done | bytes 147472 | tf_op jit(solution)/shard_map/reduce_scatter | solution.py:1259
  1203.8 1.6 bitcast_convert_fusion
  1205.5 109.9 %reduce-scatter.24.cloned.1.call-done = bf16[1,576,128]{2,1,0:T(8,128)(2,1)} async-done(((bf16[32,576,128]{2,1,0:T(8,128)(2,1)}), bf16[1,576,128]{2,1,0:T(8,128)(2,1)}) %reduce-scatter.24.cloned.1.call-update) | async-done | bytes 147472 | tf_op jit(solution)/shard_map/reduce_scatter | solution.py:1259
  1315.4 1.6 bitcast_convert_fusion.1
  1317.0 1.8 copy.73
  (63 shorter events, 0.4 us)
Async XLA Ops:
  7.2 4.4 copy-start.12
  7.2 5.0 copy-start.13
  7.2 5.6 copy-start.14
  7.2 6.1 copy-start.15
  7.2 93.7 %all-to-all-start = ((bf16[4,576,768]{2,1,0:T(8,128)(2,1)}), bf16[4,576,768]{2,1,0:T(8,128)(2,1)S(1)}, u32[]{:S(2)}, u32[]{:S(2)}) async-start(bf16[4,576,768]{2,1,0:T(8,128)(2,1)} %bitcast.42), calls=%async_computation | async-start | bytes 7077888 | tf_op jit(solution)/shard_map/all_to_all | solution.py:1223
  11.6 405.9 %reduce-scatter.14.cloned.1.call-start = ((), (), s32[]{:S(2)}) async-start(), calls=%async_computation.13 | async-start | bytes 540672 | tf_op jit(solution)/shard_map/reduce_scatter | solution.py:1259
  101.0 1.8 copy-start
  277.8 4.3 copy-start.3
  280.0 270.1 %reduce-scatter.10.cloned.1.call-start = ((), (), s32[]{:S(2)}) async-start(), calls=%async_computation.11 | async-start | bytes 540672 | tf_op jit(solution)/shard_map/reduce_scatter | solution.py:1259
  282.1 365.3 %reduce-scatter.12.cloned.1.call-start = ((), (), s32[]{:S(2)}) async-start(), calls=%async_computation.12 | async-start | bytes 1216512 | tf_op jit(solution)/shard_map/reduce_scatter | solution.py:1259
  283.4 464.2 %reduce-scatter.22.cloned.1.call-start = ((), (), s32[]{:S(2)}) async-start(), calls=%async_computation.17 | async-start | bytes 1216512 | tf_op jit(solution)/shard_map/reduce_scatter | solution.py:1259
  283.5 3.8 copy-start.2
  287.2 596.4 %reduce-scatter.18.cloned.1.call-start = ((), (), s32[]{:S(2)}) async-start(), calls=%async_computation.15 | async-start | bytes 946176 | tf_op jit(solution)/shard_map/reduce_scatter | solution.py:1259
  289.2 693.3 %reduce-scatter.16.cloned.1.call-start = ((), (), s32[]{:S(2)}) async-start(), calls=%async_computation.14 | async-start | bytes 1622016 | tf_op jit(solution)/shard_map/reduce_scatter | solution.py:1259
  289.2 4.3 copy-start.1
  293.5 798.1 %reduce-scatter.20.cloned.1.call-start = ((), (), s32[]{:S(2)}) async-start(), calls=%async_computation.16 | async-start | bytes 3649536 | tf_op jit(solution)/shard_map/reduce_scatter | solution.py:1259
  298.8 905.0 %reduce-scatter.26.cloned.1.call-start = ((), (), s32[]{:S(2)}) async-start(), calls=%async_computation.19 | async-start | bytes 4866048 | tf_op jit(solution)/shard_map/reduce_scatter | solution.py:1259
  308.1 0.7 copy-start.9
  308.1 0.9 copy-start.6
  308.1 0.9 copy-start.8
  308.1 1.0 copy-start.10
  308.1 1.0 copy-start.11
  308.1 1.0 copy-start.7
  308.1 1.1 copy-start.5
  351.9 9.0 copy-start.4
  360.9 623.1 %all-to-all-start.1 = ((bf16[4,576,768]{2,1,0:T(8,128)(2,1)}), bf16[4,576,768]{2,1,0:T(8,128)(2,1)S(1)}, u32[]{:S(2)}, u32[]{:S(2)}) async-start(bf16[4,576,768]{2,1,0:T(8,128)(2,1)} %get-tuple-element.69), calls=%async_computation.1 | async-start | bytes 7077888 | tf_op jit(solution)/shard_map/all_to_all | solution.py:1250
  364.6 950.8 %reduce-scatter.24.cloned.1.call-start = ((), (), s32[]{:S(2)}) async-start(), calls=%async_computation.18 | async-start | bytes 4866048 | tf_op jit(solution)/shard_map/reduce_scatter | solution.py:1259
Sparse Core Ops, SparseCore 0:
  280.1 137.3 reduce-scatter.13
  419.9 130.2 reduce-scatter.9
  555.2 92.1 reduce-scatter.11
  652.4 95.2 reduce-scatter.21
  749.7 133.7 reduce-scatter.17
  889.5 92.9 reduce-scatter.15
  989.4 102.1 reduce-scatter.19
  1098.0 105.8 reduce-scatter.25
  1209.3 106.0 reduce-scatter.23

commit v2 on v1

v2 whole, which is shorter than its diff:
```python
import jax
import jax.numpy as jnp
from jax import lax
from jax.experimental import pallas as pl
from jax.experimental.pallas import tpu as pltpu
from jax.sharding import PartitionSpec as P

HEADS = 12
GROUPS = 32
SIDE = 24
SIDE_SMALL = 14
LANES = 128
MIB = 1024 * 1024
BOTH = ("batch", "section")

f32 = jnp.float32
bf16 = jnp.bfloat16


def dot_nn(left, right):
    return jnp.dot(left, right, preferred_element_type=f32)


def dot_tn(left, right):
    return lax.dot_general(left, right, (((0,), (0,)), ((), ())), preferred_element_type=f32)


def dot_nt(left, right):
    return lax.dot_general(left, right, (((1,), (1,)), ((), ())), preferred_element_type=f32)


def fold(values):
    rows, columns = values.shape
    return jnp.sum(values.reshape(rows // 8, 8, columns), axis=0)


def total(values):
    return jnp.sum(values, axis=0, keepdims=True)


def line(ref):
    return ref[...].reshape(1, -1)


def spread_lanes(mask, columns):
    return jnp.concatenate([mask] * (columns // LANES), axis=1)


def cdf_pdf(values):
    bell = jnp.exp(-0.5 * (values * values))
    t = 1.0 / (1.0 + 0.23164189 * jnp.abs(values))
    tail = (
        ((((0.5307027145 * t - 0.7265760135) * t + 0.7107068705) * t - 0.142248368) * t + 0.127414796)
        * t
        * bell
    )
    return jnp.where(values < 0.0, tail, 1.0 - tail), bell * 0.3989422804014327


def group_total(row, per_group):
    channels = row.shape[1]
    rows = jnp.broadcast_to(row, (8, channels))
    lane = lax.broadcasted_iota(jnp.int32, (8, LANES), 1)
    parts = []
    for k in range(channels // LANES):
        part = rows[:, k * LANES : (k + 1) * LANES]
        step = 1
        while step < per_group:
            up = pltpu.roll(part, LANES - step, 1)
            down = pltpu.roll(part, step, 1)
            part = part + jnp.where((lane & step) == 0, up, down)
            step *= 2
        parts.append(part)
    return jnp.concatenate(parts, axis=1)[0:1]


def cell_grid(cells):
    cell = lax.broadcasted_iota(jnp.int32, (cells, LANES), 0).astype(f32)
    row = jnp.floor((cell + 0.5) * (1.0 / SIDE))
    return row, cell - row * SIDE


def validity_mask(image_class, cells):
    row, column = cell_grid(cells)
    corner = jnp.where((row < SIDE_SMALL) & (column < SIDE_SMALL), 1.0, 0.0)
    return jnp.where(image_class == 1, 1.0, corner)


def valid_count(image_class):
    return jnp.where(image_class == 1, float(SIDE * SIDE), float(SIDE_SMALL * SIDE_SMALL))


def rows_at(index, size):
    return pl.ds(pl.multiple_of(index * size, size), size)


def fill_columns(grid_value, padded, columns, sign):
    cells, channels = grid_value.shape
    _, column = cell_grid(cells)
    has_left = spread_lanes(jnp.where(column > 0.5, 1.0, 0.0), channels)
    has_right = spread_lanes(jnp.where(column < SIDE - 1.5, 1.0, 0.0), channels)
    zeros = jnp.zeros((SIDE, channels), f32)
    shifted = (
        pltpu.roll(grid_value, 1, 0) * has_left,
        grid_value,
        pltpu.roll(grid_value, cells - 1, 0) * has_right,
    )
    for k in range(3):
        padded[k, 0:SIDE, :] = zeros
        padded[k, SIDE + cells : 2 * SIDE + cells, :] = zeros
        padded[k, SIDE : SIDE + cells, :] = shifted[k]
    for row_shift in range(3):
        for column_shift in range(3):
            tap = row_shift * 3 + column_shift
            down = row_shift if sign > 0 else 2 - row_shift
            across = column_shift if sign > 0 else 2 - column_shift
            columns[:, tap * channels : (tap + 1) * channels] = padded[
                across, down * SIDE : down * SIDE + cells, :
            ].astype(bf16)


def standardized(weight):
    rows = weight.shape[0]
    centred = weight - total(weight) * (1.0 / rows)
    spread = total(centred * centred) * (1.0 / rows)
    scale = lax.rsqrt(spread + 1e-05)
    return centred * scale, scale


def standardize_back(weight, grad):
    rows = weight.shape[0]
    normal, scale = standardized(weight)
    grad_mean = total(grad) * (1.0 / rows)
    inner = total(grad * normal) * (1.0 / rows)
    return scale * (grad - grad_mean - normal * inner)


PAIRS = 16
VECTORS = 3


def store_split(ref, start, values):
    high = values.astype(bf16)
    low = (values - high.astype(f32)).astype(bf16)
    shape = (VECTORS, 8, values.shape[-1])
    ref[start : start + VECTORS] = high.astype(f32).reshape(shape).astype(bf16)
    ref[start + VECTORS : start + 2 * VECTORS] = low.astype(f32).reshape(shape).astype(bf16)


def load_split(ref, start):
    high = ref[start : start + VECTORS].astype(f32)
    low = ref[start + VECTORS : start + 2 * VECTORS].astype(f32)
    rows = high + low
    return rows.reshape(VECTORS * 8, rows.shape[-1])


def sections_of(values):
    rows, columns = values.shape
    return values.reshape(rows // 8, 8, columns).astype(bf16)


def stem_forward_kernel(
    class_ref,
    x_ref,
    w_in_ref,
    w_mid_ref,
    w_out_ref,
    gain1_ref,
    bias1_ref,
    gain2_ref,
    bias2_ref,
    gain3_ref,
    bias3_ref,
    embed_ref,
    embed_bias_ref,
    position_ref,
    std_in_ref,
    std_mid_ref,
    std_out_ref,
    first_ref,
    second_ref,
    third_ref,
    stat1_ref,
    stat2_ref,
    stat3_ref,
    stem_ref,
    tokens_ref,
    mask,
    padded,
    columns,
    act_two,
):
    image = pl.program_id(0)
    cells = x_ref.shape[1]
    channels = x_ref.shape[2]
    middle = w_in_ref.shape[1]

    @pl.when(image == 0)
    def _():
        std_in_ref[...] = standardized(w_in_ref[...].astype(f32))[0].astype(bf16)
        std_mid_ref[...] = standardized(w_mid_ref[...].astype(f32))[0].astype(bf16)
        std_out_ref[...] = standardized(w_out_ref[...].astype(f32))[0].astype(bf16)

    image_class = class_ref[image]
    mask[...] = validity_mask(image_class, cells)
    count = valid_count(image_class)
    chunk = 96
    steps = cells // chunk

    def stats(values_ref, stat_ref, sums):
        width = values_ref.shape[2]
        per_group = width // GROUPS
        inverse = 1.0 / (count * per_group)
        centre = group_total(total(sums), per_group) * inverse

        def one(step, carry):
            rows = rows_at(step, chunk)
            centred = (values_ref[0, rows, :] - centre) * spread_lanes(mask[rows, :], width)
            return carry + fold(centred * centred)

        squares = lax.fori_loop(0, steps, one, jnp.zeros((8, width), f32))
        scale = lax.rsqrt(group_total(total(squares), per_group) * inverse + 1e-05)
        stat_ref[0, 0:1, :] = centre
        stat_ref[0, 1:2, :] = scale
        return centre, scale

    def first_step(step, carry):
        rows = rows_at(step, chunk)
        low = (x_ref[0, rows, :] * spread_lanes(mask[rows, :], channels)).astype(bf16)
        values = dot_nn(low, std_in_ref[...])
        first_ref[0, rows, :] = values
        return carry + fold(values)

    sums = lax.fori_loop(0, steps, first_step, jnp.zeros((8, middle), f32))
    centre, scale = stats(first_ref, stat1_ref, sums)
    gain = scale * line(gain1_ref)
    normed = (first_ref[0] - centre) * gain + line(bias1_ref)
    act = normed * cdf_pdf(normed)[0] * spread_lanes(mask[...], middle)
    fill_columns(act, padded, columns, 1)

    def second_step(step, carry):
        rows = rows_at(step, chunk)
        values = dot_nn(columns[rows, :], std_mid_ref[...])
        second_ref[0, rows, :] = values
        return carry + fold(values * spread_lanes(mask[rows, :], middle))

    sums = lax.fori_loop(0, steps, second_step, jnp.zeros((8, middle), f32))
    centre, scale = stats(second_ref, stat2_ref, sums)
    gain = scale * line(gain2_ref)
    normed = (second_ref[0] - centre) * gain + line(bias2_ref)
    act_two[...] = (normed * cdf_pdf(normed)[0] * spread_lanes(mask[...], middle)).astype(bf16)

    def third_step(step, carry):
        rows = rows_at(step, chunk)
        values = dot_nn(act_two[rows, :], std_out_ref[...])
        third_ref[0, rows, :] = values
        return carry + fold(values)

    sums = lax.fori_loop(0, steps, third_step, jnp.zeros((8, channels), f32))
    centre, scale = stats(third_ref, stat3_ref, sums)
    gain = scale * line(gain3_ref)

    @pl.loop(0, steps)
    def _(step):
        rows = rows_at(step, chunk)
        keep = mask[rows, :]
        keep_wide = spread_lanes(keep, channels)
        argument = (
            x_ref[0, rows, :] * keep_wide + (third_ref[0, rows, :] - centre) * gain + line(bias3_ref)
        )
        stem = (argument * cdf_pdf(argument)[0] * keep_wide).astype(bf16)
        stem_ref[0, rows, :] = stem
        values = dot_nn(stem, embed_ref[...]) + line(embed_bias_ref) + position_ref[rows, :].astype(f32)
        tokens_ref[0, rows, :] = (values * spread_lanes(keep, values.shape[1])).astype(bf16)


def cost(flops, moved):
    return pl.CostEstimate(flops=flops, bytes_accessed=moved, transcendentals=0)


def whole(shape):
    return pl.BlockSpec(shape, lambda *_: (0,) * len(shape))


def per_image(shape):
    return pl.BlockSpec((1,) + shape, lambda image, *_: (image,) + (0,) * len(shape))


def stem_forward(image_class, x, w_in, w_mid, w_out, norms, embed, embed_bias, position):
    images, cells, channels = x.shape
    middle = w_in.shape[1]
    width = embed.shape[1]
    row = lambda size: whole((size,))
    return pl.pallas_call(
        stem_forward_kernel,
        out_shape=(
            jax.ShapeDtypeStruct((channels, middle), bf16),
            jax.ShapeDtypeStruct((9 * middle, middle), bf16),
            jax.ShapeDtypeStruct((middle, channels), bf16),
            jax.ShapeDtypeStruct((images, cells, middle), f32),
            jax.ShapeDtypeStruct((images, cells, middle), f32),
            jax.ShapeDtypeStruct((images, cells, channels), f32),
            jax.ShapeDtypeStruct((images, 8, middle), f32),
            jax.ShapeDtypeStruct((images, 8, middle), f32),
            jax.ShapeDtypeStruct((images, 8, channels), f32),
            jax.ShapeDtypeStruct((images, cells, channels), bf16),
            jax.ShapeDtypeStruct((images, cells, width), bf16),
        ),
        grid_spec=pltpu.PrefetchScalarGridSpec(
            num_scalar_prefetch=1,
            grid=(images,),
            in_specs=[
                per_image((cells, channels)),
                whole((channels, middle)),
                whole((9 * middle, middle)),
                whole((middle, channels)),
                row(middle),
                row(middle),
                row(middle),
                row(middle),
                row(channels),
                row(channels),
                whole((channels, width)),
                row(width),
                whole((cells, width)),
            ],
            out_specs=[
                whole((channels, middle)),
                whole((9 * middle, middle)),
                whole((middle, channels)),
                per_image((cells, middle)),
                per_image((cells, middle)),
                per_image((cells, channels)),
                per_image((8, middle)),
                per_image((8, middle)),
                per_image((8, channels)),
                per_image((cells, channels)),
                per_image((cells, width)),
            ],
            scratch_shapes=[
                pltpu.VMEM((cells, LANES), f32),
                pltpu.VMEM((3, cells + 2 * SIDE, middle), f32),
                pltpu.VMEM((cells, 9 * middle), bf16),
                pltpu.VMEM((cells, middle), bf16),
            ],
        ),
        compiler_params=pltpu.CompilerParams(vmem_limit_bytes=62 * MIB),
        cost_estimate=cost(25_000_000_000, 30 * MIB),
        name="stem_forward",
    )(image_class, x, w_in, w_mid, w_out, *norms, embed, embed_bias, position)


def row_norm(values):
    centre = jnp.mean(values, axis=-1, keepdims=True)
    centred = values - centre
    scale = lax.rsqrt(jnp.mean(centred * centred, axis=-1, keepdims=True) + 1e-06)
    return centred * scale, scale


def attend_forward_kernel(
    class_ref,
    tokens_ref,
    gain1_ref,
    bias1_ref,
    joint_ref,
    query_bias_ref,
    value_bias_ref,
    mix_ref,
    mix_bias_ref,
    gain2_ref,
    bias2_ref,
    normed_ref,
    query_ref,
    key_ref,
    value_ref,
    log_total_ref,
    mixed_ref,
    resid_ref,
    normed_two_ref,
):
    image = pl.program_id(0)
    cells, width = tokens_ref.shape[1:]
    chunk = 96
    steps = cells // chunk
    scale = (width // HEADS) ** -0.5

    @pl.loop(0, steps)
    def _(step):
        rows = rows_at(step, chunk)
        normal, _ = row_norm(tokens_ref[0, rows, :].astype(f32))
        normed_ref[0, rows, :] = (normal * line(gain1_ref) + line(bias1_ref)).astype(bf16)

    block = 256
    query_bias = line(query_bias_ref)
    value_bias = line(value_bias_ref)
    for start in range(0, width, block):
        here = slice(start, start + block)
        later = slice(width + start, width + start + block)
        last = slice(2 * width + start, 2 * width + start + block)
        normed = normed_ref[0]
        query = dot_nn(normed, joint_ref[:, here]) + query_bias[:, here]
        query_ref[0, :, here] = query.astype(bf16)
        key_ref[0, :, here] = dot_nn(normed, joint_ref[:, later]).astype(bf16)
        value = dot_nn(normed, joint_ref[:, last]) + value_bias[:, here]
        value_ref[0, :, here] = value.astype(bf16)

    _, column = cell_grid(cells)
    image_class = class_ref[image]
    cell = lax.broadcasted_iota(jnp.int32, (8, cells), 1).astype(f32)
    cell_row = jnp.floor((cell + 0.5) * (1.0 / SIDE))
    cell_column = cell - cell_row * SIDE
    outside = jnp.where((cell_row < SIDE_SMALL) & (cell_column < SIDE_SMALL), 0.0, -1000000000.0)
    key_bias = jnp.where(image_class == 1, 0.0, outside)[0:1]
    upper = lax.broadcasted_iota(jnp.int32, (cells, LANES), 1) >= LANES // 2

    @pl.loop(0, width // LANES)
    def _(pair):
        lanes = rows_at(pair, LANES)
        query = query_ref[0, :, lanes] * bf16(scale)
        key = key_ref[0, :, lanes]
        value = value_ref[0, :, lanes]
        outs = []
        for half in range(2):
            mine = upper if half else jnp.logical_not(upper)
            scores = dot_nt(jnp.where(mine, query, bf16(0)), key) + key_bias
            top = jnp.max(scores, axis=-1, keepdims=True)
            weights = jnp.exp(scores - top)
            weight_sum = jnp.sum(weights, axis=-1, keepdims=True)
            probs = (weights * (1.0 / weight_sum)).astype(bf16)
            outs.append(dot_nn(probs, value))
            log_total = jnp.broadcast_to(top + jnp.log(weight_sum), (cells, LANES))
            log_total_ref[0, 2 * pair + half] = log_total.T[0:8]
        mixed_ref[0, :, lanes] = jnp.where(upper, outs[1], outs[0]).astype(bf16)

    @pl.loop(0, steps)
    def _(step):
        rows = rows_at(step, chunk)
        resid = (
            tokens_ref[0, rows, :].astype(f32)
            + dot_nn(mixed_ref[0, rows, :], mix_ref[...])
            + line(mix_bias_ref)
        )
        resid_ref[0, rows, :] = resid
        normal, _ = row_norm(resid)
        normed_two_ref[0, rows, :] = (normal * line(gain2_ref) + line(bias2_ref)).astype(bf16)


def attend_forward(
    image_class, tokens, gain1, bias1, joint, query_bias, value_bias, mix, mix_bias, gain2, bias2
):
    images, cells, width = tokens.shape
    row = whole((width,))
    low = jax.ShapeDtypeStruct((images, cells, width), bf16)
    low_spec = per_image((cells, width))
    return pl.pallas_call(
        attend_forward_kernel,
        out_shape=(
            low,
            low,
            low,
            low,
            jax.ShapeDtypeStruct((images, HEADS, 8, cells), f32),
            low,
            jax.ShapeDtypeStruct((images, cells, width), f32),
            low,
        ),
        grid_spec=pltpu.PrefetchScalarGridSpec(
            num_scalar_prefetch=1,
            grid=(images,),
            in_specs=[
                low_spec,
                row,
                row,
                whole((width, 3 * width)),
                row,
                row,
                whole((width, width)),
                row,
                row,
                row,
            ],
            out_specs=[
                low_spec,
                low_spec,
                low_spec,
                low_spec,
                per_image((HEADS, 8, cells)),
                low_spec,
                low_spec,
                low_spec,
            ],
        ),
        compiler_params=pltpu.CompilerParams(vmem_limit_bytes=62 * MIB),
        cost_estimate=cost(35_000_000_000, 30 * MIB),
        name="attend_forward",
    )(image_class, tokens, gain1, bias1, joint, query_bias, value_bias, mix, mix_bias, gain2, bias2)


def feed_kernel(
    class_ref,
    mine_ref,
    core_ref,
    normed_ref,
    resid_ref,
    cotangent_ref,
    expand_ref,
    expand_bias_ref,
    shrink_ref,
    shrink_bias_ref,
    output_ref,
    grad_normed_ref,
    shrink_mine_ref,
    shrink_other_ref,
    expand_mine_ref,
    expand_other_ref,
    grad_expand_bias_ref,
    grad_shrink_bias_ref,
    sent,
    result,
    hidden,
    grad_pre,
    normed_turned,
    shrink_total,
    expand_total,
    biases,
):
    step = pl.program_id(0)
    images, cells, width = normed_ref.shape
    block = expand_ref.shape[1]
    part = cells // 2

    @pl.when(step == 0)
    def _():
        sums = jnp.zeros((8, width), f32)
        for image in range(images):
            keep = spread_lanes(validity_mask(class_ref[image], cells), width)
            grad = cotangent_ref[mine_ref[image]].astype(f32) * keep
            sent[image * cells : (image + 1) * cells, :] = grad.astype(bf16)
            sums = sums + fold(grad)
            result[image * cells : (image + 1) * cells, :] = resid_ref[image] + line(shrink_bias_ref)
            normed_turned[:, image * cells : (image + 1) * cells] = normed_ref[image].T
        grad_shrink_bias_ref[...] = sums
        grad_normed_ref[...] = jnp.zeros_like(grad_normed_ref)
        every = line(expand_bias_ref)
        for k in range(biases.shape[0]):
            biases[k : k + 1, :] = every[:, k * block : (k + 1) * block]

    bias_sums = jnp.zeros((8, expand_ref.shape[1]), f32)
    for image in range(images):
        for piece in range(cells // part):
            local = slice(piece * part, (piece + 1) * part)
            rows = slice(image * cells + piece * part, image * cells + (piece + 1) * part)
            pre = dot_nn(normed_ref[image, local, :], expand_ref[...]) + biases[pl.ds(step, 1), :]
            back = dot_nt(sent[rows, :], shrink_ref[...])
            cdf, pdf = cdf_pdf(pre)
            low = (pre * cdf).astype(bf16)
            hidden[rows, :] = low
            grad = back * (cdf + pre * pdf)
            bias_sums = bias_sums + fold(grad)
            grad_low = grad.astype(bf16)
            grad_pre[rows, :] = grad_low
            result[rows, :] += dot_nn(low, shrink_ref[...])
            grad_normed_ref[image, local, :] += dot_nt(grad_low, expand_ref[...])
    grad_expand_bias_ref[...] = bias_sums
    shrink_total[...] = dot_tn(hidden[...], sent[...])
    expand_total[...] = dot_nn(normed_turned[...], grad_pre[...])
    core = core_ref[0]
    size = shrink_mine_ref.shape[1] * 8
    for pair in range(shrink_mine_ref.shape[0]):
        at = pl.multiple_of((2 * pair + core) * size, 8)
        shrink_mine_ref[pair] = sections_of(shrink_total[pl.ds(at, size), :])
        at = pl.multiple_of((2 * pair + 1 - core) * size, 8)
        shrink_other_ref[pair] = sections_of(shrink_total[pl.ds(at, size), :])
    size = expand_mine_ref.shape[1] * 8
    for pair in range(PAIRS):
        at = pl.multiple_of((2 * pair + core) * size, 8)
        expand_mine_ref[pair] = sections_of(expand_total[pl.ds(at, size), :])
        at = pl.multiple_of((2 * pair + 1 - core) * size, 8)
        expand_other_ref[pair] = sections_of(expand_total[pl.ds(at, size), :])

    @pl.when(step == pl.num_programs(0) - 1)
    def _():
        output_ref[...] = jnp.zeros_like(output_ref)
        for image in range(images):
            keep = spread_lanes(validity_mask(class_ref[image], cells), width)
            rows = result[image * cells : (image + 1) * cells, :] * keep
            output_ref[mine_ref[image]] = rows.astype(bf16)


def feed(image_class, mine, core, normed, resid, cotangent, expand, expand_bias, shrink, shrink_bias):
    images, cells, width = normed.shape
    inner = expand.shape[1]
    slots = cotangent.shape[0]
    block = width // 2
    rows = images * cells
    shrink_size = inner // (2 * PAIRS)
    pairs = block // (2 * shrink_size)
    expand_size = width // (2 * PAIRS)
    shrink_half = jax.ShapeDtypeStruct((PAIRS, shrink_size // 8, 8, width), bf16)
    expand_half = jax.ShapeDtypeStruct((PAIRS, expand_size // 8 * (inner // width), 8, width), bf16)
    shrink_spec = pl.BlockSpec((pairs, shrink_size // 8, 8, width), lambda step, *_: (step, 0, 0, 0))
    expand_spec = pl.BlockSpec(
        (PAIRS, expand_size // 8, 8, block), lambda step, *_: (0, step // 2, 0, step % 2)
    )
    return pl.pallas_call(
        feed_kernel,
        out_shape=(
            jax.ShapeDtypeStruct((slots, cells, width), bf16),
            jax.ShapeDtypeStruct((images, cells, width), f32),
            shrink_half,
            shrink_half,
            expand_half,
            expand_half,
            jax.ShapeDtypeStruct((8, inner), f32),
            jax.ShapeDtypeStruct((8, width), f32),
        ),
        grid_spec=pltpu.PrefetchScalarGridSpec(
            num_scalar_prefetch=3,
            grid=(inner // block,),
            in_specs=[
                whole((images, cells, width)),
                whole((images, cells, width)),
                whole((slots, cells, width)),
                pl.BlockSpec((width, block), lambda step, *_: (0, step)),
                whole((inner,)),
                pl.BlockSpec((block, width), lambda step, *_: (step, 0)),
                whole((width,)),
            ],
            out_specs=[
                whole((slots, cells, width)),
                whole((images, cells, width)),
                shrink_spec,
                shrink_spec,
                expand_spec,
                expand_spec,
                pl.BlockSpec((8, block), lambda step, *_: (0, step)),
                whole((8, width)),
            ],
            scratch_shapes=[
                pltpu.VMEM((rows, width), bf16),
                pltpu.VMEM((rows, width), f32),
                pltpu.VMEM((rows, block), bf16),
                pltpu.VMEM((rows, block), bf16),
                pltpu.VMEM((width, rows), bf16),
                pltpu.VMEM((block, width), f32),
                pltpu.VMEM((width, block), f32),
                pltpu.VMEM((inner // block, block), f32),
            ],
        ),
        compiler_params=pltpu.CompilerParams(vmem_limit_bytes=62 * MIB),
        cost_estimate=cost(12 * rows * width * inner, 40 * MIB),
        name="feed",
    )(image_class, mine, core, normed, resid, cotangent, expand, expand_bias, shrink, shrink_bias)


def row_norm_back(grad, normal, scale, gain):
    inner = grad * gain
    mean = jnp.mean(inner, axis=-1, keepdims=True)
    cross = jnp.mean(inner * normal, axis=-1, keepdims=True)
    return scale * (inner - mean - normal * cross)


def mix_backward_kernel(
    class_ref,
    mine_ref,
    resid_ref,
    cotangent_ref,
    grad_normed_two_ref,
    mix_ref,
    gain2_ref,
    grad_resid_ref,
    grad_mixed_ref,
    sums_ref,
    mask,
):
    image = pl.program_id(0)
    cells, width = resid_ref.shape[1:]
    chunk = 96
    mask[...] = validity_mask(class_ref[image], cells)

    @pl.when(image == 0)
    def _():
        sums_ref[...] = jnp.zeros_like(sums_ref)

    @pl.loop(0, cells // chunk)
    def _(step):
        rows = rows_at(step, chunk)
        normal, row_scale = row_norm(resid_ref[0, rows, :])
        grad = grad_normed_two_ref[0, rows, :]
        sums_ref[0] += fold(grad * normal)
        sums_ref[1] += fold(grad)
        keep = spread_lanes(mask[rows, :], width)
        grad = cotangent_ref[0, rows, :].astype(f32) * keep + row_norm_back(
            grad, normal, row_scale, line(gain2_ref)
        )
        sums_ref[2] += fold(grad)
        grad_resid_ref[0, rows, :] = grad
        grad_mixed_ref[0, rows, :] = dot_nt(grad.astype(bf16), mix_ref[...]).astype(bf16)


def mix_backward(image_class, mine, resid, cotangent, grad_normed_two, mix, gain2):
    images, cells, width = resid.shape
    rows = per_image((cells, width))
    return pl.pallas_call(
        mix_backward_kernel,
        out_shape=(
            jax.ShapeDtypeStruct((images, cells, width), f32),
            jax.ShapeDtypeStruct((images, cells, width), bf16),
            jax.ShapeDtypeStruct((3, 8, width), f32),
        ),
        grid_spec=pltpu.PrefetchScalarGridSpec(
            num_scalar_prefetch=2,
            grid=(images,),
            in_specs=[
                rows,
                pl.BlockSpec((1, cells, width), lambda image, classes, mine: (mine[image], 0, 0)),
                rows,
                whole((width, width)),
                whole((width,)),
            ],
            out_specs=[rows, rows, whole((3, 8, width))],
            scratch_shapes=[pltpu.VMEM((cells, LANES), f32)],
        ),
        compiler_params=pltpu.CompilerParams(vmem_limit_bytes=62 * MIB),
        cost_estimate=cost(2 * images * cells * width * width, 20 * MIB),
        name="mix_backward",
    )(image_class, mine, resid, cotangent, grad_normed_two, mix, gain2)


def attend_backward_kernel(
    class_ref,
    query_ref,
    key_ref,
    value_ref,
    log_total_ref,
    grad_mixed_ref,
    feed_expand_ref,
    feed_shrink_ref,
    mix_sums_ref,
    grad_joint_ref,
    vectors_ref,
    sums_ref,
):
    image = pl.program_id(0)
    cells, width = query_ref.shape[1:]
    scale = (width // HEADS) ** -0.5

    @pl.when(image == 0)
    def _():
        sums_ref[...] = jnp.zeros_like(sums_ref)
        vectors_ref[...] = jnp.zeros_like(vectors_ref)
        for k in range(feed_expand_ref.shape[1] // width):
            vectors_ref[k : k + 1, :] = total(feed_expand_ref[:, k * width : (k + 1) * width])
        vectors_ref[4:5, :] = total(feed_shrink_ref[...])
        for k in range(3):
            vectors_ref[5 + k : 6 + k, :] = total(mix_sums_ref[k])

    upper = lax.broadcasted_iota(jnp.int32, (cells, LANES), 1) >= LANES // 2
    key_bias = (validity_mask(class_ref[image], cells) - 1.0) * 1000000000.0
    bias_wide = jnp.concatenate([key_bias] * 5, axis=1)[:, :cells]

    @pl.loop(0, width // LANES)
    def _(pair):
        lanes = rows_at(pair, LANES)
        query = query_ref[0, :, lanes] * bf16(scale)
        key = key_ref[0, :, lanes]
        value = value_ref[0, :, lanes]
        grad_out = grad_mixed_ref[0, :, lanes]
        grads = []
        for half in range(2):
            mine = upper if half else jnp.logical_not(upper)
            scores = dot_nt(jnp.where(mine, key, bf16(0)), query)
            log_total = log_total_ref[0, 2 * pair + half, 0:1, :]
            probs = jnp.exp(scores + bias_wide - log_total)
            grad_probs = dot_nt(jnp.where(mine, value, bf16(0)), grad_out)
            weighted = probs * grad_probs
            grad_scores = (weighted - probs * total(weighted)).astype(bf16)
            grad_value = dot_nn(probs.astype(bf16), grad_out)
            grad_key = dot_nn(grad_scores, query)
            grad_query = dot_tn(grad_scores, key) * scale
            grads.append((grad_query, grad_key, grad_value))
        for k in range(3):
            grad = jnp.where(upper, grads[1][k], grads[0][k])
            if k != 1:
                sums_ref[k // 2, :, lanes] += fold(grad)
            where = pl.ds(pl.multiple_of(k * width + pair * LANES, LANES), LANES)
            grad_joint_ref[0, :, where] = grad.astype(bf16)

    @pl.when(image == pl.num_programs(0) - 1)
    def _():
        for k in range(2):
            vectors_ref[8 + k : 9 + k, :] = total(sums_ref[k])


def attend_backward(
    image_class, query, key, value, log_total, grad_mixed, sums_expand, sums_shrink, sums_mix
):
    images, cells, width = query.shape
    rows = per_image((cells, width))
    return pl.pallas_call(
        attend_backward_kernel,
        out_shape=(
            jax.ShapeDtypeStruct((images, cells, 3 * width), bf16),
            jax.ShapeDtypeStruct((16, width), f32),
        ),
        grid_spec=pltpu.PrefetchScalarGridSpec(
            num_scalar_prefetch=1,
            grid=(images,),
            in_specs=[
                rows,
                rows,
                rows,
                per_image((HEADS, 8, cells)),
                rows,
                whole(sums_expand.shape),
                whole(sums_shrink.shape),
                whole(sums_mix.shape),
            ],
            out_specs=[per_image((cells, 3 * width)), whole((16, width))],
            scratch_shapes=[pltpu.VMEM((2, 8, width), f32)],
        ),
        compiler_params=pltpu.CompilerParams(vmem_limit_bytes=62 * MIB),
        cost_estimate=cost(40 * images * cells * cells * width, 12 * MIB),
        name="attend_backward",
    )(image_class, query, key, value, log_total, grad_mixed, sums_expand, sums_shrink, sums_mix)


def joint_backward_kernel(
    core_ref,
    tokens_ref,
    normed_ref,
    mixed_ref,
    grad_resid_ref,
    grad_joint_ref,
    gain1_ref,
    joint_ref,
    grad_tokens_ref,
    mine_ref,
    other_ref,
    sums,
    resid_low,
    joint_total,
    mix_total,
):
    image = pl.program_id(0)
    last = pl.num_programs(0) - 1
    cells, width = tokens_ref.shape[1:]
    chunk = 96
    block = 256

    @pl.when(image == 0)
    def _():
        sums[...] = jnp.zeros_like(sums)
        joint_total[...] = jnp.zeros_like(joint_total)
        mix_total[...] = jnp.zeros_like(mix_total)

    @pl.loop(0, 3 * width // block)
    def _(step):
        here = rows_at(step, block)
        joint_total[:, here] += dot_tn(normed_ref[0], grad_joint_ref[0, :, here])

    @pl.loop(0, cells // chunk)
    def _(step):
        rows = rows_at(step, chunk)
        normal, row_scale = row_norm(tokens_ref[0, rows, :].astype(f32))
        grad = dot_nt(grad_joint_ref[0, rows, :], joint_ref[...])
        sums[0] += fold(grad * normal)
        sums[1] += fold(grad)
        back = row_norm_back(grad, normal, row_scale, line(gain1_ref))
        grad_resid = grad_resid_ref[0, rows, :]
        resid_low[rows, :] = grad_resid.astype(bf16)
        grad_tokens_ref[0, rows, :] = (grad_resid + back).astype(bf16)

    mix_total[...] += dot_tn(mixed_ref[0], resid_low[...])

    @pl.when(image == last)
    def _():
        core = core_ref[0]
        size = width // (2 * PAIRS)
        parts = size // 8
        for pair in range(PAIRS):
            for ref, side in ((mine_ref, core), (other_ref, 1 - core)):
                at = pl.ds(pl.multiple_of((2 * pair + side) * size, 8), size)
                for k in range(3):
                    ref[pair, k * parts : (k + 1) * parts] = sections_of(
                        joint_total[at, k * width : (k + 1) * width]
                    )
                ref[pair, 3 * parts : 4 * parts] = sections_of(mix_total[at, :])


def joint_backward(
    core, tokens, normed, mixed, grad_resid, grad_joint, gain1, joint
):
    images, cells, width = tokens.shape
    rows = per_image((cells, width))
    size = width // (2 * PAIRS)
    half = (PAIRS, 4 * size // 8, 8, width)
    return pl.pallas_call(
        joint_backward_kernel,
        out_shape=(
            jax.ShapeDtypeStruct((images, cells, width), bf16),
            jax.ShapeDtypeStruct(half, bf16),
            jax.ShapeDtypeStruct(half, bf16),
            jax.ShapeDtypeStruct((2, 8, width), f32),
        ),
        grid_spec=pltpu.PrefetchScalarGridSpec(
            num_scalar_prefetch=1,
            grid=(images,),
            in_specs=[
                rows,
                rows,
                rows,
                rows,
                per_image((cells, 3 * width)),
                whole((width,)),
                whole((width, 3 * width)),
            ],
            out_specs=[rows, whole(half), whole(half), whole((2, 8, width))],
            scratch_shapes=[
                pltpu.VMEM((cells, width), bf16),
                pltpu.VMEM((width, 3 * width), f32),
                pltpu.VMEM((width, width), f32),
            ],
        ),
        compiler_params=pltpu.CompilerParams(vmem_limit_bytes=62 * MIB),
        cost_estimate=cost(14 * images * cells * width * width, 25 * MIB),
        name="joint_backward",
    )(
        core,
        tokens,
        normed,
        mixed,
        grad_resid,
        grad_joint,
        gain1,
        joint,
    )


def norm_means(sums, gain, per_group, count):
    inverse = 1.0 / (count * per_group)
    return [group_total(total(item) * gain, per_group) * inverse for item in sums]


def embed_backward_kernel(
    class_ref,
    core_ref,
    grad_tokens_ref,
    x_ref,
    third_ref,
    stat3_ref,
    stem_ref,
    gain3_ref,
    bias3_ref,
    embed_ref,
    grad_inner_ref,
    grad_third_ref,
    mine_ref,
    other_ref,
    sums_embed_ref,
    sums3_ref,
    mask,
    embed_total,
    grad_position,
    position_total,
):
    image = pl.program_id(0)
    last = pl.num_programs(0) - 1
    cells, channels = x_ref.shape[1:]
    width = embed_ref.shape[1]
    chunk = 96
    steps = cells // chunk
    image_class = class_ref[image]
    mask[...] = validity_mask(image_class, cells)
    count = valid_count(image_class)

    @pl.when(image == 0)
    def _():
        for ref in (grad_position, sums_embed_ref, sums3_ref, embed_total):
            ref[...] = jnp.zeros_like(ref)

    @pl.loop(0, steps)
    def _(step):
        rows = rows_at(step, chunk)
        grad = grad_tokens_ref[0, rows, :].astype(f32) * spread_lanes(mask[rows, :], width)
        grad_position[rows, :] += grad
        sums_embed_ref[...] += fold(grad)

    embed_total[...] += dot_tn(stem_ref[0], grad_tokens_ref[0])
    centre, scale = stat3_ref[0, 0:1, :], stat3_ref[0, 1:2, :]
    gain = line(gain3_ref)

    def third_step(step, carry):
        rows = rows_at(step, chunk)
        keep = spread_lanes(mask[rows, :], channels)
        grad = dot_nt(grad_tokens_ref[0, rows, :], embed_ref[...]) * keep
        normal = (third_ref[0, rows, :] - centre) * scale
        argument = x_ref[0, rows, :] * keep + normal * gain + line(bias3_ref)
        cdf, pdf = cdf_pdf(argument)
        grad = grad * (cdf + argument * pdf)
        grad_inner_ref[0, rows, :] = grad
        return carry[0] + fold(grad * normal), carry[1] + fold(grad)

    zeros = jnp.zeros((8, channels), f32)
    with_normal, plain = lax.fori_loop(0, steps, third_step, (zeros, zeros))
    sums3_ref[0] += with_normal
    sums3_ref[1] += plain
    mean, cross = norm_means((plain, with_normal), gain, channels // GROUPS, count)
    outer = scale * gain
    mean = mean * scale
    cross = cross * scale

    @pl.loop(0, steps)
    def _(step):
        rows = rows_at(step, chunk)
        keep = spread_lanes(mask[rows, :], channels)
        normal = (third_ref[0, rows, :] - centre) * scale
        grad = (grad_inner_ref[0, rows, :] * outer - mean - normal * cross) * keep
        grad_third_ref[0, rows, :] = grad.astype(bf16)

    @pl.when(image == last)
    def _():
        core = core_ref[0]
        position_rows = cells // (2 * PAIRS)
        position_total[...] = jnp.zeros_like(position_total)
        for block in range(2 * PAIRS):
            position_total[block, 0:position_rows, :] = grad_position[
                block * position_rows : (block + 1) * position_rows, :
            ]
        size = channels // (2 * PAIRS)
        for pair in range(PAIRS):
            for ref, side in ((mine_ref, core), (other_ref, 1 - core)):
                block = 2 * pair + side
                at = pl.ds(pl.multiple_of(block * size, 8), size)
                ref[pair, 0 : size // 8] = sections_of(embed_total[at, :])
                ref[pair, size // 8 :] = sections_of(position_total[block])


def embed_backward(image_class, core, grad_tokens, x, third, stat3, stem, gain3, bias3, embed):
    images, cells, channels = x.shape
    width = embed.shape[1]
    position_rows = -(-cells // (2 * PAIRS) // 8) * 8
    half = (PAIRS, (channels // (2 * PAIRS) + position_rows) // 8, 8, width)
    return pl.pallas_call(
        embed_backward_kernel,
        out_shape=(
            jax.ShapeDtypeStruct((images, cells, channels), f32),
            jax.ShapeDtypeStruct((images, cells, channels), bf16),
            jax.ShapeDtypeStruct(half, bf16),
            jax.ShapeDtypeStruct(half, bf16),
            jax.ShapeDtypeStruct((8, width), f32),
            jax.ShapeDtypeStruct((2, 8, channels), f32),
        ),
        grid_spec=pltpu.PrefetchScalarGridSpec(
            num_scalar_prefetch=2,
            grid=(images,),
            in_specs=[
                per_image((cells, width)),
                per_image((cells, channels)),
                per_image((cells, channels)),
                per_image((8, channels)),
                per_image((cells, channels)),
                whole((channels,)),
                whole((channels,)),
                whole((channels, width)),
            ],
            out_specs=[
                per_image((cells, channels)),
                per_image((cells, channels)),
                whole(half),
                whole(half),
                whole((8, width)),
                whole((2, 8, channels)),
            ],
            scratch_shapes=[
                pltpu.VMEM((cells, LANES), f32),
                pltpu.VMEM((channels, width), f32),
                pltpu.VMEM((cells, width), f32),
                pltpu.VMEM((2 * PAIRS, position_rows, width), f32),
            ],
        ),
        compiler_params=pltpu.CompilerParams(vmem_limit_bytes=62 * MIB),
        cost_estimate=cost(20_000_000_000, 30 * MIB),
        name="embed_backward",
    )(image_class, core, grad_tokens, x, third, stat3, stem, gain3, bias3, embed)


def convs_backward_kernel(
    class_ref,
    core_ref,
    grad_third_ref,
    x_ref,
    first_ref,
    second_ref,
    stat1_ref,
    stat2_ref,
    std_in_ref,
    std_mid_ref,
    std_out_ref,
    w_in_ref,
    w_mid_ref,
    w_out_ref,
    gain1_ref,
    bias1_ref,
    gain2_ref,
    bias2_ref,
    sums_embed_ref,
    sums3_ref,
    sums_attn_ref,
    grad_first_ref,
    mine_ref,
    other_ref,
    vectors,
    sums1,
    sums2,
    mask,
    act,
    padded,
    columns,
    in_total,
    mid_total,
    out_total,
    mid_done,
    in_done,
):
    image = pl.program_id(0)
    last = pl.num_programs(0) - 1
    cells, channels = x_ref.shape[1:]
    width = sums_embed_ref.shape[1]
    middle = first_ref.shape[2]
    image_class = class_ref[image]
    mask[...] = validity_mask(image_class, cells)
    count = valid_count(image_class)

    @pl.when(image == 0)
    def _():
        for ref in (sums1, sums2, in_total, mid_total, out_total):
            ref[...] = jnp.zeros_like(ref)

    def middle_norm(values_ref, stat_ref, gain_ref, bias_ref, sums_ref, grad_of):
        centre, scale = stat_ref[0, 0:1, :], stat_ref[0, 1:2, :]
        gain = line(gain_ref)
        keep = spread_lanes(mask[...], middle)
        normal = (values_ref[0] - centre) * scale
        argument = normal * gain + line(bias_ref)
        cdf, pdf = cdf_pdf(argument)
        act[...] = (argument * cdf * keep).astype(bf16)
        grad = grad_of() * keep * (cdf + argument * pdf)
        plain, with_normal = fold(grad), fold(grad * normal)
        sums_ref[0] += with_normal
        sums_ref[1] += plain
        mean, cross = norm_means((plain, with_normal), gain, middle // GROUPS, count)
        return (grad * (scale * gain) - mean * scale - normal * (cross * scale)) * keep

    grad_second = middle_norm(
        second_ref,
        stat2_ref,
        gain2_ref,
        bias2_ref,
        sums2,
        lambda: dot_nt(grad_third_ref[0], std_out_ref[...]),
    )
    out_total[...] += dot_tn(act[...], grad_third_ref[0])
    fill_columns(grad_second, padded, columns, -1)

    def spread_back():
        grad = jnp.zeros((cells, middle), f32)
        for tap in range(9):
            part = slice(tap * middle, (tap + 1) * middle)
            grad = grad + dot_nt(columns[:, part], std_mid_ref[part, :])
        return grad

    grad = middle_norm(first_ref, stat1_ref, gain1_ref, bias1_ref, sums1, spread_back)
    grad_low = grad.astype(bf16)
    grad_first_ref[0] = grad_low
    mid_total[...] += dot_tn(act[...], columns[...])
    low = (x_ref[0] * spread_lanes(mask[...], channels)).astype(bf16)
    in_total[...] += dot_tn(grad_low, low)

    @pl.when(image == last)
    def _():
        core = core_ref[0]
        out_total[...] = standardize_back(w_out_ref[...].astype(f32), out_total[...])
        in_done[...] = standardize_back(w_in_ref[...].astype(f32), in_total[...].T)
        rows = 9 * middle
        normal, scale = standardized(w_mid_ref[...].astype(f32))
        grads = [mid_total[:, tap * middle : (tap + 1) * middle] for tap in range(9)]
        grad_mean = sum(total(g) for g in grads) * (1.0 / rows)
        inner = sum(
            total(g * normal[tap * middle : (tap + 1) * middle]) for tap, g in enumerate(grads)
        ) * (1.0 / rows)
        for tap, g in enumerate(grads):
            part = slice(tap * middle, (tap + 1) * middle)
            mid_done[part, :] = scale * (g - grad_mean - normal[part] * inner)
        in_size = channels // (2 * PAIRS)
        mid_size = rows // (2 * PAIRS)
        out_size = middle // (2 * PAIRS)
        in_parts = in_size // 8
        mid_parts = mid_size // 8
        for pair in range(PAIRS):
            for ref, side in ((mine_ref, core), (other_ref, 1 - core)):
                block = 2 * pair + side
                at = pl.ds(pl.multiple_of(block * in_size, 8), in_size)
                ref[pair, 0:in_parts] = sections_of(in_done[at, :])
                at = pl.ds(pl.multiple_of(block * mid_size, 8), mid_size)
                ref[pair, in_parts : in_parts + mid_parts] = sections_of(mid_done[at, :])
                at = pl.ds(pl.multiple_of(block * out_size, 8), out_size)
                for k in range(channels // middle):
                    ref[pair, in_parts + mid_parts + k] = out_total[
                        at, k * middle : (k + 1) * middle
                    ].astype(bf16)
        vectors[...] = jnp.zeros_like(vectors)
        row = 0
        for item in (
            total(sums_embed_ref[...]),
            total(sums_attn_ref[0]),
            total(sums_attn_ref[1]),
            total(sums1[0]),
            total(sums1[1]),
            total(sums2[0]),
            total(sums2[1]),
            total(sums3_ref[0]),
            total(sums3_ref[1]),
        ):
            for start in range(0, item.shape[1], middle):
                vectors[row : row + 1, :] = item[:, start : start + middle]
                row += 1
        mine_ref[PAIRS] = jnp.zeros(mine_ref.shape[1:], bf16)
        store_split(mine_ref.at[PAIRS], 0, vectors[...])
        other_ref[PAIRS] = mine_ref[PAIRS]


def convs_backward(
    image_class,
    core,
    grad_third,
    x,
    first,
    second,
    stat1,
    stat2,
    stds,
    weights,
    norms,
    sums_embed,
    sums3,
    sums_attn,
):
    images, cells, channels = x.shape
    middle = first.shape[2]
    width = sums_embed.shape[1]
    row = lambda size: whole((size,))
    conv_rows = channels // (2 * PAIRS) + 9 * middle // (2 * PAIRS) + middle // (2 * PAIRS) * (channels // middle)
    half = (PAIRS + 1, conv_rows // 8, 8, middle)
    return pl.pallas_call(
        convs_backward_kernel,
        out_shape=(
            jax.ShapeDtypeStruct((images, cells, middle), bf16),
            jax.ShapeDtypeStruct(half, bf16),
            jax.ShapeDtypeStruct(half, bf16),
        ),
        grid_spec=pltpu.PrefetchScalarGridSpec(
            num_scalar_prefetch=2,
            grid=(images,),
            in_specs=[
                per_image((cells, channels)),
                per_image((cells, channels)),
                per_image((cells, middle)),
                per_image((cells, middle)),
                per_image((8, middle)),
                per_image((8, middle)),
                whole((channels, middle)),
                whole((9 * middle, middle)),
                whole((middle, channels)),
                whole((channels, middle)),
                whole((9 * middle, middle)),
                whole((middle, channels)),
                row(middle),
                row(middle),
                row(middle),
                row(middle),
                whole((8, width)),
                whole((2, 8, channels)),
                whole((2, 8, width)),
            ],
            out_specs=[
                per_image((cells, middle)),
                whole(half),
                whole(half),
            ],
            scratch_shapes=[
                pltpu.VMEM((VECTORS * 8, middle), f32),
                pltpu.VMEM((2, 8, middle), f32),
                pltpu.VMEM((2, 8, middle), f32),
                pltpu.VMEM((cells, LANES), f32),
                pltpu.VMEM((cells, middle), bf16),
                pltpu.VMEM((3, cells + 2 * SIDE, middle), f32),
                pltpu.VMEM((cells, 9 * middle), bf16),
                pltpu.VMEM((middle, channels), f32),
                pltpu.VMEM((middle, 9 * middle), f32),
                pltpu.VMEM((middle, channels), f32),
                pltpu.VMEM((9 * middle, middle), f32),
                pltpu.VMEM((channels, middle), f32),
            ],
        ),
        compiler_params=pltpu.CompilerParams(vmem_limit_bytes=62 * MIB),
        cost_estimate=cost(20_000_000_000, 20 * MIB),
        name="convs_backward",
    )(
        image_class,
        core,
        grad_third,
        x,
        first,
        second,
        stat1,
        stat2,
        *stds,
        *weights,
        *norms[:4],
        sums_embed,
        sums3,
        sums_attn,
    )


def input_backward_kernel(class_ref, grad_inner_ref, grad_first_ref, std_in_ref, input_grad_ref):
    cells, channels = grad_inner_ref.shape[1:]
    keep = spread_lanes(validity_mask(class_ref[pl.program_id(0)], cells), channels)
    back = dot_nt(grad_first_ref[0], std_in_ref[...])
    input_grad_ref[0] = (grad_inner_ref[0] + back) * keep


def input_backward(image_class, grad_inner, grad_first, std_in):
    images, cells, channels = grad_inner.shape
    middle = grad_first.shape[2]
    return pl.pallas_call(
        input_backward_kernel,
        out_shape=jax.ShapeDtypeStruct((images, cells, channels), f32),
        grid_spec=pltpu.PrefetchScalarGridSpec(
            num_scalar_prefetch=1,
            grid=(images,),
            in_specs=[
                per_image((cells, channels)),
                per_image((cells, middle)),
                whole((channels, middle)),
            ],
            out_specs=per_image((cells, channels)),
        ),
        compiler_params=pltpu.CompilerParams(vmem_limit_bytes=62 * MIB),
        cost_estimate=cost(2 * images * cells * channels * middle, 12 * MIB),
        name="input_backward",
    )(image_class, grad_inner, grad_first, std_in)


def combine_core_kernel(plane_ref, *refs, arrays, extra):
    mines, others, outs = refs[:arrays], refs[arrays : 2 * arrays], refs[2 * arrays :]
    start = 0
    for mine, other in zip(mines, others):
        size = mine.shape[1]
        for z in range(mine.shape[0] // 4):
            for q in range(4):
                at = 4 * z + lax.bitwise_xor(plane_ref[0], q)
                summed = mine[at].astype(f32) + other[at].astype(f32)
                outs[q][z, start : start + size] = summed.astype(bf16)
        start += size
    if extra:
        vectors = load_split(mines[0].at[PAIRS], 0) + load_split(others[0].at[PAIRS], 0)
        for out in outs:
            out[PAIRS // 4] = jnp.zeros(out.shape[1:], bf16)
            store_split(out.at[PAIRS // 4], 0, vectors)


def combine_core(plane, mines, others, extra):
    arrays = len(mines)
    depth = PAIRS // 4
    steps = 1 if extra else depth
    out_shape = (sum(item.shape[1] for item in mines),) + mines[0].shape[2:]
    in_spec = lambda item: pl.BlockSpec(
        (item.shape[0] // steps,) + item.shape[1:], lambda step, *_: (step, 0, 0, 0)
    )
    out_spec = pl.BlockSpec(((depth + extra) // steps,) + out_shape, lambda step, *_: (step, 0, 0, 0))
    size = sum(item.size for item in mines)
    return pl.pallas_call(
        lambda *refs: combine_core_kernel(*refs, arrays=arrays, extra=extra),
        out_shape=[jax.ShapeDtypeStruct((depth + extra,) + out_shape, bf16)] * 4,
        grid_spec=pltpu.PrefetchScalarGridSpec(
            num_scalar_prefetch=1,
            grid=(steps,),
            in_specs=[in_spec(item) for item in mines] * 2,
            out_specs=[out_spec] * 4,
        ),
        compiler_params=pltpu.CompilerParams(vmem_limit_bytes=62 * MIB),
        cost_estimate=cost(size, 6 * size),
        name="combine_core",
    )(plane, *mines, *others)


def four(values):
    return (values[0] + values[1]) + (values[2] + values[3])


def combine_plane_kernel(depth_ref, *refs, extra):
    parts, outs = refs[:4], refs[4:]
    size = parts[0].shape[1]
    for q in range(4):
        at = lax.bitwise_xor(depth_ref[0], q)
        outs[q][0:size] = four([part[at].astype(f32) for part in parts]).astype(bf16)
    if extra:
        vectors = four([load_split(part.at[PAIRS // 4], 0) for part in parts])
        for out in outs:
            store_split(out, size, vectors)


def combine_plane(depth, parts, extra):
    shape = (parts[0].shape[1] + 2 * VECTORS * extra,) + parts[0].shape[2:]
    size = 4 * parts[0].size
    return pl.pallas_call(
        lambda *refs: combine_plane_kernel(*refs, extra=extra),
        out_shape=[jax.ShapeDtypeStruct(shape, bf16)] * 4,
        grid_spec=pltpu.PrefetchScalarGridSpec(
            num_scalar_prefetch=1,
            grid=(1,),
            in_specs=[whole(item.shape) for item in parts],
            out_specs=[whole(shape)] * 4,
        ),
        compiler_params=pltpu.CompilerParams(vmem_limit_bytes=62 * MIB),
        cost_estimate=cost(size, 3 * size),
        name="combine_plane",
    )(depth, *parts)


def store_lines(outs, vectors, lines):
    for out, pieces in zip(outs, lines):
        out[...] = jnp.concatenate(
            [vectors[row : row + 1, 0:size] for row, size in pieces], axis=1
        ).reshape(-1)


def line_shapes(lines):
    return [jax.ShapeDtypeStruct((sum(size for _, size in pieces),), f32) for pieces in lines]


def combine_depth_kernel(*refs, places, lines):
    parts, outs = refs[:4], refs[4:]
    count = len(places)
    summed = four([part[0:count].astype(f32) for part in parts])
    for section, (out, row, column, columns, rows) in enumerate(places):
        stride = columns // LANES
        for lane in range(summed.shape[2] // LANES):
            start = row * stride + column // LANES + lane
            outs[out][pl.ds(start, rows, stride=stride), :] = summed[
                section, 0:rows, lane * LANES : (lane + 1) * LANES
            ]
    if lines:
        vectors = four([load_split(part, count) for part in parts])
        store_lines(outs[len(outs) - len(lines) :], vectors, lines)


def combine_depth(parts, places, sizes, lines):
    shapes = [jax.ShapeDtypeStruct((size // LANES, LANES), f32) for size in sizes] + line_shapes(lines)
    size = 4 * parts[0].size
    outs = pl.pallas_call(
        lambda *refs: combine_depth_kernel(*refs, places=places, lines=lines),
        out_shape=shapes,
        grid=(1,),
        in_specs=[whole(item.shape) for item in parts],
        out_specs=[whole(item.shape) for item in shapes],
        compiler_params=pltpu.CompilerParams(vmem_limit_bytes=62 * MIB),
        cost_estimate=cost(size, 3 * size),
        name="combine_depth",
    )(*parts)
    return [item.reshape(-1) for item in outs[: len(sizes)]], list(outs[len(sizes) :])


def sum_vectors_kernel(gathered_ref, *outs, lines):
    store_lines(outs, jnp.sum(gathered_ref[...], axis=0), lines)


def sum_vectors(gathered, lines):
    shapes = line_shapes(lines)
    return pl.pallas_call(
        lambda *refs: sum_vectors_kernel(*refs, lines=lines),
        out_shape=shapes,
        grid=(1,),
        in_specs=[whole(gathered.shape)],
        out_specs=[whole(item.shape) for item in shapes],
        compiler_params=pltpu.CompilerParams(vmem_limit_bytes=62 * MIB),
        name="sum_vectors",
    )(gathered)


def permuted(item, distance, devices):
    return lax.ppermute(item, BOTH, [(k, k ^ distance) for k in range(devices)])


class Sums:
    def __init__(self, index, devices):
        self.devices = devices
        self.plane = ((index // 2) % 4).astype(jnp.int32).reshape(1)
        self.depth = (index // 8).astype(jnp.int32).reshape(1)

    def spread(self, parts, unit):
        return [parts[0]] + [permuted(parts[q], q * unit, self.devices) for q in (1, 2, 3)]

    def start_core(self, mines, others):
        return mines, [permuted(item, 1, self.devices) for item in others]

    def end_core(self, started, extra=0):
        return combine_core(self.plane, *started, extra)

    def start_plane(self, parts):
        return self.spread(parts, 2)

    def end_plane(self, started, extra=0):
        return combine_plane(self.depth, started, extra)

    def start_depth(self, parts):
        return self.spread(parts, 8)


def after(value, *others):
    return lax.optimization_barrier((value,) + others)[0]


def ahead(value, others):
    leaves, tree = jax.tree.flatten(others)
    held = lax.optimization_barrier((value, *leaves))
    return jax.tree.unflatten(tree, held[1:])


def octets(out, rows, columns, width, offset=0):
    return [
        (out, 8 * part, start, columns, min(8, rows - 8 * part))
        for start in range(0, columns, width)
        for part in range(-(-rows // 8))
    ]


def scattered(mine, other, places, sizes, devices):
    blocks = jnp.stack([mine, other], axis=1).reshape((2 * PAIRS,) + mine.shape[1:])
    results = []
    for out, size in sizes:
        chosen = [k for k, place in enumerate(places) if place[0] == out]
        columns = places[chosen[0]][3]
        width = mine.shape[-1]
        rows = size // columns
        groups = columns // width
        values = blocks[:, chosen[0] : chosen[-1] + 1]
        values = values.reshape(2 * PAIRS, groups, -1, width)[:, :, :rows]
        values = jnp.moveaxis(values, 1, 2).reshape(devices, -1)
        length = values.shape[1]
        padded = -(-length // LANES) * LANES
        values = jnp.pad(values, ((0, 0), (0, padded - length))).reshape(devices, -1, LANES)
        own = lax.psum_scatter(values, BOTH, scatter_dimension=0, tiled=True)
        results.append(own.astype(f32).reshape(-1)[:length])
    return results


def shards(
    stem_input,
    image_class,
    owner,
    conv_in_weight,
    first_gain,
    first_bias,
    conv_mid_weight,
    second_gain,
    second_bias,
    conv_out_weight,
    third_gain,
    third_bias,
    embed_weight,
    embed_bias,
    position_table,
    attn_gain,
    attn_bias,
    joint_weight,
    query_bias,
    value_bias,
    mix_weight,
    mix_bias,
    mlp_gain,
    mlp_bias,
    expand_weight,
    expand_bias,
    shrink_weight,
    shrink_bias,
    cotangent,
):
    sections = lax.axis_size("section")
    devices = sections * lax.axis_size("batch")
    staged = (devices, sections) == (2 * PAIRS, 4)
    index = lax.axis_index(BOTH)
    images, cells, channels = stem_input.shape
    middle = conv_in_weight.shape[1]
    width = embed_weight.shape[1]
    inner = expand_weight.shape[1]
    section_index = lax.axis_index("section")
    mine = lax.dynamic_index_in_dim(owner.reshape(sections, images), section_index, 0, keepdims=False)
    core = ((index % 2) if staged else jnp.zeros((), jnp.int32)).astype(jnp.int32).reshape(1)
    received = lax.all_to_all(cotangent[0], "section", split_axis=0, concat_axis=0, tiled=True)
    norms = (first_gain, first_bias, second_gain, second_bias, third_gain, third_bias)
    weights = (conv_in_weight, conv_mid_weight.reshape(-1, middle), conv_out_weight)
    std_in, std_mid, std_out, first, second, third, stat1, stat2, stat3, stem, tokens = stem_forward(
        image_class, stem_input, *weights, norms, embed_weight, embed_bias, position_table
    )
    normed, query, key, value, log_total, mixed, resid, normed_two = attend_forward(
        image_class,
        tokens,
        attn_gain,
        attn_bias,
        joint_weight,
        query_bias,
        value_bias,
        mix_weight,
        mix_bias,
        mlp_gain,
        mlp_bias,
    )
    (
        outgoing,
        grad_normed_two,
        shrink_mine,
        shrink_other,
        expand_mine,
        expand_other,
        sums_expand,
        sums_shrink,
    ) = feed(
        image_class,
        mine,
        core,
        normed_two,
        resid,
        received,
        expand_weight,
        expand_bias,
        shrink_weight,
        shrink_bias,
    )
    sums = Sums(index, devices)
    if staged:
        feed_core = sums.start_core([shrink_mine, expand_mine], [shrink_other, expand_other])
    arrived = lax.all_to_all(outgoing, "section", split_axis=0, concat_axis=0, tiled=True)
    grad_resid, grad_mixed, sums_mix = mix_backward(
        image_class, mine, resid, received, grad_normed_two, mix_weight, mlp_gain
    )
    if staged:
        feed_core = ahead(grad_resid, feed_core)
        feed_plane = sums.start_plane(sums.end_core(feed_core))
        grad_mixed = after(grad_mixed, feed_plane[0])
    grad_joint, vectors_block = attend_backward(
        image_class, query, key, value, log_total, grad_mixed, sums_expand, sums_shrink, sums_mix
    )
    gathered = lax.all_gather(vectors_block, BOTH)
    grad_tokens, joint_mine, joint_other, sums_attn = joint_backward(
        core, tokens, normed, mixed, grad_resid, grad_joint, attn_gain, joint_weight
    )
    if staged:
        joint_core = sums.start_core([joint_mine], [joint_other])
        feed_plane, arrived = ahead(grad_tokens, (feed_plane, arrived))
        feed_depth = sums.start_depth(sums.end_plane(feed_plane))
        grad_tokens = after(grad_tokens, feed_depth[0], arrived)
    block_output = arrived[None]
    grad_inner, grad_third, embed_mine, embed_other, sums_embed, sums3 = embed_backward(
        image_class,
        core,
        grad_tokens,
        stem_input,
        third,
        stat3,
        stem,
        third_gain,
        third_bias,
        embed_weight,
    )
    if staged:
        embed_core = sums.start_core([embed_mine], [embed_other])
        joint_core, feed_depth = ahead(grad_third, (joint_core, feed_depth))
        joint_plane = sums.start_plane(sums.end_core(joint_core))
        grad_third = after(grad_third, joint_plane[0], *feed_depth)
    grad_first, conv_mine, conv_other = convs_backward(
        image_class,
        core,
        grad_third,
        stem_input,
        first,
        second,
        stat1,
        stat2,
        (std_in, std_mid, std_out),
        weights,
        norms,
        sums_embed,
        sums3,
        sums_attn,
    )
    if staged:
        embed_core, joint_plane = ahead(grad_first, (embed_core, joint_plane))
        conv_other = after(conv_other, *joint_plane)
        conv_core = sums.start_core([conv_mine], [conv_other])
        embed_plane = sums.start_plane(sums.end_core(embed_core))
        joint_depth = sums.start_depth(sums.end_plane(joint_plane))
        grad_first = after(grad_first, embed_plane[0], joint_depth[0])
    input_grad = input_backward(image_class, grad_inner, grad_first, std_in)

    parts = 2 * PAIRS
    shrink_places = octets(0, inner // parts, width, width)
    expand_places = octets(1, width // parts, inner, width)
    feed_sizes = [inner // parts * width] * 2
    joint_places = octets(0, width // parts, 3 * width, width) + octets(1, width // parts, width, width)
    joint_sizes = [3 * width * width // parts, width * width // parts]
    embed_places = octets(0, channels // parts, width, width) + octets(1, cells // parts, width, width)
    embed_sizes = [channels * width // parts, cells * width // parts]
    conv_places = (
        octets(0, channels // parts, middle, middle)
        + octets(1, 9 * middle // parts, middle, middle)
        + octets(2, middle // parts, channels, middle)
    )
    conv_sizes = [
        channels * middle // parts,
        9 * middle * middle // parts,
        middle * channels // parts,
    ]
    block_lines = [[(row, width) for row in range(inner // width)]] + [
        [(row, width)] for row in range(inner // width, inner // width + 6)
    ]
    stem_lines = []
    row = 0
    for size in [width] * 3 + [middle] * 4 + [channels] * 2:
        stem_lines.append([(row + k, middle) for k in range(size // middle)])
        row += size // middle
    block_vectors = sum_vectors(gathered.reshape((-1,) + vectors_block.shape), block_lines)
    if staged:
        conv_plane = sums.start_plane(sums.end_core(conv_core, 1))
        embed_depth = sums.start_depth(sums.end_plane(embed_plane))
        conv_depth = sums.start_depth(sums.end_plane(conv_plane, 1))
        (grad_shrink, grad_expand), _ = combine_depth(
            feed_depth, shrink_places + expand_places, feed_sizes, []
        )
        (grad_joint, grad_mix), _ = combine_depth(joint_depth, joint_places, joint_sizes, [])
        (grad_embed, grad_position), _ = combine_depth(embed_depth, embed_places, embed_sizes, [])
        (grad_in, grad_mid, grad_out), stem_vectors = combine_depth(
            conv_depth, conv_places, conv_sizes, stem_lines
        )
    else:
        (grad_shrink,) = scattered(
            shrink_mine, shrink_other, shrink_places, [(0, feed_sizes[0])], devices
        )
        (grad_expand,) = scattered(
            expand_mine, expand_other, expand_places, [(1, feed_sizes[1])], devices
        )
        grad_joint, grad_mix = scattered(
            joint_mine, joint_other, joint_places, list(enumerate(joint_sizes)), devices
        )
        grad_embed, grad_position = scattered(
            embed_mine, embed_other, embed_places, list(enumerate(embed_sizes)), devices
        )
        rows = conv_mine[PAIRS, :VECTORS].astype(f32) + conv_mine[PAIRS, VECTORS : 2 * VECTORS].astype(f32)
        rows = lax.psum(rows.reshape(-1, middle), BOTH)
        stem_vectors = [rows[pieces[0][0] : pieces[-1][0] + 1].reshape(-1) for pieces in stem_lines]
        conv_mine, conv_other = conv_mine[:PAIRS], conv_other[:PAIRS]
        grad_in, grad_mid, grad_out = scattered(
            conv_mine, conv_other, conv_places, list(enumerate(conv_sizes)), devices
        )
    (
        grad_expand_bias,
        grad_shrink_bias,
        grad_mlp_gain,
        grad_mlp_bias,
        grad_mix_bias,
        grad_query_bias,
        grad_value_bias,
    ) = block_vectors
    (
        grad_embed_bias,
        grad_attn_gain,
        grad_attn_bias,
        grad_first_gain,
        grad_first_bias,
        grad_second_gain,
        grad_second_bias,
        grad_third_gain,
        grad_third_bias,
    ) = stem_vectors
    return (
        block_output,
        input_grad,
        grad_in,
        grad_first_gain,
        grad_first_bias,
        grad_mid,
        grad_second_gain,
        grad_second_bias,
        grad_out,
        grad_third_gain,
        grad_third_bias,
        grad_embed,
        grad_embed_bias,
        grad_position,
        grad_attn_gain,
        grad_attn_bias,
        grad_joint,
        grad_query_bias,
        grad_value_bias,
        grad_mix,
        grad_mix_bias,
        grad_mlp_gain,
        grad_mlp_bias,
        grad_expand,
        grad_expand_bias,
        grad_shrink,
        grad_shrink_bias,
    )


def solution(mesh):
    split = P(BOTH)
    images = P(BOTH, None, None)
    slots = P(BOTH, None, None, None)
    full = P()
    in_specs = (images, split, P("batch")) + (full,) * 25 + (slots,)
    out_specs = (
        slots,
        images,
        split,
        full,
        full,
        split,
        full,
        full,
        split,
        full,
        full,
        split,
        full,
        split,
        full,
        full,
        split,
        full,
        full,
        split,
        full,
        full,
        full,
        split,
        full,
        split,
        full,
    )
    return jax.shard_map(shards, mesh=mesh, in_specs=in_specs, out_specs=out_specs, check_vma=False)
```

time: 1330 us -> 411 us (0.31)
  waiting for transfers between devices: 935 us -> 19.2 us
  Pallas kernels: 254 us -> 313 us
  local copies, waits for them, and re-layouts: 57.2 us -> 8.45 us
  blocking collectives: 42.5 us -> 0 us
  starting transfers between devices: 8.45 us -> 47.9 us
  other arithmetic: 13.4 us -> 0 us
    reduce_scatter x9 -> x0, waiting for transfers between devices: 935 us -> none  [scatter(): own = lax.psum_scatter(parts, BOTH, scatter_dimension=0, tiled=True)]
    pallas_call x1 -> x18, Pallas kernels: 43.1 us -> 138 us  [the longest x1 36.3 us: joint_backward(): pl.pallas_call(joint_backward_kernel, out_shape=(jax.ShapeDtypeStruct((im...]
    pallas_call x1, Pallas kernels: 77.6 us -> 33.2 us  [attend_backward(): pl.pallas_call(attend_backward_kernel, out_shape=(jax.ShapeDtypeStruct((i...]
    psum x1 -> x0, blocking collectives: 42.5 us -> none  [shards(): lax.psum(jnp.concatenate([jnp.sum(vector, axis=0) for vector in vectors])...]
    ppermute x0 -> x29, starting transfers between devices: none -> 38.3 us  [permuted(): return lax.ppermute(item, BOTH, [(k, k ^ distance) for k in range(devices)])]
    another operation x9 -> x0, local copies, waits for them, and re-layouts: 37.9 us -> none  [scatter(): parts = parts.reshape(devices, -1, LANES)]
    ppermute x0 -> x29, waiting for transfers between devices: none -> 19.1 us  [permuted(): return lax.ppermute(item, BOTH, [(k, k ^ distance) for k in range(devices)])]
  transfers between devices with their start and end apart: 11 -> 32, of which waited for: 9 -> 6; matrix products, arithmetic and copies ran while one was open for 5% -> 0% of each run, Pallas kernels for 6% -> 62%
where the time goes in v2:
time: 411 us; the launch traced here: 404 us
  Pallas kernels  313 us (76%)
  starting transfers between devices  47.9 us (12%)
  waiting for transfers between devices  19.2 us (5%)
  between operations  14.9 us (4%)
  local copies, waits for them, and re-layouts  8.45 us (2%)
    pallas_call x1, Pallas kernels, feed(): pl.pallas_call(feed_kernel, out_shape=(jax.ShapeDtypeStruct((slots, cells...  63.2 us
    pallas_call x1, Pallas kernels, attend_forward(): pl.pallas_call(attend_forward_kernel, out_shape=(low, low, low, low, jax....  43.4 us
    ppermute x29, starting transfers between devices, permuted(): return lax.ppermute(item, BOTH, [(k, k ^ distance) for k in range(devices)])  38.3 us
    pallas_call x1, Pallas kernels, joint_backward(): pl.pallas_call(joint_backward_kernel, out_shape=(jax.ShapeDtypeStruct((im...  36.3 us
    pallas_call x1, Pallas kernels, stem_forward(): pl.pallas_call(stem_forward_kernel, out_shape=(jax.ShapeDtypeStruct((chan...  35.4 us
    pallas_call x1, Pallas kernels, attend_backward(): pl.pallas_call(attend_backward_kernel, out_shape=(jax.ShapeDtypeStruct((i...  33.2 us
    pallas_call x1, Pallas kernels, embed_backward(): pl.pallas_call(embed_backward_kernel, out_shape=(jax.ShapeDtypeStruct((im...  24 us
    pallas_call x1, Pallas kernels, convs_backward(): pl.pallas_call(convs_backward_kernel, out_shape=(jax.ShapeDtypeStruct((im...  20.2 us
  transfers between devices with their start and end apart: 32, of which 6 were waited for; matrix products, arithmetic and copies ran while one was open for 0% of the time, Pallas kernels for 62%

profile of v2, /device:TPU:0, one launch (start us, length us, event | category | flops | bytes accessed | tf_op | source)
XLA Modules:
  0.0 403.7 jit_solution(12663396807315732968)
XLA Ops:
  7.2 4.8 %all-to-all-start = ((bf16[4,576,768]{2,1,0:T(8,128)(2,1)}), bf16[4,576,768]{2,1,0:T(8,128)(2,1)}, u32[]{:S(2)}, u32[]{:S(2)}) async-start(bf16[4,576,768]{2,1,0:T(8,128)(2,1)} %bitcast.18), calls=%async_computation | async-start | bytes 7077888 | tf_op jit(solution)/shard_map/all_to_all | solution.py:1602
  12.0 0.1 reshape.98
  12.1 0.5 dynamic-slice_bitcast_fusion.mine_ref
  12.6 35.4 %stem_forward.1 = (bf16[1024,256]{1,0:T(8,128)(2,1)}, bf16[2304,256]{1,0:T(8,128)(2,1)}, bf16[256,1024]{1,0:T(8,128)(2,1)}, f32[2,576,256]{2,1,0:T(8,128)}, f32[...) custom-call(s32[2]{0:T(128)} %class_ref.15, ...), custom_call_target="tpu_custom_call" | custom-call | flops 24999999488 | bytes 31457280 | tf_op jit(solution)/shard_map/stem_forward/pallas_call | solution.py:294
  48.0 43.4 %attend_forward.1 = (bf16[2,576,768]{2,1,0:T(8,128)(2,1)}, bf16[2,576,768]{2,1,0:T(8,128)(2,1)}, bf16[2,576,768]{2,1,0:T(8,128)(2,1)}, bf16[2,576,768]{2,1,0:T(8...) custom-call(s32[2]{0:T(128)} %class_ref.15, ...), custom_call_target="tpu_custom_call" | custom-call | flops 35000000512 | bytes 31457280 | tf_op jit(solution)/shard_map/attend_forward/pallas_call | solution.py:455
  91.3 63.2 %feed.1 = (bf16[4,576,768]{2,1,0:T(8,128)(2,1)}, f32[2,576,768]{2,1,0:T(8,128)}, bf16[16,12,8,768]{3,2,1,0:T(8,128)(2,1)}, bf16[16,12,8,768]{3,2,1,0:T(8,128)(2,...) custom-call(s32[2]{0:T(128)} %class_ref.15, ...), custom_call_target="tpu_custom_call" | custom-call | flops 32614907904 | bytes 41943040 | tf_op jit(solution)/shard_map/feed/pallas_call | solution.py:605
  154.5 0.6 collective-permute-start
  155.1 0.1 collective-permute-start.1
  155.2 4.7 %all-to-all-start.1 = ((bf16[4,576,768]{2,1,0:T(8,128)(2,1)}), bf16[4,576,768]{2,1,0:T(8,128)(2,1)}, u32[]{:S(2)}, u32[]{:S(2)}) async-start(bf16[4,576,768]{2,1,0:T(8,128)(2,1)} %get-tuple-element.185), calls=%async_computation.1 | async-start | bytes 7077888 | tf_op jit(solution)/shard_map/all_to_all | solution.py:1645
  160.0 14.9 %mix_backward.1 = (f32[2,576,768]{2,1,0:T(8,128)}, bf16[2,576,768]{2,1,0:T(8,128)(2,1)}, f32[3,8,768]{2,1,0:T(8,128)}) custom-call(s32[2]{0:T(128)} %class_ref.15, s32[2]{0:T(128)} %dynamic-slice_bitcast_fusion.mine_ref, f32[2,576,768]{2,1,0:T(8,128)} %get-tuple-element.158.resid_ref, bf16[4,576,768]{2,1,0:T(8,128)(2,1)} %all-to-all-done.cotangent_ref, ...), custom_call_target="tpu_custom_call" | custom-call | flops 1358954496 | bytes 20971520 | tf_op jit(solution)/shard_map/mix_backward/pallas_call | solution.py:704
  174.9 6.2 %combine_core.4 = (bf16[4,24,8,768]{3,2,1,0:T(8,128)(2,1)}, bf16[4,24,8,768]{3,2,1,0:T(8,128)(2,1)}, bf16[4,24,8,768]{3,2,1,0:T(8,128)(2,1)}, bf16[4,24,8,768]{3,2,1,0:T(8,128)(2,1)}) custom-call(s32[1]{0:T(128)} %bitcast.4.refs_0_, bf16[16,12,8,768]{3,2,1,0:T(8,128)(2,1)} %get-tuple-element.171.refs_1_, ...), custom_call_target="tpu_custom_call" | custom-call | flops 2359296 | bytes 14155776 | tf_op jit(solution)/shard_map/combine_core/pallas_call | solution.py:1384
  181.1 2.9 collective-permute-start.2
  184.0 2.0 collective-permute-start.3
  186.0 33.2 %attend_backward.1 = (bf16[2,576,2304]{2,1,0:T(8,128)(2,1)}, f32[16,768]{1,0:T(8,128)}) custom-call(s32[2]{0:T(128)} %class_ref.15, bf16[2,576,768]{2,1,0:T(8,128)(2,1)} %get-tuple-element.162.query_ref, bf16[2,576,768]{2,1,0:T(8,128)(2,1)} %get-tuple-element.163.key_ref, bf16[2,576,768]{2,1,0:T(8,128)(2,1)} %get-tuple-element.164.value_ref, ...), custom_call_target="tpu_custom_call" | custom-call | flops 20384317440 | bytes 12582912 | tf_op jit(solution)/shard_map/attend_backward/pallas_call | solution.py:800
  219.2 36.3 %joint_backward.1 = (bf16[2,576,768]{2,1,0:T(8,128)(2,1)}, bf16[16,12,8,768]{3,2,1,0:T(8,128)(2,1)}, bf16[16,12,8,768]{3,2,1,0:T(8,128)(2,1)}, f32[2,8,768]{2,1,0:T(8,128)}) custom-call(s32[1]{0:T(128)} %bitcast.core_ref, bf16[2,576,768]{2,1,0:T(8,128)(2,1)} %get-tuple-element.155.tokens_ref, bf16[2,576,768]{2,1,0:T(8,128)(2,1)} %get-tuple-element.156.normed_ref, ...), custom_call_target="tpu_custom_call" | custom-call | flops 9512681472 | bytes 26214400 | tf_op jit(solution)/shard_map/joint_backward/pallas_call | solution.py:898
  255.5 0.1 collective-permute-start.5
  255.7 1.0 copy-done.1
  256.7 3.9 combine_plane.4
  260.5 1.6 collective-permute-start.6
  262.2 2.6 collective-permute-start.7
  264.7 0.2 collective-permute-start.8
  264.9 24.0 %embed_backward.1 = (f32[2,576,1024]{2,1,0:T(8,128)}, bf16[2,576,1024]{2,1,0:T(8,128)(2,1)}, bf16[16,7,8,768]{3,2,1,0:T(8,128)(2,1)}, bf16[16,7,8,768]{3,2,1,0:T...) custom-call(s32[2]{0:T(128)} %class_ref.15, s32[1]{0:T(128)} %bitcast.core_ref, ...), custom_call_target="tpu_custom_call" | custom-call | flops 20000000000 | bytes 31457280 | tf_op jit(solution)/shard_map/embed_backward/pallas_call | solution.py:1044
  288.9 0.1 collective-permute-start.9
  289.0 4.5 %combine_core.5 = (bf16[4,12,8,768]{3,2,1,0:T(8,128)(2,1)}, bf16[4,12,8,768]{3,2,1,0:T(8,128)(2,1)}, bf16[4,12,8,768]{3,2,1,0:T(8,128)(2,1)}, bf16[4,12,8,768]{3,2,1,0:T(8,128)(2,1)}) custom-call(s32[1]{0:T(128)} %bitcast.4.refs_0_, bf16[16,12,8,768]{3,2,1,0:T(8,128)(2,1)} %get-tuple-element.203.refs_1_, bf16[16,12,8,768]{3,2,1,0:T(8,128)(2,1)} %collective-permute-done.5.refs_2_), custom_call_target="tpu_custom_call" | custom-call | flops 1179648 | bytes 7077888 | tf_op jit(solution)/shard_map/combine_core/pallas_call | solution.py:1384
  293.5 1.8 collective-permute-start.10
  295.4 1.7 collective-permute-start.11
  297.1 20.2 %convs_backward.1 = (bf16[2,576,256]{2,1,0:T(8,128)(2,1)}, bf16[17,17,8,256]{3,2,1,0:T(8,128)(2,1)}, bf16[17,17,8,256]{3,2,1,0:T(8,128)(2,1)}) custom-call(s32[2]{0:T(128)} %class_ref.15, s32[1]{0:T(128)} %bitcast.core_ref, bf16[2,576,1024]{2,1,0:T(8,128)(2,1)} %get-tuple-element.210.grad_third_ref, f32[2,576,1024]{2,1,0:T(8,128)} %x_ref.5, ...), custom_call_target="tpu_custom_call" | custom-call | flops 20000000000 | bytes 20971520 | tf_op jit(solution)/shard_map/convs_backward/pallas_call | solution.py:1255
  317.4 10.0 %collective-permute-done.12.refs_4_ = bf16[4,12,8,768]{3,2,1,0:T(8,128)(2,1)} collective-permute-done((bf16[4,12,8,768]{3,2,1,0:T(8,128)(2,1)}, bf16[4,12,8,768]{3,2,1,0:T(8,128)(2,1)}, u32[]{:S(2)}, u32[]{:S(2)}) %collective-permute-start.12) | collective-permute-done | bytes 589856 | tf_op jit(solution)/shard_map/ppermute | solution.py:1494
  327.4 3.8 combine_core.6
  331.2 0.7 collective-permute-start.20
  331.9 1.7 collective-permute-start.21
  333.6 1.1 collective-permute-start.22
  334.7 2.9 combine_core.7
  337.6 0.7 collective-permute-start.14
  338.2 1.7 collective-permute-start.15
  340.0 2.3 collective-permute-done.20.refs_2_
  342.3 0.7 copy-done.6
  343.0 1.8 collective-permute-start.16
  344.8 2.6 combine_plane.5
  347.5 2.7 collective-permute-start.26
  350.1 1.2 collective-permute-done.22.refs_4_
  351.3 2.9 collective-permute-start.27
  354.2 2.5 collective-permute-done.14.refs_2_
  356.7 3.3 collective-permute-start.28
  360.0 2.1 combine_plane.7
  362.2 0.2 collective-permute-start.23
  362.4 3.0 collective-permute-done.16.refs_4_
  365.4 0.7 copy-done.5
  366.2 2.1 combine_plane.6
  368.3 1.9 collective-permute-start.17
  370.2 2.0 collective-permute-start.18
  372.2 0.6 collective-permute-start.19
  372.8 1.9 collective-permute-start.24
  374.7 1.4 collective-permute-start.25
  376.1 2.1 combine_depth.7
  378.2 5.2 %input_backward.1 = f32[2,576,1024]{2,1,0:T(8,128)} custom-call(s32[2]{0:T(128)} %class_ref.15, f32[2,576,1024]{2,1,0:T(8,128)} %get-tuple-element.196.grad_inner_ref, bf16[2,576,256]{2,1,0:T(8,128)(2,1)} %get-tuple-element.235.grad_first_ref, bf16[1024,256]{1,0:T(8,128)(2,1)} %get-tuple-element.215.std_in_ref), custom_call_target="tpu_custom_call" | custom-call | flops 603979776 | bytes 12582912 | tf_op jit(solution)/shard_map/input_backward/pallas_call | solution.py:1337
  383.5 2.1 sum_vectors.1
  385.6 1.9 combine_depth.6
  387.5 0.1 collective-permute-done.24.refs_2_
  387.6 0.6 copy-done.16
  388.2 1.7 combine_depth.5
  390.0 0.6 copy-done.12
  390.6 1.7 combine_depth.4
  392.4 4.0 copy.57
  (64 shorter events, 0.3 us)
Async XLA Ops:
  7.2 4.8 %copy-start.18 = (s32[8]{0:T(128)S(1)}, s32[8]{0:T(128)}, u32[]{:S(2)}) copy-start(s32[8]{0:T(128)} %param.31) | copy-start | bytes 100
  7.2 84.1 %all-to-all-start = ((bf16[4,576,768]{2,1,0:T(8,128)(2,1)}), bf16[4,576,768]{2,1,0:T(8,128)(2,1)}, u32[]{:S(2)}, u32[]{:S(2)}) async-start(bf16[4,576,768]{2,1,0:T(8,128)(2,1)} %bitcast.18), calls=%async_computation | async-start | bytes 7077888 | tf_op jit(solution)/shard_map/all_to_all | solution.py:1602
  154.5 20.3 %collective-permute-start = (bf16[16,12,8,768]{3,2,1,0:T(8,128)(2,1)}, bf16[16,12,8,768]{3,2,1,0:T(8,128)(2,1)}, u32[]{:S(2)}, u32[]{:S(2)}) collective-permute-start(bf16[16,12,8,768]{3,2,1,0:T(8,128)(2,1)} %get-tuple-element.169), channel_id=1, source_target_pairs={{0,1},{1,0},{2,3},{3,2},{4,5},{5,4},{6,7},{7,6},{8,9},{9,8},{10,11... | collective-permute-start | bytes 7077896 | tf_op jit(solution)/shard_map/ppermute | solution.py:1494
  155.1 19.8 %collective-permute-start.1 = (bf16[16,12,8,768]{3,2,1,0:T(8,128)(2,1)}, bf16[16,12,8,768]{3,2,1,0:T(8,128)(2,1)}, u32[]{:S(2)}, u32[]{:S(2)}) collective-permute-start(bf16[16,12,8,768]{3,2,1,0:T(8,128)(2,1)} %get-tuple-element.170), channel_id=1, source_target_pairs={{0,1},{1,0},{2,3},{3,2},{4,5},{5,4},{6,7},{7,6},{8,9},{9,8},{10,11... | collective-permute-start | bytes 7077896 | tf_op jit(solution)/shard_map/ppermute | solution.py:1494
  155.2 100.4 %all-to-all-start.1 = ((bf16[4,576,768]{2,1,0:T(8,128)(2,1)}), bf16[4,576,768]{2,1,0:T(8,128)(2,1)}, u32[]{:S(2)}, u32[]{:S(2)}) async-start(bf16[4,576,768]{2,1,0:T(8,128)(2,1)} %get-tuple-element.185), calls=%async_computation.1 | async-start | bytes 7077888 | tf_op jit(solution)/shard_map/all_to_all | solution.py:1645
  159.9 223.6 %all-gather.3.cloned.1.call-start = ((), (), s32[]{:S(2)}) async-start(), calls=%async_computation.2 | async-start | bytes 1622016 | tf_op jit(solution)/shard_map/all_gather | solution.py:1656
  181.1 74.5 %collective-permute-start.2 = (bf16[4,24,8,768]{3,2,1,0:T(8,128)(2,1)}, bf16[4,24,8,768]{3,2,1,0:T(8,128)(2,1)S(1)}, u32[]{:S(2)}, u32[]{:S(2)}) collective-permute-start(bf16[4,24,8,768]{3,2,1,0:T(8,128)(2,1)} %get-tuple-element.182), channel_id=1, source_target_pairs={{0,2},{1,3},{2,0},{3,1},{4,6},{5,7},{6,4},{7,5},{8,10},{9,11},{10,... | collective-permute-start | bytes 3538952 | tf_op jit(solution)/shard_map/ppermute | solution.py:1494
  184.0 71.6 %collective-permute-start.3 = (bf16[4,24,8,768]{3,2,1,0:T(8,128)(2,1)}, bf16[4,24,8,768]{3,2,1,0:T(8,128)(2,1)}, u32[]{:S(2)}, u32[]{:S(2)}) collective-permute-start(bf16[4,24,8,768]{3,2,1,0:T(8,128)(2,1)} %get-tuple-element.183), channel_id=1, source_target_pairs={{0,4},{1,5},{2,6},{3,7},{4,0},{5,1},{6,2},{7,3},{8,12},{9,13},{10,... | collective-permute-start | bytes 3538952 | tf_op jit(solution)/shard_map/ppermute | solution.py:1494
  186.0 69.7 %collective-permute-start.4 = (bf16[4,24,8,768]{3,2,1,0:T(8,128)(2,1)}, bf16[4,24,8,768]{3,2,1,0:T(8,128)(2,1)}, u32[]{:S(2)}, u32[]{:S(2)}) collective-permute-start(bf16[4,24,8,768]{3,2,1,0:T(8,128)(2,1)} %get-tuple-element.184), channel_id=1, source_target_pairs={{0,6},{1,7},{2,4},{3,5},{4,2},{5,3},{6,0},{7,1},{8,14},{9,15},{10,... | collective-permute-start | bytes 3538952 | tf_op jit(solution)/shard_map/ppermute | solution.py:1494
  255.5 33.5 %collective-permute-start.5 = (bf16[16,12,8,768]{3,2,1,0:T(8,128)(2,1)}, bf16[16,12,8,768]{3,2,1,0:T(8,128)(2,1)}, u32[]{:S(2)}, u32[]{:S(2)}) collective-permute-start(bf16[16,12,8,768]{3,2,1,0:T(8,128)(2,1)} %get-tuple-element.199), channel_id=1, source_target_pairs={{0,1},{1,0},{2,3},{3,2},{4,5},{5,4},{6,7},{7,6},{8,9},{9,8},{10,11... | collective-permute-start | bytes 7077896 | tf_op jit(solution)/shard_map/ppermute | solution.py:1494
  255.6 1.0 copy-start.1
  260.5 28.5 %collective-permute-start.6 = (bf16[24,8,768]{2,1,0:T(8,128)(2,1)}, bf16[24,8,768]{2,1,0:T(8,128)(2,1)S(1)}, u32[]{:S(2)}, u32[]{:S(2)}) collective-permute-start(bf16[24,8,768]{2,1,0:T(8,128)(2,1)} %get-tuple-element.200), channel_id=1, source_target_pairs={{0,8},{1,9},{2,10},{3,11},{4,12},{5,13},{6,14},{7,15},{8,0},{9,1},... | collective-permute-start | bytes 884744 | tf_op jit(solution)/shard_map/ppermute | solution.py:1494
  262.2 26.8 %collective-permute-start.7 = (bf16[24,8,768]{2,1,0:T(8,128)(2,1)}, bf16[24,8,768]{2,1,0:T(8,128)(2,1)S(1)}, u32[]{:S(2)}, u32[]{:S(2)}) collective-permute-start(bf16[24,8,768]{2,1,0:T(8,128)(2,1)} %get-tuple-element.201), channel_id=1, source_target_pairs={{0,16},{1,17},{2,18},{3,19},{4,20},{5,21},{6,22},{7,23},{8,24},{9,... | collective-permute-start | bytes 884744 | tf_op jit(solution)/shard_map/ppermute | solution.py:1494
  264.7 24.3 %collective-permute-start.8 = (bf16[24,8,768]{2,1,0:T(8,128)(2,1)}, bf16[24,8,768]{2,1,0:T(8,128)(2,1)}, u32[]{:S(2)}, u32[]{:S(2)}) collective-permute-start(bf16[24,8,768]{2,1,0:T(8,128)(2,1)} %get-tuple-element.202), channel_id=1, source_target_pairs={{0,24},{1,25},{2,26},{3,27},{4,28},{5,29},{6,30},{7,31},{8,16},{9,... | collective-permute-start | bytes 884744 | tf_op jit(solution)/shard_map/ppermute | solution.py:1494
  288.9 28.4 %collective-permute-start.9 = (bf16[16,7,8,768]{3,2,1,0:T(8,128)(2,1)}, bf16[16,7,8,768]{3,2,1,0:T(8,128)(2,1)S(1)}, u32[]{:S(2)}, u32[]{:S(2)}) collective-permute-start(bf16[16,7,8,768]{3,2,1,0:T(8,128)(2,1)} %get-tuple-element.223), channel_id=1, source_target_pairs={{0,1},{1,0},{2,3},{3,2},{4,5},{5,4},{6,7},{7,6},{8,9},{9,8},{10,11... | collective-permute-start | bytes 4128776 | tf_op jit(solution)/shard_map/ppermute | solution.py:1494
  289.0 4.5 %copy-start.7 = (bf16[24,8,768]{2,1,0:T(8,128)(2,1)}, bf16[24,8,768]{2,1,0:T(8,128)(2,1)S(1)}, u32[]{:S(2)}) copy-start(bf16[24,8,768]{2,1,0:T(8,128)(2,1)S(1)} %collective-permute-done.6.refs_1_) | copy-start | bytes 884740
  289.0 4.5 %copy-start.8 = (bf16[24,8,768]{2,1,0:T(8,128)(2,1)}, bf16[24,8,768]{2,1,0:T(8,128)(2,1)S(1)}, u32[]{:S(2)}) copy-start(bf16[24,8,768]{2,1,0:T(8,128)(2,1)S(1)} %collective-permute-done.7.refs_2_) | copy-start | bytes 884740
  293.5 23.8 %collective-permute-start.10 = (bf16[4,12,8,768]{3,2,1,0:T(8,128)(2,1)}, bf16[4,12,8,768]{3,2,1,0:T(8,128)(2,1)S(1)}, u32[]{:S(2)}, u32[]{:S(2)}) collective-permute-start(bf16[4,12,8,768]{3,2,1,0:T(8,128)(2,1)} %get-tuple-element.224), channel_id=1, source_target_pairs={{0,2},{1,3},{2,0},{3,1},{4,6},{5,7},{6,4},{7,5},{8,10},{9,11},{10,... | collective-permute-start | bytes 1769480 | tf_op jit(solution)/shard_map/ppermute | solution.py:1494
  295.4 22.0 %collective-permute-start.11 = (bf16[4,12,8,768]{3,2,1,0:T(8,128)(2,1)}, bf16[4,12,8,768]{3,2,1,0:T(8,128)(2,1)}, u32[]{:S(2)}, u32[]{:S(2)}) collective-permute-start(bf16[4,12,8,768]{3,2,1,0:T(8,128)(2,1)} %get-tuple-element.225), channel_id=1, source_target_pairs={{0,4},{1,5},{2,6},{3,7},{4,0},{5,1},{6,2},{7,3},{8,12},{9,13},{10,... | collective-permute-start | bytes 1769480 | tf_op jit(solution)/shard_map/ppermute | solution.py:1494
  297.1 30.3 %collective-permute-start.12 = (bf16[4,12,8,768]{3,2,1,0:T(8,128)(2,1)}, bf16[4,12,8,768]{3,2,1,0:T(8,128)(2,1)}, u32[]{:S(2)}, u32[]{:S(2)}) collective-permute-start(bf16[4,12,8,768]{3,2,1,0:T(8,128)(2,1)} %get-tuple-element.226), channel_id=1, source_target_pairs={{0,6},{1,7},{2,4},{3,5},{4,2},{5,3},{6,0},{7,1},{8,14},{9,15},{10,... | collective-permute-start | bytes 1769480 | tf_op jit(solution)/shard_map/ppermute | solution.py:1494
  317.3 10.1 %copy-start = (bf16[16,7,8,768]{3,2,1,0:T(8,128)(2,1)}, bf16[16,7,8,768]{3,2,1,0:T(8,128)(2,1)S(1)}, u32[]{:S(2)}) copy-start(bf16[16,7,8,768]{3,2,1,0:T(8,128)(2,1)S(1)} %collective-permute-done.9.refs_2_) | copy-start | bytes 4128772
  317.3 20.2 %copy-start.2 = (bf16[4,12,8,768]{3,2,1,0:T(8,128)(2,1)}, bf16[4,12,8,768]{3,2,1,0:T(8,128)(2,1)S(1)}, u32[]{:S(2)}) copy-start(bf16[4,12,8,768]{3,2,1,0:T(8,128)(2,1)S(1)} %collective-permute-done.10.refs_2_) | copy-start | bytes 1769476
  327.4 7.3 %collective-permute-start.13 = (bf16[17,17,8,256]{3,2,1,0:T(8,128)(2,1)}, bf16[17,17,8,256]{3,2,1,0:T(8,128)(2,1)}, u32[]{:S(2)}, u32[]{:S(2)}) collective-permute-start(bf16[17,17,8,256]{3,2,1,0:T(8,128)(2,1)} %get-tuple-element.238), channel_id=1, source_target_pairs={{0,1},{1,0},{2,3},{3,2},{4,5},{5,4},{6,7},{7,6},{8,9},{9,8},{10,11... | collective-permute-start | bytes 3551240 | tf_op jit(solution)/shard_map/ppermute | solution.py:1494
  331.2 11.1 %collective-permute-start.20 = (bf16[4,7,8,768]{3,2,1,0:T(8,128)(2,1)}, bf16[4,7,8,768]{3,2,1,0:T(8,128)(2,1)S(1)}, u32[]{:S(2)}, u32[]{:S(2)}) collective-permute-start(bf16[4,7,8,768]{3,2,1,0:T(8,128)(2,1)} %get-tuple-element.256), channel_id=1, source_target_pairs={{0,2},{1,3},{2,0},{3,1},{4,6},{5,7},{6,4},{7,5},{8,10},{9,11},{10,... | collective-permute-start | bytes 1032200 | tf_op jit(solution)/shard_map/ppermute | solution.py:1494
  331.9 15.6 %collective-permute-start.21 = (bf16[4,7,8,768]{3,2,1,0:T(8,128)(2,1)}, bf16[4,7,8,768]{3,2,1,0:T(8,128)(2,1)}, u32[]{:S(2)}, u32[]{:S(2)}) collective-permute-start(bf16[4,7,8,768]{3,2,1,0:T(8,128)(2,1)} %get-tuple-element.257), channel_id=1, source_target_pairs={{0,4},{1,5},{2,6},{3,7},{4,0},{5,1},{6,2},{7,3},{8,12},{9,13},{10,... | collective-permute-start | bytes 1032200 | tf_op jit(solution)/shard_map/ppermute | solution.py:1494
  333.6 17.7 %collective-permute-start.22 = (bf16[4,7,8,768]{3,2,1,0:T(8,128)(2,1)}, bf16[4,7,8,768]{3,2,1,0:T(8,128)(2,1)}, u32[]{:S(2)}, u32[]{:S(2)}) collective-permute-start(bf16[4,7,8,768]{3,2,1,0:T(8,128)(2,1)} %get-tuple-element.258), channel_id=1, source_target_pairs={{0,6},{1,7},{2,4},{3,5},{4,2},{5,3},{6,0},{7,1},{8,14},{9,15},{10,... | collective-permute-start | bytes 1032200 | tf_op jit(solution)/shard_map/ppermute | solution.py:1494
  337.6 19.2 %collective-permute-start.14 = (bf16[5,17,8,256]{3,2,1,0:T(8,128)(2,1)}, bf16[5,17,8,256]{3,2,1,0:T(8,128)(2,1)S(1)}, u32[]{:S(2)}, u32[]{:S(2)}) collective-permute-start(bf16[5,17,8,256]{3,2,1,0:T(8,128)(2,1)} %get-tuple-element.240), channel_id=1, source_target_pairs={{0,2},{1,3},{2,0},{3,1},{4,6},{5,7},{6,4},{7,5},{8,10},{9,11},{10,... | collective-permute-start | bytes 1044488 | tf_op jit(solution)/shard_map/ppermute | solution.py:1494
  338.2 23.9 %collective-permute-start.15 = (bf16[5,17,8,256]{3,2,1,0:T(8,128)(2,1)}, bf16[5,17,8,256]{3,2,1,0:T(8,128)(2,1)S(1)}, u32[]{:S(2)}, u32[]{:S(2)}) collective-permute-start(bf16[5,17,8,256]{3,2,1,0:T(8,128)(2,1)} %get-tuple-element.241), channel_id=1, source_target_pairs={{0,4},{1,5},{2,6},{3,7},{4,0},{5,1},{6,2},{7,3},{8,12},{9,13},{10,... | collective-permute-start | bytes 1044488 | tf_op jit(solution)/shard_map/ppermute | solution.py:1494
  342.3 0.7 copy-start.6
  343.0 22.4 %collective-permute-start.16 = (bf16[5,17,8,256]{3,2,1,0:T(8,128)(2,1)}, bf16[5,17,8,256]{3,2,1,0:T(8,128)(2,1)S(1)}, u32[]{:S(2)}, u32[]{:S(2)}) collective-permute-start(bf16[5,17,8,256]{3,2,1,0:T(8,128)(2,1)} %get-tuple-element.242), channel_id=1, source_target_pairs={{0,6},{1,7},{2,4},{3,5},{4,2},{5,3},{6,0},{7,1},{8,14},{9,15},{10,... | collective-permute-start | bytes 1044488 | tf_op jit(solution)/shard_map/ppermute | solution.py:1494
  347.5 22.8 %collective-permute-start.26 = (bf16[12,8,768]{2,1,0:T(8,128)(2,1)}, bf16[12,8,768]{2,1,0:T(8,128)(2,1)S(1)}, u32[]{:S(2)}, u32[]{:S(2)}) collective-permute-start(bf16[12,8,768]{2,1,0:T(8,128)(2,1)} %get-tuple-element.268), channel_id=1, source_target_pairs={{0,8},{1,9},{2,10},{3,11},{4,12},{5,13},{6,14},{7,15},{8,0},{9,1},... | collective-permute-start | bytes 442376 | tf_op jit(solution)/shard_map/ppermute | solution.py:1494
  351.3 20.9 %collective-permute-start.27 = (bf16[12,8,768]{2,1,0:T(8,128)(2,1)}, bf16[12,8,768]{2,1,0:T(8,128)(2,1)S(1)}, u32[]{:S(2)}, u32[]{:S(2)}) collective-permute-start(bf16[12,8,768]{2,1,0:T(8,128)(2,1)} %get-tuple-element.269), channel_id=1, source_target_pairs={{0,16},{1,17},{2,18},{3,19},{4,20},{5,21},{6,22},{7,23},{8,24},{9,... | collective-permute-start | bytes 442376 | tf_op jit(solution)/shard_map/ppermute | solution.py:1494
  356.7 8.7 %copy-start.3 = (bf16[5,17,8,256]{3,2,1,0:T(8,128)(2,1)}, bf16[5,17,8,256]{3,2,1,0:T(8,128)(2,1)S(1)}, u32[]{:S(2)}) copy-start(bf16[5,17,8,256]{3,2,1,0:T(8,128)(2,1)S(1)} %collective-permute-done.14.refs_2_) | copy-start | bytes 1044484
  356.7 16.1 %collective-permute-start.28 = (bf16[12,8,768]{2,1,0:T(8,128)(2,1)}, bf16[12,8,768]{2,1,0:T(8,128)(2,1)S(1)}, u32[]{:S(2)}, u32[]{:S(2)}) collective-permute-start(bf16[12,8,768]{2,1,0:T(8,128)(2,1)} %get-tuple-element.270), channel_id=1, source_target_pairs={{0,24},{1,25},{2,26},{3,27},{4,28},{5,29},{6,30},{7,31},{8,16},{9,... | collective-permute-start | bytes 442376 | tf_op jit(solution)/shard_map/ppermute | solution.py:1494
  362.2 3.2 copy-start.4
  362.2 12.6 %collective-permute-start.23 = (bf16[7,8,768]{2,1,0:T(8,128)(2,1)}, bf16[7,8,768]{2,1,0:T(8,128)(2,1)S(1)}, u32[]{:S(2)}, u32[]{:S(2)}) collective-permute-start(bf16[7,8,768]{2,1,0:T(8,128)(2,1)} %get-tuple-element.260), channel_id=1, source_target_pairs={{0,8},{1,9},{2,10},{3,11},{4,12},{5,13},{6,14},{7,15},{8,0},{9,1},... | collective-permute-start | bytes 258056 | tf_op jit(solution)/shard_map/ppermute | solution.py:1494
  365.4 0.8 copy-start.5
  368.3 21.6 %collective-permute-start.17 = (bf16[23,8,256]{2,1,0:T(8,128)(2,1)}, bf16[23,8,256]{2,1,0:T(8,128)(2,1)S(1)}, u32[]{:S(2)}, u32[]{:S(2)}) collective-permute-start(bf16[23,8,256]{2,1,0:T(8,128)(2,1)} %get-tuple-element.244), channel_id=1, source_target_pairs={{0,8},{1,9},{2,10},{3,11},{4,12},{5,13},{6,14},{7,15},{8,0},{9,1},... | collective-permute-start | bytes 282632 | tf_op jit(solution)/shard_map/ppermute | solution.py:1494
  370.2 13.2 %copy-start.9 = (bf16[12,8,768]{2,1,0:T(8,128)(2,1)}, bf16[12,8,768]{2,1,0:T(8,128)(2,1)S(1)}, u32[]{:S(2)}) copy-start(bf16[12,8,768]{2,1,0:T(8,128)(2,1)S(1)} %collective-permute-done.26.refs_1_) | copy-start | bytes 442372
  370.2 19.7 %collective-permute-start.18 = (bf16[23,8,256]{2,1,0:T(8,128)(2,1)}, bf16[23,8,256]{2,1,0:T(8,128)(2,1)S(1)}, u32[]{:S(2)}, u32[]{:S(2)}) collective-permute-start(bf16[23,8,256]{2,1,0:T(8,128)(2,1)} %get-tuple-element.245), channel_id=1, source_target_pairs={{0,16},{1,17},{2,18},{3,19},{4,20},{5,21},{6,22},{7,23},{8,24},{9,... | collective-permute-start | bytes 282632 | tf_op jit(solution)/shard_map/ppermute | solution.py:1494
  372.2 11.3 %copy-start.10 = (bf16[12,8,768]{2,1,0:T(8,128)(2,1)}, bf16[12,8,768]{2,1,0:T(8,128)(2,1)S(1)}, u32[]{:S(2)}) copy-start(bf16[12,8,768]{2,1,0:T(8,128)(2,1)S(1)} %collective-permute-done.27.refs_2_) | copy-start | bytes 442372
  372.2 17.8 %collective-permute-start.19 = (bf16[23,8,256]{2,1,0:T(8,128)(2,1)}, bf16[23,8,256]{2,1,0:T(8,128)(2,1)S(1)}, u32[]{:S(2)}, u32[]{:S(2)}) collective-permute-start(bf16[23,8,256]{2,1,0:T(8,128)(2,1)} %get-tuple-element.246), channel_id=1, source_target_pairs={{0,24},{1,25},{2,26},{3,27},{4,28},{5,29},{6,30},{7,31},{8,16},{9,... | collective-permute-start | bytes 282632 | tf_op jit(solution)/shard_map/ppermute | solution.py:1494
  372.8 10.7 %copy-start.11 = (bf16[12,8,768]{2,1,0:T(8,128)(2,1)}, bf16[12,8,768]{2,1,0:T(8,128)(2,1)S(1)}, u32[]{:S(2)}) copy-start(bf16[12,8,768]{2,1,0:T(8,128)(2,1)S(1)} %collective-permute-done.28.refs_3_) | copy-start | bytes 442372
  372.8 14.8 %collective-permute-start.24 = (bf16[7,8,768]{2,1,0:T(8,128)(2,1)}, bf16[7,8,768]{2,1,0:T(8,128)(2,1)S(1)}, u32[]{:S(2)}, u32[]{:S(2)}) collective-permute-start(bf16[7,8,768]{2,1,0:T(8,128)(2,1)} %get-tuple-element.261), channel_id=1, source_target_pairs={{0,16},{1,17},{2,18},{3,19},{4,20},{5,21},{6,22},{7,23},{8,24},{9,... | collective-permute-start | bytes 258056 | tf_op jit(solution)/shard_map/ppermute | solution.py:1494
  374.7 8.7 %copy-start.15 = (bf16[7,8,768]{2,1,0:T(8,128)(2,1)}, bf16[7,8,768]{2,1,0:T(8,128)(2,1)S(1)}, u32[]{:S(2)}) copy-start(bf16[7,8,768]{2,1,0:T(8,128)(2,1)S(1)} %collective-permute-done.23.refs_1_) | copy-start | bytes 258052
  374.7 12.9 %collective-permute-start.25 = (bf16[7,8,768]{2,1,0:T(8,128)(2,1)}, bf16[7,8,768]{2,1,0:T(8,128)(2,1)S(1)}, u32[]{:S(2)}, u32[]{:S(2)}) collective-permute-start(bf16[7,8,768]{2,1,0:T(8,128)(2,1)} %get-tuple-element.262), channel_id=1, source_target_pairs={{0,24},{1,25},{2,26},{3,27},{4,28},{5,29},{6,30},{7,31},{8,16},{9,... | collective-permute-start | bytes 258056 | tf_op jit(solution)/shard_map/ppermute | solution.py:1494
  387.6 0.6 copy-start.16
  387.6 0.7 copy-start.17
  389.9 0.6 copy-start.12
  389.9 0.7 copy-start.13
  390.0 0.7 copy-start.14
Sparse Core Ops, SparseCore 0:
  255.7 72.5 all-gather.2

commit v3 on v2

--- a/solution.py
+++ b/solution.py
@@ -137,6 +137,14 @@
 
 PAIRS = 16
 VECTORS = 3
+
+
+def store_pairs(values, mine_ref, other_ref, core):
+    pairs, parts = mine_ref.shape[:2]
+    for pair in range(pairs):
+        for ref, side in ((mine_ref, core), (other_ref, 1 - core)):
+            at = pl.multiple_of((2 * pair + side) * parts * 8, 8)
+            ref[pair] = sections_of(values[pl.ds(at, parts * 8), :])
 
 
 def store_split(ref, start, values):
@@ -204,7 +212,7 @@
     image_class = class_ref[image]
     mask[...] = validity_mask(image_class, cells)
     count = valid_count(image_class)
-    chunk = 96
+    chunk = cells
     steps = cells // chunk
 
     def stats(values_ref, stat_ref, sums):
@@ -380,7 +388,7 @@
 ):
     image = pl.program_id(0)
     cells, width = tokens_ref.shape[1:]
-    chunk = 96
+    chunk = cells
     steps = cells // chunk
     scale = (width // HEADS) ** -0.5
 
@@ -404,16 +412,12 @@
         value = dot_nn(normed, joint_ref[:, last]) + value_bias[:, here]
         value_ref[0, :, here] = value.astype(bf16)
 
-    _, column = cell_grid(cells)
-    image_class = class_ref[image]
-    cell = lax.broadcasted_iota(jnp.int32, (8, cells), 1).astype(f32)
-    cell_row = jnp.floor((cell + 0.5) * (1.0 / SIDE))
-    cell_column = cell - cell_row * SIDE
-    outside = jnp.where((cell_row < SIDE_SMALL) & (cell_column < SIDE_SMALL), 0.0, -1000000000.0)
-    key_bias = jnp.where(image_class == 1, 0.0, outside)[0:1]
     upper = lax.broadcasted_iota(jnp.int32, (cells, LANES), 1) >= LANES // 2
-
-    @pl.loop(0, width // LANES)
+    key_bias = (validity_mask(class_ref[image], cells) - 1.0) * 1000000000.0
+    key_bias = key_bias.astype(bf16)
+    lane = lax.broadcasted_iota(jnp.int32, (cells, LANES), 1)
+
+    @pl.loop(0, width // LANES, unroll=True)
     def _(pair):
         lanes = rows_at(pair, LANES)
         query = query_ref[0, :, lanes] * bf16(scale)
@@ -422,14 +426,17 @@
         outs = []
         for half in range(2):
             mine = upper if half else jnp.logical_not(upper)
-            scores = dot_nt(jnp.where(mine, query, bf16(0)), key) + key_bias
-            top = jnp.max(scores, axis=-1, keepdims=True)
+            spare = lane == (0 if half else LANES // 2)
+            scores = dot_nt(
+                jnp.where(mine, key, jnp.where(spare, key_bias, bf16(0))),
+                jnp.where(spare, bf16(1), query),
+            )
+            top = jnp.max(scores, axis=0, keepdims=True)
             weights = jnp.exp(scores - top)
-            weight_sum = jnp.sum(weights, axis=-1, keepdims=True)
+            weight_sum = total(weights)
             probs = (weights * (1.0 / weight_sum)).astype(bf16)
-            outs.append(dot_nn(probs, value))
-            log_total = jnp.broadcast_to(top + jnp.log(weight_sum), (cells, LANES))
-            log_total_ref[0, 2 * pair + half] = log_total.T[0:8]
+            outs.append(dot_tn(probs, value))
+            log_total_ref[0, 2 * pair + half] = jnp.broadcast_to(top + jnp.log(weight_sum), (8, cells))
         mixed_ref[0, :, lanes] = jnp.where(upper, outs[1], outs[0]).astype(bf16)
 
     @pl.loop(0, steps)
@@ -501,51 +508,86 @@
     mine_ref,
     core_ref,
     normed_ref,
-    resid_ref,
-    cotangent_ref,
+    cotangent0_ref,
+    cotangent1_ref,
     expand_ref,
     expand_bias_ref,
     shrink_ref,
     shrink_bias_ref,
+    gain2_ref,
+    resid_ref,
+    mix_ref,
     output_ref,
-    grad_normed_ref,
+    grad_resid_ref,
+    grad_mixed_ref,
     shrink_mine_ref,
     shrink_other_ref,
     expand_mine_ref,
     expand_other_ref,
     grad_expand_bias_ref,
     grad_shrink_bias_ref,
+    sums_ref,
     sent,
     result,
+    grad_normed,
     hidden,
     grad_pre,
     normed_turned,
     shrink_total,
     expand_total,
     biases,
+    resid,
+    mix,
+    empty,
+    in_sems,
+    out_sems,
+    empty_sems,
 ):
     step = pl.program_id(0)
+    last = pl.num_programs(0) - 1
     images, cells, width = normed_ref.shape
+    slots = output_ref.shape[0]
     block = expand_ref.shape[1]
     part = cells // 2
+    loads = [
+        pltpu.make_async_copy(resid_ref, resid, in_sems.at[0]),
+        pltpu.make_async_copy(mix_ref, mix, in_sems.at[1]),
+    ]
+
+    def image_rows(image):
+        return slice(image * cells, (image + 1) * cells)
+
+    def each_empty(act):
+        for slot in range(slots):
+            taken = mine_ref[0] == slot
+            for image in range(1, images):
+                taken = taken | (mine_ref[image] == slot)
+
+            @pl.when(jnp.logical_not(taken))
+            def _():
+                act(pltpu.make_async_copy(empty, output_ref.at[slot], empty_sems.at[slot]))
 
     @pl.when(step == 0)
     def _():
+        empty[...] = jnp.zeros_like(empty)
+        each_empty(lambda copy: copy.start())
+        for copy in loads:
+            copy.start()
         sums = jnp.zeros((8, width), f32)
-        for image in range(images):
+        for image, ref in enumerate((cotangent0_ref, cotangent1_ref)):
             keep = spread_lanes(validity_mask(class_ref[image], cells), width)
-            grad = cotangent_ref[mine_ref[image]].astype(f32) * keep
-            sent[image * cells : (image + 1) * cells, :] = grad.astype(bf16)
+            grad = ref[0].astype(f32) * keep
+            sent[image_rows(image), :] = grad.astype(bf16)
             sums = sums + fold(grad)
-            result[image * cells : (image + 1) * cells, :] = resid_ref[image] + line(shrink_bias_ref)
-            normed_turned[:, image * cells : (image + 1) * cells] = normed_ref[image].T
+            normed_turned[:, image_rows(image)] = normed_ref[image].T
         grad_shrink_bias_ref[...] = sums
-        grad_normed_ref[...] = jnp.zeros_like(grad_normed_ref)
+        result[...] = jnp.zeros_like(result)
+        grad_normed[...] = jnp.zeros_like(grad_normed)
         every = line(expand_bias_ref)
         for k in range(biases.shape[0]):
             biases[k : k + 1, :] = every[:, k * block : (k + 1) * block]
 
-    bias_sums = jnp.zeros((8, expand_ref.shape[1]), f32)
+    bias_sums = jnp.zeros((8, block), f32)
     for image in range(images):
         for piece in range(cells // part):
             local = slice(piece * part, (piece + 1) * part)
@@ -560,38 +602,69 @@
             grad_low = grad.astype(bf16)
             grad_pre[rows, :] = grad_low
             result[rows, :] += dot_nn(low, shrink_ref[...])
-            grad_normed_ref[image, local, :] += dot_nt(grad_low, expand_ref[...])
+            grad_normed[rows, :] += dot_nt(grad_low, expand_ref[...])
     grad_expand_bias_ref[...] = bias_sums
     shrink_total[...] = dot_tn(hidden[...], sent[...])
     expand_total[...] = dot_nn(normed_turned[...], grad_pre[...])
     core = core_ref[0]
-    size = shrink_mine_ref.shape[1] * 8
-    for pair in range(shrink_mine_ref.shape[0]):
-        at = pl.multiple_of((2 * pair + core) * size, 8)
-        shrink_mine_ref[pair] = sections_of(shrink_total[pl.ds(at, size), :])
-        at = pl.multiple_of((2 * pair + 1 - core) * size, 8)
-        shrink_other_ref[pair] = sections_of(shrink_total[pl.ds(at, size), :])
-    size = expand_mine_ref.shape[1] * 8
-    for pair in range(PAIRS):
-        at = pl.multiple_of((2 * pair + core) * size, 8)
-        expand_mine_ref[pair] = sections_of(expand_total[pl.ds(at, size), :])
-        at = pl.multiple_of((2 * pair + 1 - core) * size, 8)
-        expand_other_ref[pair] = sections_of(expand_total[pl.ds(at, size), :])
-
-    @pl.when(step == pl.num_programs(0) - 1)
+    store_pairs(shrink_total, shrink_mine_ref, shrink_other_ref, core)
+    store_pairs(expand_total, expand_mine_ref, expand_other_ref, core)
+
+    @pl.when(step == last)
     def _():
-        output_ref[...] = jnp.zeros_like(output_ref)
+        for copy in loads:
+            copy.wait()
+        stores = []
         for image in range(images):
+            rows = image_rows(image)
             keep = spread_lanes(validity_mask(class_ref[image], cells), width)
-            rows = result[image * cells : (image + 1) * cells, :] * keep
-            output_ref[mine_ref[image]] = rows.astype(bf16)
-
-
-def feed(image_class, mine, core, normed, resid, cotangent, expand, expand_bias, shrink, shrink_bias):
+            out = (resid[image] + result[rows, :] + line(shrink_bias_ref)) * keep
+            hidden[rows, :] = out.astype(bf16)
+            stores.append(
+                pltpu.make_async_copy(
+                    hidden.at[pl.ds(image * cells, cells)],
+                    output_ref.at[mine_ref[image]],
+                    out_sems.at[3 * image],
+                )
+            )
+            stores[-1].start()
+        sums = [jnp.zeros((8, width), f32)] * 3
+        for image in range(images):
+            rows = image_rows(image)
+            normal, row_scale = row_norm(resid[image])
+            grad = grad_normed[rows, :]
+            sums[0] = sums[0] + fold(grad * normal)
+            sums[1] = sums[1] + fold(grad)
+            grad = sent[rows, :].astype(f32) + row_norm_back(grad, normal, row_scale, line(gain2_ref))
+            sums[2] = sums[2] + fold(grad)
+            resid[image] = grad
+            stores.append(
+                pltpu.make_async_copy(resid.at[image], grad_resid_ref.at[image], out_sems.at[3 * image + 1])
+            )
+            stores[-1].start()
+            grad_pre[rows, :] = dot_nt(grad.astype(bf16), mix[...]).astype(bf16)
+            stores.append(
+                pltpu.make_async_copy(
+                    grad_pre.at[pl.ds(image * cells, cells)],
+                    grad_mixed_ref.at[image],
+                    out_sems.at[3 * image + 2],
+                )
+            )
+            stores[-1].start()
+        for k in range(3):
+            sums_ref[k] = sums[k]
+        each_empty(lambda copy: copy.wait())
+        for copy in stores:
+            copy.wait()
+
+
+def feed(
+    image_class, mine, core, normed, resid, cotangent, expand, expand_bias, shrink, shrink_bias, gain2, mix
+):
     images, cells, width = normed.shape
     inner = expand.shape[1]
     slots = cotangent.shape[0]
-    block = width // 2
+    block = width
     rows = images * cells
     shrink_size = inner // (2 * PAIRS)
     pairs = block // (2 * shrink_size)
@@ -599,45 +672,52 @@
     shrink_half = jax.ShapeDtypeStruct((PAIRS, shrink_size // 8, 8, width), bf16)
     expand_half = jax.ShapeDtypeStruct((PAIRS, expand_size // 8 * (inner // width), 8, width), bf16)
     shrink_spec = pl.BlockSpec((pairs, shrink_size // 8, 8, width), lambda step, *_: (step, 0, 0, 0))
-    expand_spec = pl.BlockSpec(
-        (PAIRS, expand_size // 8, 8, block), lambda step, *_: (0, step // 2, 0, step % 2)
-    )
+    expand_spec = pl.BlockSpec((PAIRS, expand_size // 8, 8, block), lambda step, *_: (0, step, 0, 0))
+    anywhere = pl.BlockSpec(memory_space=pl.ANY)
     return pl.pallas_call(
         feed_kernel,
         out_shape=(
             jax.ShapeDtypeStruct((slots, cells, width), bf16),
             jax.ShapeDtypeStruct((images, cells, width), f32),
+            jax.ShapeDtypeStruct((images, cells, width), bf16),
             shrink_half,
             shrink_half,
             expand_half,
             expand_half,
             jax.ShapeDtypeStruct((8, inner), f32),
             jax.ShapeDtypeStruct((8, width), f32),
+            jax.ShapeDtypeStruct((3, 8, width), f32),
         ),
         grid_spec=pltpu.PrefetchScalarGridSpec(
             num_scalar_prefetch=3,
             grid=(inner // block,),
             in_specs=[
                 whole((images, cells, width)),
-                whole((images, cells, width)),
-                whole((slots, cells, width)),
+                pl.BlockSpec((1, cells, width), lambda step, classes, mine, core: (mine[0], 0, 0)),
+                pl.BlockSpec((1, cells, width), lambda step, classes, mine, core: (mine[1], 0, 0)),
                 pl.BlockSpec((width, block), lambda step, *_: (0, step)),
                 whole((inner,)),
                 pl.BlockSpec((block, width), lambda step, *_: (step, 0)),
                 whole((width,)),
+                whole((width,)),
+                anywhere,
+                anywhere,
             ],
             out_specs=[
-                whole((slots, cells, width)),
-                whole((images, cells, width)),
+                anywhere,
+                anywhere,
+                anywhere,
                 shrink_spec,
                 shrink_spec,
                 expand_spec,
                 expand_spec,
                 pl.BlockSpec((8, block), lambda step, *_: (0, step)),
                 whole((8, width)),
+                whole((3, 8, width)),
             ],
             scratch_shapes=[
                 pltpu.VMEM((rows, width), bf16),
+                pltpu.VMEM((rows, width), f32),
                 pltpu.VMEM((rows, width), f32),
                 pltpu.VMEM((rows, block), bf16),
                 pltpu.VMEM((rows, block), bf16),
@@ -645,12 +725,32 @@
                 pltpu.VMEM((block, width), f32),
                 pltpu.VMEM((width, block), f32),
                 pltpu.VMEM((inner // block, block), f32),
+                pltpu.VMEM((images, cells, width), f32),
+                pltpu.VMEM((width, width), bf16),
+                pltpu.VMEM((cells, width), bf16),
+                pltpu.SemaphoreType.DMA((2,)),
+                pltpu.SemaphoreType.DMA((3 * images,)),
+                pltpu.SemaphoreType.DMA((slots,)),
             ],
         ),
         compiler_params=pltpu.CompilerParams(vmem_limit_bytes=62 * MIB),
-        cost_estimate=cost(12 * rows * width * inner, 40 * MIB),
+        cost_estimate=cost(14 * rows * width * inner, 40 * MIB),
         name="feed",
-    )(image_class, mine, core, normed, resid, cotangent, expand, expand_bias, shrink, shrink_bias)
+    )(
+        image_class,
+        mine,
+        core,
+        normed,
+        cotangent,
+        cotangent,
+        expand,
+        expand_bias,
+        shrink,
+        shrink_bias,
+        gain2,
+        resid,
+        mix,
+    )
 
 
 def row_norm_back(grad, normal, scale, gain):
@@ -658,73 +758,6 @@
     mean = jnp.mean(inner, axis=-1, keepdims=True)
     cross = jnp.mean(inner * normal, axis=-1, keepdims=True)
     return scale * (inner - mean - normal * cross)
-
-
-def mix_backward_kernel(
-    class_ref,
-    mine_ref,
-    resid_ref,
-    cotangent_ref,
-    grad_normed_two_ref,
-    mix_ref,
-    gain2_ref,
-    grad_resid_ref,
-    grad_mixed_ref,
-    sums_ref,
-    mask,
-):
-    image = pl.program_id(0)
-    cells, width = resid_ref.shape[1:]
-    chunk = 96
-    mask[...] = validity_mask(class_ref[image], cells)
-
-    @pl.when(image == 0)
-    def _():
-        sums_ref[...] = jnp.zeros_like(sums_ref)
-
-    @pl.loop(0, cells // chunk)
-    def _(step):
-        rows = rows_at(step, chunk)
-        normal, row_scale = row_norm(resid_ref[0, rows, :])
-        grad = grad_normed_two_ref[0, rows, :]
-        sums_ref[0] += fold(grad * normal)
-        sums_ref[1] += fold(grad)
-        keep = spread_lanes(mask[rows, :], width)
-        grad = cotangent_ref[0, rows, :].astype(f32) * keep + row_norm_back(
-            grad, normal, row_scale, line(gain2_ref)
-        )
-        sums_ref[2] += fold(grad)
-        grad_resid_ref[0, rows, :] = grad
-        grad_mixed_ref[0, rows, :] = dot_nt(grad.astype(bf16), mix_ref[...]).astype(bf16)
-
-
-def mix_backward(image_class, mine, resid, cotangent, grad_normed_two, mix, gain2):
-    images, cells, width = resid.shape
-    rows = per_image((cells, width))
-    return pl.pallas_call(
-        mix_backward_kernel,
-        out_shape=(
-            jax.ShapeDtypeStruct((images, cells, width), f32),
-            jax.ShapeDtypeStruct((images, cells, width), bf16),
-            jax.ShapeDtypeStruct((3, 8, width), f32),
-        ),
-        grid_spec=pltpu.PrefetchScalarGridSpec(
-            num_scalar_prefetch=2,
-            grid=(images,),
-            in_specs=[
-                rows,
-                pl.BlockSpec((1, cells, width), lambda image, classes, mine: (mine[image], 0, 0)),
-                rows,
-                whole((width, width)),
-                whole((width,)),
-            ],
-            out_specs=[rows, rows, whole((3, 8, width))],
-            scratch_shapes=[pltpu.VMEM((cells, LANES), f32)],
-        ),
-        compiler_params=pltpu.CompilerParams(vmem_limit_bytes=62 * MIB),
-        cost_estimate=cost(2 * images * cells * width * width, 20 * MIB),
-        name="mix_backward",
-    )(image_class, mine, resid, cotangent, grad_normed_two, mix, gain2)
 
 
 def attend_backward_kernel(
@@ -734,32 +767,20 @@
     value_ref,
     log_total_ref,
     grad_mixed_ref,
-    feed_expand_ref,
-    feed_shrink_ref,
-    mix_sums_ref,
     grad_joint_ref,
-    vectors_ref,
     sums_ref,
+    *,
+    image,
 ):
-    image = pl.program_id(0)
     cells, width = query_ref.shape[1:]
     scale = (width // HEADS) ** -0.5
 
-    @pl.when(image == 0)
-    def _():
-        sums_ref[...] = jnp.zeros_like(sums_ref)
-        vectors_ref[...] = jnp.zeros_like(vectors_ref)
-        for k in range(feed_expand_ref.shape[1] // width):
-            vectors_ref[k : k + 1, :] = total(feed_expand_ref[:, k * width : (k + 1) * width])
-        vectors_ref[4:5, :] = total(feed_shrink_ref[...])
-        for k in range(3):
-            vectors_ref[5 + k : 6 + k, :] = total(mix_sums_ref[k])
-
     upper = lax.broadcasted_iota(jnp.int32, (cells, LANES), 1) >= LANES // 2
     key_bias = (validity_mask(class_ref[image], cells) - 1.0) * 1000000000.0
-    bias_wide = jnp.concatenate([key_bias] * 5, axis=1)[:, :cells]
-
-    @pl.loop(0, width // LANES)
+    key_bias = key_bias.astype(bf16)
+    lane = lax.broadcasted_iota(jnp.int32, (cells, LANES), 1)
+
+    @pl.loop(0, width // LANES, unroll=True)
     def _(pair):
         lanes = rows_at(pair, LANES)
         query = query_ref[0, :, lanes] * bf16(scale)
@@ -769,9 +790,13 @@
         grads = []
         for half in range(2):
             mine = upper if half else jnp.logical_not(upper)
-            scores = dot_nt(jnp.where(mine, key, bf16(0)), query)
+            spare = lane == (0 if half else LANES // 2)
+            scores = dot_nt(
+                jnp.where(mine, key, jnp.where(spare, key_bias, bf16(0))),
+                jnp.where(spare, bf16(1), query),
+            )
             log_total = log_total_ref[0, 2 * pair + half, 0:1, :]
-            probs = jnp.exp(scores + bias_wide - log_total)
+            probs = jnp.exp(scores - log_total)
             grad_probs = dot_nt(jnp.where(mine, value, bf16(0)), grad_out)
             weighted = probs * grad_probs
             grad_scores = (weighted - probs * total(weighted)).astype(bf16)
@@ -782,119 +807,135 @@
         for k in range(3):
             grad = jnp.where(upper, grads[1][k], grads[0][k])
             if k != 1:
-                sums_ref[k // 2, :, lanes] += fold(grad)
+                sums_ref[k // 2, :, lanes] = fold(grad)
             where = pl.ds(pl.multiple_of(k * width + pair * LANES, LANES), LANES)
             grad_joint_ref[0, :, where] = grad.astype(bf16)
 
-    @pl.when(image == pl.num_programs(0) - 1)
-    def _():
-        for k in range(2):
-            vectors_ref[8 + k : 9 + k, :] = total(sums_ref[k])
-
-
-def attend_backward(
-    image_class, query, key, value, log_total, grad_mixed, sums_expand, sums_shrink, sums_mix
-):
+
+def attend_backward(image, image_class, query, key, value, log_total, grad_mixed):
     images, cells, width = query.shape
-    rows = per_image((cells, width))
+    own = lambda shape: pl.BlockSpec((1,) + shape, lambda *_: (image,) + (0,) * len(shape))
+    rows = own((cells, width))
     return pl.pallas_call(
-        attend_backward_kernel,
+        lambda *refs: attend_backward_kernel(*refs, image=image),
         out_shape=(
-            jax.ShapeDtypeStruct((images, cells, 3 * width), bf16),
-            jax.ShapeDtypeStruct((16, width), f32),
+            jax.ShapeDtypeStruct((1, cells, 3 * width), bf16),
+            jax.ShapeDtypeStruct((2, 8, width), f32),
         ),
         grid_spec=pltpu.PrefetchScalarGridSpec(
             num_scalar_prefetch=1,
-            grid=(images,),
-            in_specs=[
-                rows,
-                rows,
-                rows,
-                per_image((HEADS, 8, cells)),
-                rows,
-                whole(sums_expand.shape),
-                whole(sums_shrink.shape),
-                whole(sums_mix.shape),
-            ],
-            out_specs=[per_image((cells, 3 * width)), whole((16, width))],
-            scratch_shapes=[pltpu.VMEM((2, 8, width), f32)],
+            grid=(1,),
+            in_specs=[rows, rows, rows, own((HEADS, 8, cells)), rows],
+            out_specs=[whole((1, cells, 3 * width)), whole((2, 8, width))],
         ),
         compiler_params=pltpu.CompilerParams(vmem_limit_bytes=62 * MIB),
-        cost_estimate=cost(40 * images * cells * cells * width, 12 * MIB),
+        cost_estimate=cost(40 * cells * cells * width, 6 * MIB),
         name="attend_backward",
-    )(image_class, query, key, value, log_total, grad_mixed, sums_expand, sums_shrink, sums_mix)
+    )(image_class, query, key, value, log_total, grad_mixed)
 
 
 def joint_backward_kernel(
     core_ref,
+    normed_ref,
+    grad_joint0_ref,
+    grad_joint1_ref,
+    joint_ref,
+    gain1_ref,
     tokens_ref,
-    normed_ref,
     mixed_ref,
     grad_resid_ref,
-    grad_joint_ref,
-    gain1_ref,
-    joint_ref,
+    feed_expand_ref,
+    feed_shrink_ref,
+    mix_sums_ref,
+    attend_sums0_ref,
+    attend_sums1_ref,
     grad_tokens_ref,
     mine_ref,
     other_ref,
-    sums,
-    resid_low,
-    joint_total,
-    mix_total,
+    sums_ref,
+    vectors_ref,
+    grad_joint,
+    weight_total,
+    grad_normed,
+    tokens,
+    mixed,
+    grad_resid,
+    sems,
 ):
-    image = pl.program_id(0)
+    step = pl.program_id(0)
     last = pl.num_programs(0) - 1
-    cells, width = tokens_ref.shape[1:]
-    chunk = 96
-    block = 256
-
-    @pl.when(image == 0)
+    images, cells, width = normed_ref.shape
+    rows = images * cells
+    loads = [
+        pltpu.make_async_copy(mixed_ref, mixed, sems.at[0]),
+        pltpu.make_async_copy(grad_resid_ref, grad_resid, sems.at[1]),
+        pltpu.make_async_copy(tokens_ref, tokens, sems.at[2]),
+    ]
+
+    @pl.when(step == 0)
     def _():
-        sums[...] = jnp.zeros_like(sums)
-        joint_total[...] = jnp.zeros_like(joint_total)
-        mix_total[...] = jnp.zeros_like(mix_total)
-
-    @pl.loop(0, 3 * width // block)
-    def _(step):
-        here = rows_at(step, block)
-        joint_total[:, here] += dot_tn(normed_ref[0], grad_joint_ref[0, :, here])
-
-    @pl.loop(0, cells // chunk)
-    def _(step):
-        rows = rows_at(step, chunk)
-        normal, row_scale = row_norm(tokens_ref[0, rows, :].astype(f32))
-        grad = dot_nt(grad_joint_ref[0, rows, :], joint_ref[...])
-        sums[0] += fold(grad * normal)
-        sums[1] += fold(grad)
-        back = row_norm_back(grad, normal, row_scale, line(gain1_ref))
-        grad_resid = grad_resid_ref[0, rows, :]
-        resid_low[rows, :] = grad_resid.astype(bf16)
-        grad_tokens_ref[0, rows, :] = (grad_resid + back).astype(bf16)
-
-    mix_total[...] += dot_tn(mixed_ref[0], resid_low[...])
-
-    @pl.when(image == last)
+        for copy in loads:
+            copy.start()
+        grad_normed[...] = jnp.zeros_like(grad_normed)
+        vectors_ref[...] = jnp.zeros_like(vectors_ref)
+        for k in range(feed_expand_ref.shape[1] // width):
+            vectors_ref[k : k + 1, :] = total(feed_expand_ref[:, k * width : (k + 1) * width])
+        vectors_ref[4:5, :] = total(feed_shrink_ref[...])
+        for k in range(3):
+            vectors_ref[5 + k : 6 + k, :] = total(mix_sums_ref[k])
+        for k in range(2):
+            vectors_ref[8 + k : 9 + k, :] = total(attend_sums0_ref[k] + attend_sums1_ref[k])
+
+    @pl.when(step < last)
     def _():
-        core = core_ref[0]
-        size = width // (2 * PAIRS)
-        parts = size // 8
-        for pair in range(PAIRS):
-            for ref, side in ((mine_ref, core), (other_ref, 1 - core)):
-                at = pl.ds(pl.multiple_of((2 * pair + side) * size, 8), size)
-                for k in range(3):
-                    ref[pair, k * parts : (k + 1) * parts] = sections_of(
-                        joint_total[at, k * width : (k + 1) * width]
-                    )
-                ref[pair, 3 * parts : 4 * parts] = sections_of(mix_total[at, :])
+        grad_joint[0:cells, :] = grad_joint0_ref[0]
+        grad_joint[cells:rows, :] = grad_joint1_ref[0]
+        weight_total[...] = dot_tn(normed_ref[...].reshape(rows, width), grad_joint[...])
+        grad_normed[...] += dot_nt(grad_joint[...], joint_ref[...])
+
+    @pl.when(step == last)
+    def _():
+        for copy in loads:
+            copy.wait()
+        low = grad_resid[...].reshape(rows, width).astype(bf16)
+        weight_total[...] = dot_tn(mixed[...].reshape(rows, width), low)
+        sums = [jnp.zeros((8, width), f32)] * 2
+        for image in range(images):
+            at = slice(image * cells, (image + 1) * cells)
+            normal, row_scale = row_norm(tokens[image].astype(f32))
+            grad = grad_normed[at, :]
+            sums[0] = sums[0] + fold(grad * normal)
+            sums[1] = sums[1] + fold(grad)
+            back = row_norm_back(grad, normal, row_scale, line(gain1_ref))
+            grad_tokens_ref[image] = (grad_resid[image] + back).astype(bf16)
+        sums_ref[0] = sums[0]
+        sums_ref[1] = sums[1]
+
+    store_pairs(weight_total, mine_ref, other_ref, core_ref[0])
 
 
 def joint_backward(
-    core, tokens, normed, mixed, grad_resid, grad_joint, gain1, joint
+    core,
+    tokens,
+    normed,
+    mixed,
+    grad_resid,
+    grad_joint0,
+    grad_joint1,
+    gain1,
+    joint,
+    sums_expand,
+    sums_shrink,
+    sums_mix,
+    sums_attend0,
+    sums_attend1,
 ):
     images, cells, width = tokens.shape
-    rows = per_image((cells, width))
     size = width // (2 * PAIRS)
     half = (PAIRS, 4 * size // 8, 8, width)
+    half_spec = pl.BlockSpec((PAIRS, size // 8, 8, width), lambda step, *_: (0, step, 0, 0))
+    column = lambda step, *_: (0, 0, jnp.minimum(step, 2))
+    anywhere = pl.BlockSpec(memory_space=pl.ANY)
     return pl.pallas_call(
         joint_backward_kernel,
         out_shape=(
@@ -902,24 +943,41 @@
             jax.ShapeDtypeStruct(half, bf16),
             jax.ShapeDtypeStruct(half, bf16),
             jax.ShapeDtypeStruct((2, 8, width), f32),
+            jax.ShapeDtypeStruct((16, width), f32),
         ),
         grid_spec=pltpu.PrefetchScalarGridSpec(
             num_scalar_prefetch=1,
-            grid=(images,),
+            grid=(4,),
             in_specs=[
-                rows,
-                rows,
-                rows,
-                rows,
-                per_image((cells, 3 * width)),
+                whole((images, cells, width)),
+                pl.BlockSpec((1, cells, width), column),
+                pl.BlockSpec((1, cells, width), column),
+                pl.BlockSpec((width, width), lambda step, *_: (0, jnp.minimum(step, 2))),
                 whole((width,)),
-                whole((width, 3 * width)),
+                anywhere,
+                anywhere,
+                anywhere,
+                whole(sums_expand.shape),
+                whole(sums_shrink.shape),
+                whole(sums_mix.shape),
+                whole(sums_attend0.shape),
+                whole(sums_attend1.shape),
             ],
-            out_specs=[rows, whole(half), whole(half), whole((2, 8, width))],
+            out_specs=[
+                whole((images, cells, width)),
+                half_spec,
+                half_spec,
+                whole((2, 8, width)),
+                whole((16, width)),
+            ],
             scratch_shapes=[
-                pltpu.VMEM((cells, width), bf16),
-                pltpu.VMEM((width, 3 * width), f32),
+                pltpu.VMEM((images * cells, width), bf16),
                 pltpu.VMEM((width, width), f32),
+                pltpu.VMEM((images * cells, width), f32),
+                pltpu.VMEM((images, cells, width), bf16),
+                pltpu.VMEM((images, cells, width), bf16),
+                pltpu.VMEM((images, cells, width), f32),
+                pltpu.SemaphoreType.DMA((3,)),
             ],
         ),
         compiler_params=pltpu.CompilerParams(vmem_limit_bytes=62 * MIB),
@@ -927,13 +985,19 @@
         name="joint_backward",
     )(
         core,
+        normed,
+        grad_joint0,
+        grad_joint1,
+        joint,
+        gain1,
         tokens,
-        normed,
         mixed,
         grad_resid,
-        grad_joint,
-        gain1,
-        joint,
+        sums_expand,
+        sums_shrink,
+        sums_mix,
+        sums_attend0,
+        sums_attend1,
     )
 
 
@@ -942,33 +1006,94 @@
     return [group_total(total(item) * gain, per_group) * inverse for item in sums]
 
 
+def embed_weights_kernel(
+    class_ref,
+    core_ref,
+    grad_tokens_ref,
+    stem_ref,
+    mine_ref,
+    other_ref,
+    sums_ref,
+    grad_masked,
+    weight_total,
+    position_total,
+):
+    images, cells, width = grad_tokens_ref.shape
+    channels = stem_ref.shape[2]
+    sums = jnp.zeros((8, width), f32)
+    position = jnp.zeros((cells, width), f32)
+    for image in range(images):
+        keep = spread_lanes(validity_mask(class_ref[image], cells), width)
+        grad = grad_tokens_ref[image].astype(f32) * keep
+        grad_masked[image * cells : (image + 1) * cells, :] = grad.astype(bf16)
+        sums = sums + fold(grad)
+        position = position + grad
+    sums_ref[...] = sums
+    grad_position = weight_total.at[pl.ds(0, cells)]
+    grad_position[...] = position
+    position_rows = cells // (2 * PAIRS)
+    position_total[...] = jnp.zeros_like(position_total)
+    for block in range(2 * PAIRS):
+        position_total[block, 0:position_rows, :] = grad_position[
+            block * position_rows : (block + 1) * position_rows, :
+        ]
+    weight_total[...] = dot_tn(stem_ref[...].reshape(images * cells, channels), grad_masked[...])
+    core = core_ref[0]
+    size = channels // (2 * PAIRS)
+    for pair in range(PAIRS):
+        for ref, side in ((mine_ref, core), (other_ref, 1 - core)):
+            block = 2 * pair + side
+            at = pl.ds(pl.multiple_of(block * size, 8), size)
+            ref[pair, 0 : size // 8] = sections_of(weight_total[at, :])
+            ref[pair, size // 8 :] = sections_of(position_total[block])
+
+
+def embed_weights(image_class, core, grad_tokens, stem):
+    images, cells, width = grad_tokens.shape
+    channels = stem.shape[2]
+    position_rows = -(-cells // (2 * PAIRS) // 8) * 8
+    half = (PAIRS, (channels // (2 * PAIRS) + position_rows) // 8, 8, width)
+    return pl.pallas_call(
+        embed_weights_kernel,
+        out_shape=(
+            jax.ShapeDtypeStruct(half, bf16),
+            jax.ShapeDtypeStruct(half, bf16),
+            jax.ShapeDtypeStruct((8, width), f32),
+        ),
+        grid_spec=pltpu.PrefetchScalarGridSpec(
+            num_scalar_prefetch=2,
+            grid=(1,),
+            in_specs=[whole(grad_tokens.shape), whole(stem.shape)],
+            out_specs=[whole(half), whole(half), whole((8, width))],
+            scratch_shapes=[
+                pltpu.VMEM((images * cells, width), bf16),
+                pltpu.VMEM((channels, width), f32),
+                pltpu.VMEM((2 * PAIRS, position_rows, width), f32),
+            ],
+        ),
+        compiler_params=pltpu.CompilerParams(vmem_limit_bytes=62 * MIB),
+        cost_estimate=cost(8_000_000_000, 8 * MIB),
+        name="embed_weights",
+    )(image_class, core, grad_tokens, stem)
+
+
 def embed_backward_kernel(
     class_ref,
-    core_ref,
     grad_tokens_ref,
     x_ref,
     third_ref,
     stat3_ref,
-    stem_ref,
     gain3_ref,
     bias3_ref,
     embed_ref,
     grad_inner_ref,
     grad_third_ref,
-    mine_ref,
-    other_ref,
-    sums_embed_ref,
     sums3_ref,
     mask,
-    embed_total,
-    grad_position,
-    position_total,
 ):
     image = pl.program_id(0)
-    last = pl.num_programs(0) - 1
     cells, channels = x_ref.shape[1:]
-    width = embed_ref.shape[1]
-    chunk = 96
+    chunk = cells
     steps = cells // chunk
     image_class = class_ref[image]
     mask[...] = validity_mask(image_class, cells)
@@ -976,17 +1101,8 @@
 
     @pl.when(image == 0)
     def _():
-        for ref in (grad_position, sums_embed_ref, sums3_ref, embed_total):
-            ref[...] = jnp.zeros_like(ref)
-
-    @pl.loop(0, steps)
-    def _(step):
-        rows = rows_at(step, chunk)
-        grad = grad_tokens_ref[0, rows, :].astype(f32) * spread_lanes(mask[rows, :], width)
-        grad_position[rows, :] += grad
-        sums_embed_ref[...] += fold(grad)
-
-    embed_total[...] += dot_tn(stem_ref[0], grad_tokens_ref[0])
+        sums3_ref[...] = jnp.zeros_like(sums3_ref)
+
     centre, scale = stat3_ref[0, 0:1, :], stat3_ref[0, 1:2, :]
     gain = line(gain3_ref)
 
@@ -1018,48 +1134,25 @@
         grad = (grad_inner_ref[0, rows, :] * outer - mean - normal * cross) * keep
         grad_third_ref[0, rows, :] = grad.astype(bf16)
 
-    @pl.when(image == last)
-    def _():
-        core = core_ref[0]
-        position_rows = cells // (2 * PAIRS)
-        position_total[...] = jnp.zeros_like(position_total)
-        for block in range(2 * PAIRS):
-            position_total[block, 0:position_rows, :] = grad_position[
-                block * position_rows : (block + 1) * position_rows, :
-            ]
-        size = channels // (2 * PAIRS)
-        for pair in range(PAIRS):
-            for ref, side in ((mine_ref, core), (other_ref, 1 - core)):
-                block = 2 * pair + side
-                at = pl.ds(pl.multiple_of(block * size, 8), size)
-                ref[pair, 0 : size // 8] = sections_of(embed_total[at, :])
-                ref[pair, size // 8 :] = sections_of(position_total[block])
-
-
-def embed_backward(image_class, core, grad_tokens, x, third, stat3, stem, gain3, bias3, embed):
+
+def embed_backward(image_class, grad_tokens, x, third, stat3, gain3, bias3, embed):
     images, cells, channels = x.shape
     width = embed.shape[1]
-    position_rows = -(-cells // (2 * PAIRS) // 8) * 8
-    half = (PAIRS, (channels // (2 * PAIRS) + position_rows) // 8, 8, width)
     return pl.pallas_call(
         embed_backward_kernel,
         out_shape=(
             jax.ShapeDtypeStruct((images, cells, channels), f32),
             jax.ShapeDtypeStruct((images, cells, channels), bf16),
-            jax.ShapeDtypeStruct(half, bf16),
-            jax.ShapeDtypeStruct(half, bf16),
-            jax.ShapeDtypeStruct((8, width), f32),
             jax.ShapeDtypeStruct((2, 8, channels), f32),
         ),
         grid_spec=pltpu.PrefetchScalarGridSpec(
-            num_scalar_prefetch=2,
+            num_scalar_prefetch=1,
             grid=(images,),
             in_specs=[
                 per_image((cells, width)),
                 per_image((cells, channels)),
                 per_image((cells, channels)),
                 per_image((8, channels)),
-                per_image((cells, channels)),
                 whole((channels,)),
                 whole((channels,)),
                 whole((channels, width)),
@@ -1067,22 +1160,16 @@
             out_specs=[
                 per_image((cells, channels)),
                 per_image((cells, channels)),
-                whole(half),
-                whole(half),
-                whole((8, width)),
                 whole((2, 8, channels)),
             ],
             scratch_shapes=[
                 pltpu.VMEM((cells, LANES), f32),
-                pltpu.VMEM((channels, width), f32),
-                pltpu.VMEM((cells, width), f32),
-                pltpu.VMEM((2 * PAIRS, position_rows, width), f32),
             ],
         ),
         compiler_params=pltpu.CompilerParams(vmem_limit_bytes=62 * MIB),
         cost_estimate=cost(20_000_000_000, 30 * MIB),
         name="embed_backward",
-    )(image_class, core, grad_tokens, x, third, stat3, stem, gain3, bias3, embed)
+    )(image_class, grad_tokens, x, third, stat3, gain3, bias3, embed)
 
 
 def convs_backward_kernel(
@@ -1107,9 +1194,11 @@
     sums_embed_ref,
     sums3_ref,
     sums_attn_ref,
+    arrived_ref,
     grad_first_ref,
     mine_ref,
     other_ref,
+    output_ref,
     vectors,
     sums1,
     sums2,
@@ -1125,6 +1214,7 @@
 ):
     image = pl.program_id(0)
     last = pl.num_programs(0) - 1
+    output_ref[...] = arrived_ref[...]
     cells, channels = x_ref.shape[1:]
     width = sums_embed_ref.shape[1]
     middle = first_ref.shape[2]
@@ -1245,6 +1335,7 @@
     sums_embed,
     sums3,
     sums_attn,
+    arrived,
 ):
     images, cells, channels = x.shape
     middle = first.shape[2]
@@ -1252,12 +1343,16 @@
     row = lambda size: whole((size,))
     conv_rows = channels // (2 * PAIRS) + 9 * middle // (2 * PAIRS) + middle // (2 * PAIRS) * (channels // middle)
     half = (PAIRS + 1, conv_rows // 8, 8, middle)
+    slot_spec = pl.BlockSpec(
+        (arrived.shape[0] // images,) + arrived.shape[1:], lambda image, *_: (image, 0, 0)
+    )
     return pl.pallas_call(
         convs_backward_kernel,
         out_shape=(
             jax.ShapeDtypeStruct((images, cells, middle), bf16),
             jax.ShapeDtypeStruct(half, bf16),
             jax.ShapeDtypeStruct(half, bf16),
+            jax.ShapeDtypeStruct(arrived.shape, bf16),
         ),
         grid_spec=pltpu.PrefetchScalarGridSpec(
             num_scalar_prefetch=2,
@@ -1282,11 +1377,13 @@
                 whole((8, width)),
                 whole((2, 8, channels)),
                 whole((2, 8, width)),
+                slot_spec,
             ],
             out_specs=[
                 per_image((cells, middle)),
                 whole(half),
                 whole(half),
+                slot_spec,
             ],
             scratch_shapes=[
                 pltpu.VMEM((VECTORS * 8, middle), f32),
@@ -1321,6 +1418,7 @@
         sums_embed,
         sums3,
         sums_attn,
+        arrived,
     )
 
 
@@ -1396,6 +1494,74 @@
     )(plane, *mines, *others)
 
 
+def split_two_kernel(bits_ref, *refs, modes):
+    count = len(modes)
+    outs = refs[2 * count :]
+    for k, (inner, bit) in enumerate(modes):
+        left, right = refs[2 * k], refs[2 * k + 1]
+        for at in range(left.shape[0] // 2):
+            base = at // inner * 2 * inner + at % inner
+            for q in range(2):
+                here = base + inner * lax.bitwise_xor(bits_ref[bit], q)
+                summed = left[here].astype(f32) + right[here].astype(f32)
+                outs[2 * k + q][at] = summed.astype(bf16)
+
+
+def split_two(bits, pairs, modes, steps):
+    flat = [item for pair in pairs for item in pair]
+    spec = lambda shape: pl.BlockSpec(
+        (shape[0] // steps,) + shape[1:], lambda step, *_: (step, 0, 0, 0)
+    )
+    half = lambda item: (item.shape[0] // 2,) + item.shape[1:]
+    outs = [jax.ShapeDtypeStruct(half(pair[0]), bf16) for pair in pairs for _ in range(2)]
+    size = sum(item.size for item in flat)
+    return pl.pallas_call(
+        lambda *refs: split_two_kernel(*refs, modes=modes),
+        out_shape=outs,
+        grid_spec=pltpu.PrefetchScalarGridSpec(
+            num_scalar_prefetch=1,
+            grid=(steps,),
+            in_specs=[spec(item.shape) for item in flat],
+            out_specs=[spec(item.shape) for item in outs],
+        ),
+        compiler_params=pltpu.CompilerParams(vmem_limit_bytes=62 * MIB),
+        cost_estimate=cost(size, 3 * size),
+        name="split_two",
+    )(bits, *flat)
+
+
+def split_depth_kernel(depth_ref, *refs):
+    outs = refs[-4:]
+    start = 0
+    for k in range(len(refs) // 2 - 2):
+        left, right = refs[2 * k], refs[2 * k + 1]
+        size = left.shape[1]
+        for q in range(4):
+            at = lax.bitwise_xor(depth_ref[0], q)
+            summed = left[at].astype(f32) + right[at].astype(f32)
+            outs[q][start : start + size] = summed.astype(bf16)
+        start += size
+
+
+def split_depth(depth, pairs):
+    flat = [item for pair in pairs for item in pair]
+    shape = (sum(pair[0].shape[1] for pair in pairs),) + flat[0].shape[2:]
+    size = sum(item.size for item in flat)
+    return pl.pallas_call(
+        split_depth_kernel,
+        out_shape=[jax.ShapeDtypeStruct(shape, bf16)] * 4,
+        grid_spec=pltpu.PrefetchScalarGridSpec(
+            num_scalar_prefetch=1,
+            grid=(1,),
+            in_specs=[whole(item.shape) for item in flat],
+            out_specs=[whole(shape)] * 4,
+        ),
+        compiler_params=pltpu.CompilerParams(vmem_limit_bytes=62 * MIB),
+        cost_estimate=cost(size, 3 * size),
+        name="split_depth",
+    )(depth, *flat)
+
+
 def four(values):
     return (values[0] + values[1]) + (values[2] + values[3])
 
@@ -1499,6 +1665,7 @@
         self.devices = devices
         self.plane = ((index // 2) % 4).astype(jnp.int32).reshape(1)
         self.depth = (index // 8).astype(jnp.int32).reshape(1)
+        self.bits = jnp.stack([index // 4 % 2, index // 2 % 2]).astype(jnp.int32)
 
     def spread(self, parts, unit):
         return [parts[0]] + [permuted(parts[q], q * unit, self.devices) for q in (1, 2, 3)]
@@ -1509,6 +1676,13 @@
     def end_core(self, started, extra=0):
         return combine_core(self.plane, *started, extra)
 
+    def halves(self, pairs, modes, distances, steps):
+        outs = split_two(self.bits, pairs, modes, steps)
+        return [
+            (outs[2 * k], permuted(outs[2 * k + 1], distance, self.devices))
+            for k, distance in enumerate(distances)
+        ]
+
     def start_plane(self, parts):
         return self.spread(parts, 2)
 
@@ -1525,8 +1699,8 @@
 
 def ahead(value, others):
     leaves, tree = jax.tree.flatten(others)
-    held = lax.optimization_barrier((value, *leaves))
-    return jax.tree.unflatten(tree, held[1:])
+    held = lax.optimization_barrier((value, leaves))
+    return jax.tree.unflatten(tree, held[1])
 
 
 def octets(out, rows, columns, width, offset=0):
@@ -1620,13 +1794,15 @@
     )
     (
         outgoing,
-        grad_normed_two,
+        grad_resid,
+        grad_mixed,
         shrink_mine,
         shrink_other,
         expand_mine,
         expand_other,
         sums_expand,
         sums_shrink,
+        sums_mix,
     ) = feed(
         image_class,
         mine,
@@ -1638,49 +1814,78 @@
         expand_bias,
         shrink_weight,
         shrink_bias,
+        mlp_gain,
+        mix_weight,
     )
     sums = Sums(index, devices)
     if staged:
         feed_core = sums.start_core([shrink_mine, expand_mine], [shrink_other, expand_other])
     arrived = lax.all_to_all(outgoing, "section", split_axis=0, concat_axis=0, tiled=True)
-    grad_resid, grad_mixed, sums_mix = mix_backward(
-        image_class, mine, resid, received, grad_normed_two, mix_weight, mlp_gain
+    grad_joint0, sums_attend0 = attend_backward(
+        0, image_class, query, key, value, log_total, grad_mixed
     )
     if staged:
-        feed_core = ahead(grad_resid, feed_core)
-        feed_plane = sums.start_plane(sums.end_core(feed_core))
-        grad_mixed = after(grad_mixed, feed_plane[0])
-    grad_joint, vectors_block = attend_backward(
-        image_class, query, key, value, log_total, grad_mixed, sums_expand, sums_shrink, sums_mix
+        feed_core = ahead(grad_joint0, feed_core)
+        feed_half = sums.halves(
+            list(zip(*feed_core)), ((2, 0), (1, 1)), (4, 2), 4
+        )
+        grad_mixed = after(grad_mixed, feed_half[0][0])
+    grad_joint1, sums_attend1 = attend_backward(
+        1, image_class, query, key, value, log_total, grad_mixed
+    )
+    grad_tokens, joint_mine, joint_other, sums_attn, vectors_block = joint_backward(
+        core,
+        tokens,
+        normed,
+        mixed,
+        grad_resid,
+        grad_joint0,
+        grad_joint1,
+        attn_gain,
+        joint_weight,
+        sums_expand,
+        sums_shrink,
+        sums_mix,
+        sums_attend0,
+        sums_attend1,
     )
     gathered = lax.all_gather(vectors_block, BOTH)
-    grad_tokens, joint_mine, joint_other, sums_attn = joint_backward(
-        core, tokens, normed, mixed, grad_resid, grad_joint, attn_gain, joint_weight
-    )
     if staged:
+        feed_half, arrived, joint_other = ahead(grad_tokens, (feed_half, arrived, joint_other))
+        joint_other = after(joint_other, *feed_half[0], *feed_half[1], arrived)
         joint_core = sums.start_core([joint_mine], [joint_other])
-        feed_plane, arrived = ahead(grad_tokens, (feed_plane, arrived))
-        feed_depth = sums.start_depth(sums.end_plane(feed_plane))
-        grad_tokens = after(grad_tokens, feed_depth[0], arrived)
-    block_output = arrived[None]
-    grad_inner, grad_third, embed_mine, embed_other, sums_embed, sums3 = embed_backward(
+        feed_quarter = sums.halves(feed_half, ((1, 1), (1, 0)), (2, 4), 1)
+        grad_tokens = after(grad_tokens, feed_quarter[0][0])
+    embed_mine, embed_other, sums_embed = embed_weights(image_class, core, grad_tokens, stem)
+    if staged:
+        joint_core, feed_quarter, grad_tokens = ahead(
+            embed_mine, (joint_core, feed_quarter, grad_tokens)
+        )
+        embed_core = sums.start_core([embed_mine], [embed_other])
+        joint_parts = sums.end_core(joint_core)
+        joint_plane = sums.start_plane(joint_parts)
+        feed_depth = split_depth(sums.depth, feed_quarter)
+        grad_tokens = after(grad_tokens, joint_plane[0], feed_depth[0])
+    grad_inner, grad_third, sums3 = embed_backward(
         image_class,
-        core,
         grad_tokens,
         stem_input,
         third,
         stat3,
-        stem,
         third_gain,
         third_bias,
         embed_weight,
     )
     if staged:
-        embed_core = sums.start_core([embed_mine], [embed_other])
-        joint_core, feed_depth = ahead(grad_third, (joint_core, feed_depth))
-        joint_plane = sums.start_plane(sums.end_core(joint_core))
-        grad_third = after(grad_third, joint_plane[0], *feed_depth)
-    grad_first, conv_mine, conv_other = convs_backward(
+        embed_core, joint_plane = ahead(grad_third, (embed_core, joint_plane))
+        feed_depth = after(feed_depth, *joint_plane)
+        feed_depth = sums.start_depth(feed_depth)
+        embed_half = sums.halves(
+            [(embed_core[0][0], embed_core[1][0])], ((2, 0),), (4,), 4
+        )
+        joint_parts = sums.end_plane(joint_plane)
+        grad_third = after(grad_third, joint_parts[0], embed_half[0][0])
+    grad_first, conv_mine, conv_other, block_output = convs_backward(
         image_class,
         core,
         grad_third,
@@ -1695,14 +1900,16 @@
         sums_embed,
         sums3,
         sums_attn,
+        arrived,
     )
+    block_output = block_output[None]
     if staged:
-        embed_core, joint_plane = ahead(grad_first, (embed_core, joint_plane))
-        conv_other = after(conv_other, *joint_plane)
+        feed_depth, embed_half = ahead(grad_first, (feed_depth, embed_half))
+        conv_other = after(conv_other, *feed_depth, *embed_half[0])
         conv_core = sums.start_core([conv_mine], [conv_other])
-        embed_plane = sums.start_plane(sums.end_core(embed_core))
-        joint_depth = sums.start_depth(sums.end_plane(joint_plane))
-        grad_first = after(grad_first, embed_plane[0], joint_depth[0])
+        embed_quarter = sums.halves(embed_half, ((1, 1),), (2,), 1)
+        joint_depth = sums.start_depth(joint_parts)
+        grad_first = after(grad_first, embed_quarter[0][0])
     input_grad = input_backward(image_class, grad_inner, grad_first, std_in)
 
     parts = 2 * PAIRS
@@ -1734,12 +1941,15 @@
     block_vectors = sum_vectors(gathered.reshape((-1,) + vectors_block.shape), block_lines)
     if staged:
         conv_plane = sums.start_plane(sums.end_core(conv_core, 1))
-        embed_depth = sums.start_depth(sums.end_plane(embed_plane))
-        conv_depth = sums.start_depth(sums.end_plane(conv_plane, 1))
+        embed_depth = sums.start_depth(split_depth(sums.depth, embed_quarter))
         (grad_shrink, grad_expand), _ = combine_depth(
             feed_depth, shrink_places + expand_places, feed_sizes, []
         )
         (grad_joint, grad_mix), _ = combine_depth(joint_depth, joint_places, joint_sizes, [])
+        conv_plane = ahead(
+            (input_grad, grad_shrink, grad_joint, block_vectors), conv_plane
+        )
+        conv_depth = sums.start_depth(sums.end_plane(conv_plane, 1))
         (grad_embed, grad_position), _ = combine_depth(embed_depth, embed_places, embed_sizes, [])
         (grad_in, grad_mid, grad_out), stem_vectors = combine_depth(
             conv_depth, conv_places, conv_sizes, stem_lines

time: 411 us -> 374 us (0.910)
  Pallas kernels: 313 us -> 260 us
  waiting for transfers between devices: 19.2 us -> 39.6 us
    ppermute x29, waiting for transfers between devices: 19.1 us -> 39.6 us  [permuted(): return lax.ppermute(item, BOTH, [(k, k ^ distance) for k in range(devices)])]
    pallas_call x1, Pallas kernels: 36.3 us -> 18.1 us  [joint_backward(): pl.pallas_call(joint_backward_kernel, out_shape=(jax.ShapeDtypeStruct((im...]
    pallas_call x2 -> x9, Pallas kernels: 48.1 us -> 65.2 us  [the longest x2 34.2 us: attend_backward(): pl.pallas_call(lambda *refs: attend_backward_kernel(*refs, image=image),...]
    pallas_call x1, Pallas kernels: 35.4 us -> 24.7 us  [stem_forward(): pl.pallas_call(stem_forward_kernel, out_shape=(jax.ShapeDtypeStruct((chan...]
    pallas_call x1, Pallas kernels: 43.4 us -> 32.8 us  [attend_forward(): pl.pallas_call(attend_forward_kernel, out_shape=(low, low, low, low, jax....]
    pallas_call x4 -> x2, Pallas kernels: 17.4 us -> 7.31 us  [combine_core(): pl.pallas_call(lambda *refs: combine_core_kernel(*refs, arrays=arrays, ex...]
    pallas_call x1, Pallas kernels: 24 us -> 15 us  [embed_backward(): pl.pallas_call(embed_backward_kernel, out_shape=(jax.ShapeDtypeStruct((im...]
    pallas_call x1, Pallas kernels: 63.2 us -> 56.4 us  [feed(): pl.pallas_call(feed_kernel, out_shape=(jax.ShapeDtypeStruct((slots, cells...]
  transfers between devices with their start and end apart: 32 -> 32, of which waited for: 6 -> 7; matrix products, arithmetic and copies ran while one was open for 0% -> 0% of each run, Pallas kernels for 62% -> 55%
where the time goes in v3:
time: 374 us; the launch traced here: 367 us
  Pallas kernels  260 us (70%)
  starting transfers between devices  45.9 us (12%)
  waiting for transfers between devices  39.6 us (11%)
  between operations  14.6 us (4%)
  local copies, waits for them, and re-layouts  5.41 us (1%)
    pallas_call x1, Pallas kernels, feed(): pl.pallas_call(feed_kernel, out_shape=(jax.ShapeDtypeStruct((slots, cells...  56.4 us
    ppermute x29, waiting for transfers between devices, permuted(): return lax.ppermute(item, BOTH, [(k, k ^ distance) for k in range(devices)])  39.6 us
    ppermute x29, starting transfers between devices, permuted(): return lax.ppermute(item, BOTH, [(k, k ^ distance) for k in range(devices)])  36.4 us
    pallas_call x2, Pallas kernels, attend_backward(): pl.pallas_call(lambda *refs: attend_backward_kernel(*refs, image=image),...  34.2 us
    pallas_call x1, Pallas kernels, attend_forward(): pl.pallas_call(attend_forward_kernel, out_shape=(low, low, low, low, jax....  32.8 us
    pallas_call x1, Pallas kernels, stem_forward(): pl.pallas_call(stem_forward_kernel, out_shape=(jax.ShapeDtypeStruct((chan...  24.7 us
    pallas_call x1, Pallas kernels, convs_backward(): pl.pallas_call(convs_backward_kernel, out_shape=(jax.ShapeDtypeStruct((im...  21.4 us
    pallas_call x4, Pallas kernels, split_two(): pl.pallas_call(lambda *refs: split_two_kernel(*refs, modes=modes), out_sh...  19.3 us
  transfers between devices with their start and end apart: 32, of which 7 were waited for; matrix products, arithmetic and copies ran while one was open for 0% of the time, Pallas kernels for 55%

profile of v3, /device:TPU:0, one launch (start us, length us, event | category | flops | bytes accessed | tf_op | source)
XLA Modules:
  0.0 366.6 jit_solution(12323957920129794261)
XLA Ops:
  7.2 4.8 %all-to-all-start = ((bf16[4,576,768]{2,1,0:T(8,128)(2,1)}), bf16[4,576,768]{2,1,0:T(8,128)(2,1)}, u32[]{:S(2)}, u32[]{:S(2)}) async-start(bf16[4,576,768]{2,1,0:T(8,128)(2,1)} %bitcast.20), calls=%async_computation | async-start | bytes 7077888 | tf_op jit(solution)/shard_map/all_to_all | solution.py:1776
  12.1 0.5 dynamic-slice_bitcast_fusion.mine_ref
  12.6 24.7 %stem_forward.1 = (bf16[1024,256]{1,0:T(8,128)(2,1)}, bf16[2304,256]{1,0:T(8,128)(2,1)}, bf16[256,1024]{1,0:T(8,128)(2,1)}, f32[2,576,256]{2,1,0:T(8,128)}, f32[...) custom-call(s32[2]{0:T(128)} %class_ref.13, ...), custom_call_target="tpu_custom_call" | custom-call | flops 24999999488 | bytes 31457280 | tf_op jit(solution)/shard_map/stem_forward/pallas_call | solution.py:302
  37.3 32.8 %attend_forward.1 = (bf16[2,576,768]{2,1,0:T(8,128)(2,1)}, bf16[2,576,768]{2,1,0:T(8,128)(2,1)}, bf16[2,576,768]{2,1,0:T(8,128)(2,1)}, bf16[2,576,768]{2,1,0:T(8...) custom-call(s32[2]{0:T(128)} %class_ref.13, ...), custom_call_target="tpu_custom_call" | custom-call | flops 35000000512 | bytes 31457280 | tf_op jit(solution)/shard_map/attend_forward/pallas_call | solution.py:462
  70.1 56.4 %feed.1 = (bf16[4,576,768]{2,1,0:T(8,128)(2,1)}, f32[2,576,768]{2,1,0:T(8,128)}, bf16[2,576,768]{2,1,0:T(8,128)(2,1)}, bf16[16,12,8,768]{3,2,1,0:T(8,128)(2,1)},...) custom-call(s32[2]{0:T(128)} %class_ref.13, ...), custom_call_target="tpu_custom_call" | custom-call | flops 38050725888 | bytes 41943040 | tf_op jit(solution)/shard_map/feed/pallas_call | solution.py:677
  126.5 0.5 collective-permute-start
  127.0 0.6 pad_add_fusion.refs_0_
  127.6 4.7 %all-to-all-start.1 = ((bf16[4,576,768]{2,1,0:T(8,128)(2,1)}), bf16[4,576,768]{2,1,0:T(8,128)(2,1)}, u32[]{:S(2)}, u32[]{:S(2)}) async-start(bf16[4,576,768]{2,1,0:T(8,128)(2,1)} %get-tuple-element.212), calls=%async_computation.1 | async-start | bytes 7077888 | tf_op jit(solution)/shard_map/all_to_all | solution.py:1823
  132.4 17.0 %attend_backward.2 = (bf16[1,576,2304]{2,1,0:T(8,128)(2,1)}, f32[2,8,768]{2,1,0:T(8,128)}) custom-call(s32[2]{0:T(128)} %class_ref.13, bf16[2,576,768]{2,1,0:T(8,128)(2,1)} %get-tuple-element.182.refs_1_, bf16[2,576,768]{2,1,0:T(8,128)(2,1)} %get-tuple-element.183.refs_2_, bf16[2,576,768]{2,1,0:T(8,128)(2,1)} %get-tuple-element.184.refs_3_, ...), custom_call_target="tpu_custom_call" | custom-call | flops 10192158720 | bytes 6291456 | tf_op jit(solution)/shard_map/attend_backward/pallas_call | solution.py:819
  149.4 6.9 %split_two.4 = (bf16[8,12,8,768]{3,2,1,0:T(8,128)(2,1)}, bf16[8,12,8,768]{3,2,1,0:T(8,128)(2,1)}, bf16[8,12,8,768]{3,2,1,0:T(8,128)(2,1)}, bf16[8,12,8,768]{3,2,1,0:T(8,128)(2,1)}) custom-call(s32[2]{0:T(128)} %pad_add_fusion.refs_0_, bf16[16,12,8,768]{3,2,1,0:T(8,128)(2,1)} %get-tuple-element.194.refs_1_, ...), custom_call_target="tpu_custom_call" | custom-call | flops 4718592 | bytes 14155776 | tf_op jit(solution)/shard_map/split_two/pallas_call | solution.py:1518
  156.3 2.9 collective-permute-start.2
  159.3 2.0 collective-permute-start.3
  161.3 17.2 %attend_backward.3 = (bf16[1,576,2304]{2,1,0:T(8,128)(2,1)}, f32[2,8,768]{2,1,0:T(8,128)}) custom-call(s32[2]{0:T(128)} %class_ref.13, bf16[2,576,768]{2,1,0:T(8,128)(2,1)} %get-tuple-element.182.refs_1_, bf16[2,576,768]{2,1,0:T(8,128)(2,1)} %get-tuple-element.183.refs_2_, bf16[2,576,768]{2,1,0:T(8,128)(2,1)} %get-tuple-element.184.refs_3_, ...), custom_call_target="tpu_custom_call" | custom-call | flops 10192158720 | bytes 6291456 | tf_op jit(solution)/shard_map/attend_backward/pallas_call | solution.py:819
  178.5 18.1 %joint_backward.1 = (bf16[2,576,768]{2,1,0:T(8,128)(2,1)}, bf16[16,12,8,768]{3,2,1,0:T(8,128)(2,1)}, bf16[16,12,8,768]{3,2,1,0:T(8,128)(2,1)}, f32[2,8,768]{2,1,0:T(8,128)}, f32[16,768]{1,0:T(8,128)}) custom-call(s32[1]{0:T(128)} %bitcast.core_ref, bf16[2,576,768]{2,1,0:T(8,128)(2,1)} %get-tuple-element.181.normed_ref, ...), custom_call_target="tpu_custom_call" | custom-call | flops 9512681472 | bytes 26214400 | tf_op jit(solution)/shard_map/joint_backward/pallas_call | solution.py:939
  196.7 3.1 collective-permute-done.3.refs_4_
  199.8 4.9 %split_two.5 = (bf16[4,12,8,768]{3,2,1,0:T(8,128)(2,1)}, bf16[4,12,8,768]{3,2,1,0:T(8,128)(2,1)}, bf16[4,12,8,768]{3,2,1,0:T(8,128)(2,1)}, bf16[4,12,8,768]{3,2,1,0:T(8,128)(2,1)}) custom-call(s32[2]{0:T(128)} %pad_add_fusion.refs_0_, bf16[8,12,8,768]{3,2,1,0:T(8,128)(2,1)} %get-tuple-element.214.refs_1_, bf16[8,12,8,768]{3,2,1,0:T(8,128)(2,1)} %copy-done.2, ...), custom_call_target="tpu_custom_call" | custom-call | flops 2359296 | bytes 7077888 | tf_op jit(solution)/shard_map/split_two/pallas_call | solution.py:1518
  204.7 2.4 collective-permute-start.6
  207.1 7.0 %embed_weights.1 = (bf16[16,7,8,768]{3,2,1,0:T(8,128)(2,1)}, bf16[16,7,8,768]{3,2,1,0:T(8,128)(2,1)}, f32[8,768]{1,0:T(8,128)}) custom-call(s32[2]{0:T(128)} %class_ref.13, s32[1]{0:T(128)} %bitcast.core_ref, bf16[2,576,768]{2,1,0:T(8,128)(2,1)} %get-tuple-element.238.grad_tokens_ref, bf16[2,576,1024]{2,1,0:T(8,128)(2,1)} %get-tuple-element.220.stem_ref), custom_call_target="tpu_custom_call" | custom-call | flops 8000000000 | bytes 8388608 | tf_op jit(solution)/shard_map/embed_weights/pallas_call | solution.py:1056
  214.2 6.9 %collective-permute-done.5.refs_1_ = bf16[4,12,8,768]{3,2,1,0:T(8,128)(2,1)S(1)} collective-permute-done((bf16[4,12,8,768]{3,2,1,0:T(8,128)(2,1)}, bf16[4,12,8,768]{3,2,1,0:T(8,128)(2,1)S(1)}, u32[]{:S(2)}, u32[]{:S(2)}) %collective-permute-start.5) | collective-permute-done | bytes 589856 | tf_op jit(solution)/shard_map/ppermute | solution.py:1660
  221.0 0.5 collective-permute-done.6.refs_3_
  221.5 4.4 %combine_core.2 = (bf16[4,12,8,768]{3,2,1,0:T(8,128)(2,1)}, bf16[4,12,8,768]{3,2,1,0:T(8,128)(2,1)}, bf16[4,12,8,768]{3,2,1,0:T(8,128)(2,1)}, bf16[4,12,8,768]{3,2,1,0:T(8,128)(2,1)}) custom-call(s32[1]{0:T(128)} %bitcast.6.refs_0_, bf16[16,12,8,768]{3,2,1,0:T(8,128)(2,1)} %get-tuple-element.230.refs_1_, bf16[16,12,8,768]{3,2,1,0:T(8,128)(2,1)} %collective-permute-done.4.refs_2_), custom_call_target="tpu_custom_call" | custom-call | flops 1179648 | bytes 7077888 | tf_op jit(solution)/shard_map/combine_core/pallas_call | solution.py:1482
  226.0 2.8 split_depth.2
  228.7 1.7 collective-permute-start.8
  230.4 1.7 collective-permute-start.9
  232.2 15.0 %embed_backward.1 = (f32[2,576,1024]{2,1,0:T(8,128)}, bf16[2,576,1024]{2,1,0:T(8,128)(2,1)}, f32[2,8,1024]{2,1,0:T(8,128)}) custom-call(s32[2]{0:T(128)} %class_ref.13, bf16[2,576,768]{2,1,0:T(8,128)(2,1)} %get-tuple-element.238.grad_tokens_ref, f32[2,576,1024]{2,1,0:T(8,128)} %x_ref.5, f32[2,576,1024]{2,1,0:T(8,128)} %get-tuple-element.239.third_ref, ...), custom_call_target="tpu_custom_call" | custom-call | flops 20000000000 | bytes 31457280 | tf_op jit(solution)/shard_map/embed_backward/pallas_call | solution.py:1141
  247.3 2.5 collective-permute-done.9.refs_3_
  249.8 11.0 %collective-permute-done.10.refs_4_ = bf16[4,12,8,768]{3,2,1,0:T(8,128)(2,1)} collective-permute-done((bf16[4,12,8,768]{3,2,1,0:T(8,128)(2,1)}, bf16[4,12,8,768]{3,2,1,0:T(8,128)(2,1)}, u32[]{:S(2)}, u32[]{:S(2)}) %collective-permute-start.10) | collective-permute-done | bytes 589856 | tf_op jit(solution)/shard_map/ppermute | solution.py:1660
  260.8 2.6 combine_plane.2
  263.4 1.8 collective-permute-start.11
  265.3 2.6 collective-permute-start.12
  267.9 4.5 %split_two.6 = (bf16[8,7,8,768]{3,2,1,0:T(8,128)(2,1)}, bf16[8,7,8,768]{3,2,1,0:T(8,128)(2,1)}) custom-call(s32[2]{0:T(128)} %pad_add_fusion.refs_0_, bf16[16,7,8,768]{3,2,1,0:T(8,128)(2,1)} %get-tuple-element.251.refs_1_, bf16[16,7,8,768]{3,2,1,0:T(8,128)(2,1)} %copy-done), custom_call_target="tpu_custom_call" | custom-call | flops 1376256 | bytes 4128768 | tf_op jit(solution)/shard_map/split_two/pallas_call | solution.py:1518
  272.4 1.7 collective-permute-start.14
  274.1 21.4 %convs_backward.1 = (bf16[2,576,256]{2,1,0:T(8,128)(2,1)}, bf16[17,17,8,256]{3,2,1,0:T(8,128)(2,1)}, bf16[17,17,8,256]{3,2,1,0:T(8,128)(2,1)}, bf16[4,576,768]{2,1,0:T(8,128)(2,1)}) custom-call(s32[2]{0:T(128)} %class_ref.13, s32[1]{0:T(128)} %bitcast.core_ref, bf16[2,576,1024]{2,1,0:T(8,128)(2,1)} %get-tuple-element.254.grad_third_ref, ...), custom_call_target="tpu_custom_call" | custom-call | flops 20000000000 | bytes 20971520 | tf_op jit(solution)/shard_map/convs_backward/pallas_call | solution.py:1349
  295.6 0.8 copy-done.3
  296.4 3.0 split_two.7
  299.4 1.2 collective-permute-start.25
  300.6 0.7 collective-permute-start.15
  301.3 1.0 copy-done.1
  302.3 2.9 combine_core.3
  305.2 0.8 collective-permute-start.19
  306.0 0.5 collective-permute-start.20
  306.6 2.1 collective-permute-start.21
  308.7 3.5 collective-permute-start.16
  312.2 2.0 collective-permute-start.17
  314.2 1.8 split_depth.3
  316.0 5.9 %collective-permute-done.16.refs_2_ = bf16[12,8,768]{2,1,0:T(8,128)(2,1)S(1)} collective-permute-done((bf16[12,8,768]{2,1,0:T(8,128)(2,1)}, bf16[12,8,768]{2,1,0:T(8,128)(2,1)S(1)}, u32[]{:S(2)}, u32[]{:S(2)}) %collective-permute-start.16) | collective-permute-done | bytes 147488 | tf_op jit(solution)/shard_map/ppermute | solution.py:1660
  322.0 2.1 sum_vectors.1
  324.2 0.7 copy-done.12
  324.8 1.9 combine_depth.5
  326.7 2.1 combine_depth.4
  328.8 5.4 %input_backward.1 = f32[2,576,1024]{2,1,0:T(8,128)} custom-call(s32[2]{0:T(128)} %class_ref.13, f32[2,576,1024]{2,1,0:T(8,128)} %get-tuple-element.266.grad_inner_ref, bf16[2,576,256]{2,1,0:T(8,128)(2,1)} %get-tuple-element.279.grad_first_ref, bf16[1024,256]{1,0:T(8,128)(2,1)} %get-tuple-element.259.std_in_ref), custom_call_target="tpu_custom_call" | custom-call | flops 603979776 | bytes 12582912 | tf_op jit(solution)/shard_map/input_backward/pallas_call | solution.py:1435
  334.2 0.7 copy-done.6
  334.9 0.2 copy-done.7
  335.2 2.1 combine_plane.3
  337.3 1.9 collective-permute-start.22
  339.2 1.5 collective-permute-start.23
  340.6 1.4 collective-permute-start.24
  342.0 2.0 collective-permute-start.27
  344.1 1.0 collective-permute-start.28
  345.1 9.7 %collective-permute-done.27.refs_2_ = bf16[7,8,768]{2,1,0:T(8,128)(2,1)S(1)} collective-permute-done((bf16[7,8,768]{2,1,0:T(8,128)(2,1)S(1)}, bf16[7,8,768]{2,1,0:T(8,128)(2,1)S(1)}, u32[]{:S(2)}, u32[]{:S(2)}) %collective-permute-start.27) | collective-permute-done | bytes 86048 | tf_op jit(solution)/shard_map/ppermute | solution.py:1660
  354.8 0.6 copy-done.17
  355.4 1.7 combine_depth.7
  357.2 0.6 copy-done.13
  357.8 1.7 combine_depth.6
  (75 shorter events, 0.8 us)
Async XLA Ops:
  7.2 4.8 %copy-start.19 = (s32[8]{0:T(128)S(1)}, s32[8]{0:T(128)}, u32[]{:S(2)}) copy-start(s32[8]{0:T(128)} %param.31) | copy-start | bytes 100
  7.2 62.9 %all-to-all-start = ((bf16[4,576,768]{2,1,0:T(8,128)(2,1)}), bf16[4,576,768]{2,1,0:T(8,128)(2,1)}, u32[]{:S(2)}, u32[]{:S(2)}) async-start(bf16[4,576,768]{2,1,0:T(8,128)(2,1)} %bitcast.20), calls=%async_computation | async-start | bytes 7077888 | tf_op jit(solution)/shard_map/all_to_all | solution.py:1776
  126.5 23.0 %collective-permute-start = (bf16[16,12,8,768]{3,2,1,0:T(8,128)(2,1)}, bf16[16,12,8,768]{3,2,1,0:T(8,128)(2,1)}, u32[]{:S(2)}, u32[]{:S(2)}) collective-permute-start(bf16[16,12,8,768]{3,2,1,0:T(8,128)(2,1)} %get-tuple-element.192), channel_id=1, source_target_pairs={{0,1},{1,0},{2,3},{3,2},{4,5},{5,4},{6,7},{7,6},{8,9},{9,8},{10,11... | collective-permute-start | bytes 7077896 | tf_op jit(solution)/shard_map/ppermute | solution.py:1660
  127.0 22.5 %collective-permute-start.1 = (bf16[16,12,8,768]{3,2,1,0:T(8,128)(2,1)}, bf16[16,12,8,768]{3,2,1,0:T(8,128)(2,1)}, u32[]{:S(2)}, u32[]{:S(2)}) collective-permute-start(bf16[16,12,8,768]{3,2,1,0:T(8,128)(2,1)} %get-tuple-element.193), channel_id=1, source_target_pairs={{0,1},{1,0},{2,3},{3,2},{4,5},{5,4},{6,7},{7,6},{8,9},{9,8},{10,11... | collective-permute-start | bytes 7077896 | tf_op jit(solution)/shard_map/ppermute | solution.py:1660
  127.6 69.0 %all-to-all-start.1 = ((bf16[4,576,768]{2,1,0:T(8,128)(2,1)}), bf16[4,576,768]{2,1,0:T(8,128)(2,1)}, u32[]{:S(2)}, u32[]{:S(2)}) async-start(bf16[4,576,768]{2,1,0:T(8,128)(2,1)} %get-tuple-element.212), calls=%async_computation.1 | async-start | bytes 7077888 | tf_op jit(solution)/shard_map/all_to_all | solution.py:1823
  132.4 189.7 %all-gather.3.cloned.1.call-start = ((), (), s32[]{:S(2)}) async-start(), calls=%async_computation.2 | async-start | bytes 1622016 | tf_op jit(solution)/shard_map/all_gather | solution.py:1852
  156.3 40.3 %collective-permute-start.2 = (bf16[8,12,8,768]{3,2,1,0:T(8,128)(2,1)}, bf16[8,12,8,768]{3,2,1,0:T(8,128)(2,1)S(1)}, u32[]{:S(2)}, u32[]{:S(2)}) collective-permute-start(bf16[8,12,8,768]{3,2,1,0:T(8,128)(2,1)} %get-tuple-element.209), channel_id=1, source_target_pairs={{0,4},{1,5},{2,6},{3,7},{4,0},{5,1},{6,2},{7,3},{8,12},{9,13},{10,... | collective-permute-start | bytes 3538952 | tf_op jit(solution)/shard_map/ppermute | solution.py:1660
  159.3 40.5 %collective-permute-start.3 = (bf16[8,12,8,768]{3,2,1,0:T(8,128)(2,1)}, bf16[8,12,8,768]{3,2,1,0:T(8,128)(2,1)}, u32[]{:S(2)}, u32[]{:S(2)}) collective-permute-start(bf16[8,12,8,768]{3,2,1,0:T(8,128)(2,1)} %get-tuple-element.211), channel_id=1, source_target_pairs={{0,2},{1,3},{2,0},{3,1},{4,6},{5,7},{6,4},{7,5},{8,10},{9,11},{10,... | collective-permute-start | bytes 3538952 | tf_op jit(solution)/shard_map/ppermute | solution.py:1660
  196.6 3.2 copy-start.2
  199.8 21.7 %collective-permute-start.4 = (bf16[16,12,8,768]{3,2,1,0:T(8,128)(2,1)}, bf16[16,12,8,768]{3,2,1,0:T(8,128)(2,1)}, u32[]{:S(2)}, u32[]{:S(2)}) collective-permute-start(bf16[16,12,8,768]{3,2,1,0:T(8,128)(2,1)} %get-tuple-element.225), channel_id=1, source_target_pairs={{0,1},{1,0},{2,3},{3,2},{4,5},{5,4},{6,7},{7,6},{8,9},{9,8},{10,11... | collective-permute-start | bytes 7077896 | tf_op jit(solution)/shard_map/ppermute | solution.py:1660
  204.7 16.3 %collective-permute-start.5 = (bf16[4,12,8,768]{3,2,1,0:T(8,128)(2,1)}, bf16[4,12,8,768]{3,2,1,0:T(8,128)(2,1)S(1)}, u32[]{:S(2)}, u32[]{:S(2)}) collective-permute-start(bf16[4,12,8,768]{3,2,1,0:T(8,128)(2,1)} %get-tuple-element.226), channel_id=1, source_target_pairs={{0,2},{1,3},{2,0},{3,1},{4,6},{5,7},{6,4},{7,5},{8,10},{9,11},{10,... | collective-permute-start | bytes 1769480 | tf_op jit(solution)/shard_map/ppermute | solution.py:1660
  204.7 16.8 %collective-permute-start.6 = (bf16[4,12,8,768]{3,2,1,0:T(8,128)(2,1)}, bf16[4,12,8,768]{3,2,1,0:T(8,128)(2,1)}, u32[]{:S(2)}, u32[]{:S(2)}) collective-permute-start(bf16[4,12,8,768]{3,2,1,0:T(8,128)(2,1)} %get-tuple-element.228), channel_id=1, source_target_pairs={{0,4},{1,5},{2,6},{3,7},{4,0},{5,1},{6,2},{7,3},{8,12},{9,13},{10,... | collective-permute-start | bytes 1769480 | tf_op jit(solution)/shard_map/ppermute | solution.py:1660
  214.2 33.1 %collective-permute-start.7 = (bf16[16,7,8,768]{3,2,1,0:T(8,128)(2,1)}, bf16[16,7,8,768]{3,2,1,0:T(8,128)(2,1)S(1)}, u32[]{:S(2)}, u32[]{:S(2)}) collective-permute-start(bf16[16,7,8,768]{3,2,1,0:T(8,128)(2,1)} %get-tuple-element.242), channel_id=1, source_target_pairs={{0,1},{1,0},{2,3},{3,2},{4,5},{5,4},{6,7},{7,6},{8,9},{9,8},{10,11... | collective-permute-start | bytes 4128776 | tf_op jit(solution)/shard_map/ppermute | solution.py:1660
  221.0 4.9 %copy-start.4 = (bf16[4,12,8,768]{3,2,1,0:T(8,128)(2,1)}, bf16[4,12,8,768]{3,2,1,0:T(8,128)(2,1)S(1)}, u32[]{:S(2)}) copy-start(bf16[4,12,8,768]{3,2,1,0:T(8,128)(2,1)S(1)} %collective-permute-done.5.refs_1_) | copy-start | bytes 1769476
  228.7 18.5 %collective-permute-start.8 = (bf16[4,12,8,768]{3,2,1,0:T(8,128)(2,1)}, bf16[4,12,8,768]{3,2,1,0:T(8,128)(2,1)S(1)}, u32[]{:S(2)}, u32[]{:S(2)}) collective-permute-start(bf16[4,12,8,768]{3,2,1,0:T(8,128)(2,1)} %get-tuple-element.243), channel_id=1, source_target_pairs={{0,2},{1,3},{2,0},{3,1},{4,6},{5,7},{6,4},{7,5},{8,10},{9,11},{10,... | collective-permute-start | bytes 1769480 | tf_op jit(solution)/shard_map/ppermute | solution.py:1660
  230.4 19.4 %collective-permute-start.9 = (bf16[4,12,8,768]{3,2,1,0:T(8,128)(2,1)}, bf16[4,12,8,768]{3,2,1,0:T(8,128)(2,1)}, u32[]{:S(2)}, u32[]{:S(2)}) collective-permute-start(bf16[4,12,8,768]{3,2,1,0:T(8,128)(2,1)} %get-tuple-element.244), channel_id=1, source_target_pairs={{0,4},{1,5},{2,6},{3,7},{4,0},{5,1},{6,2},{7,3},{8,12},{9,13},{10,... | collective-permute-start | bytes 1769480 | tf_op jit(solution)/shard_map/ppermute | solution.py:1660
  232.2 28.6 %collective-permute-start.10 = (bf16[4,12,8,768]{3,2,1,0:T(8,128)(2,1)}, bf16[4,12,8,768]{3,2,1,0:T(8,128)(2,1)}, u32[]{:S(2)}, u32[]{:S(2)}) collective-permute-start(bf16[4,12,8,768]{3,2,1,0:T(8,128)(2,1)} %get-tuple-element.245), channel_id=1, source_target_pairs={{0,6},{1,7},{2,4},{3,5},{4,2},{5,3},{6,0},{7,1},{8,14},{9,15},{10,... | collective-permute-start | bytes 1769480 | tf_op jit(solution)/shard_map/ppermute | solution.py:1660
  247.2 20.6 %copy-start = (bf16[16,7,8,768]{3,2,1,0:T(8,128)(2,1)}, bf16[16,7,8,768]{3,2,1,0:T(8,128)(2,1)S(1)}, u32[]{:S(2)}) copy-start(bf16[16,7,8,768]{3,2,1,0:T(8,128)(2,1)S(1)} %collective-permute-done.7.refs_2_) | copy-start | bytes 4128772
  247.3 13.5 %copy-start.5 = (bf16[4,12,8,768]{3,2,1,0:T(8,128)(2,1)}, bf16[4,12,8,768]{3,2,1,0:T(8,128)(2,1)S(1)}, u32[]{:S(2)}) copy-start(bf16[4,12,8,768]{3,2,1,0:T(8,128)(2,1)S(1)} %collective-permute-done.8.refs_2_) | copy-start | bytes 1769476
  263.4 32.1 %collective-permute-start.11 = (bf16[24,8,768]{2,1,0:T(8,128)(2,1)}, bf16[24,8,768]{2,1,0:T(8,128)(2,1)}, u32[]{:S(2)}, u32[]{:S(2)}) collective-permute-start(bf16[24,8,768]{2,1,0:T(8,128)(2,1)} %get-tuple-element.272), channel_id=1, source_target_pairs={{0,8},{1,9},{2,10},{3,11},{4,12},{5,13},{6,14},{7,15},{8,0},{9,1},... | collective-permute-start | bytes 884744 | tf_op jit(solution)/shard_map/ppermute | solution.py:1660
  265.3 30.2 %collective-permute-start.12 = (bf16[24,8,768]{2,1,0:T(8,128)(2,1)}, bf16[24,8,768]{2,1,0:T(8,128)(2,1)}, u32[]{:S(2)}, u32[]{:S(2)}) collective-permute-start(bf16[24,8,768]{2,1,0:T(8,128)(2,1)} %get-tuple-element.273), channel_id=1, source_target_pairs={{0,16},{1,17},{2,18},{3,19},{4,20},{5,21},{6,22},{7,23},{8,24},{9,... | collective-permute-start | bytes 884744 | tf_op jit(solution)/shard_map/ppermute | solution.py:1660
  267.9 27.7 %collective-permute-start.13 = (bf16[24,8,768]{2,1,0:T(8,128)(2,1)}, bf16[24,8,768]{2,1,0:T(8,128)(2,1)}, u32[]{:S(2)}, u32[]{:S(2)}) collective-permute-start(bf16[24,8,768]{2,1,0:T(8,128)(2,1)} %get-tuple-element.274), channel_id=1, source_target_pairs={{0,24},{1,25},{2,26},{3,27},{4,28},{5,29},{6,30},{7,31},{8,16},{9,... | collective-permute-start | bytes 884744 | tf_op jit(solution)/shard_map/ppermute | solution.py:1660
  272.4 23.2 %collective-permute-start.14 = (bf16[8,7,8,768]{3,2,1,0:T(8,128)(2,1)}, bf16[8,7,8,768]{3,2,1,0:T(8,128)(2,1)S(1)}, u32[]{:S(2)}, u32[]{:S(2)}) collective-permute-start(bf16[8,7,8,768]{3,2,1,0:T(8,128)(2,1)} %get-tuple-element.275), channel_id=1, source_target_pairs={{0,4},{1,5},{2,6},{3,7},{4,0},{5,1},{6,2},{7,3},{8,12},{9,13},{10,... | collective-permute-start | bytes 2064392 | tf_op jit(solution)/shard_map/ppermute | solution.py:1660
  274.1 26.5 %copy-start.20 = (bf16[12,8,768]{2,1,0:T(8,128)(2,1)S(1)}, bf16[12,8,768]{2,1,0:T(8,128)(2,1)}, u32[]{:S(2)}) copy-start(bf16[12,8,768]{2,1,0:T(8,128)(2,1)} %get-tuple-element.285) | copy-start | bytes 442372
  295.5 0.9 copy-start.3
  295.6 5.7 %collective-permute-start.18 = (bf16[17,17,8,256]{3,2,1,0:T(8,128)(2,1)}, bf16[17,17,8,256]{3,2,1,0:T(8,128)(2,1)S(1)}, u32[]{:S(2)}, u32[]{:S(2)}) collective-permute-start(bf16[17,17,8,256]{3,2,1,0:T(8,128)(2,1)} %get-tuple-element.299), channel_id=1, source_target_pairs={{0,1},{1,0},{2,3},{3,2},{4,5},{5,4},{6,7},{7,6},{8,9},{9,8},{10,11... | collective-permute-start | bytes 3551240 | tf_op jit(solution)/shard_map/ppermute | solution.py:1660
  299.4 12.8 %collective-permute-start.25 = (bf16[4,7,8,768]{3,2,1,0:T(8,128)(2,1)}, bf16[4,7,8,768]{3,2,1,0:T(8,128)(2,1)S(1)}, u32[]{:S(2)}, u32[]{:S(2)}) collective-permute-start(bf16[4,7,8,768]{3,2,1,0:T(8,128)(2,1)} %get-tuple-element.321), channel_id=1, source_target_pairs={{0,2},{1,3},{2,0},{3,1},{4,6},{5,7},{6,4},{7,5},{8,10},{9,11},{10,... | collective-permute-start | bytes 1032200 | tf_op jit(solution)/shard_map/ppermute | solution.py:1660
  300.6 8.1 %collective-permute-start.15 = (bf16[12,8,768]{2,1,0:T(8,128)(2,1)S(1)}, bf16[12,8,768]{2,1,0:T(8,128)(2,1)S(1)}, u32[]{:S(2)}, u32[]{:S(2)}) collective-permute-start(bf16[12,8,768]{2,1,0:T(8,128)(2,1)S(1)} %copy-done.20), channel_id=1, source_target_pairs={{0,8},{1,9},{2,10},{3,11},{4,12},{5,13},{6,14},{7,15},{8,0},{9,1},... | collective-permute-start | bytes 442376 | tf_op jit(solution)/shard_map/ppermute | solution.py:1660
  301.3 1.0 copy-start.1
  305.2 29.0 %collective-permute-start.19 = (bf16[5,17,8,256]{3,2,1,0:T(8,128)(2,1)}, bf16[5,17,8,256]{3,2,1,0:T(8,128)(2,1)S(1)}, u32[]{:S(2)}, u32[]{:S(2)}) collective-permute-start(bf16[5,17,8,256]{3,2,1,0:T(8,128)(2,1)} %get-tuple-element.301), channel_id=1, source_target_pairs={{0,2},{1,3},{2,0},{3,1},{4,6},{5,7},{6,4},{7,5},{8,10},{9,11},{10,... | collective-permute-start | bytes 1044488 | tf_op jit(solution)/shard_map/ppermute | solution.py:1660
  306.0 28.2 %collective-permute-start.20 = (bf16[5,17,8,256]{3,2,1,0:T(8,128)(2,1)}, bf16[5,17,8,256]{3,2,1,0:T(8,128)(2,1)S(1)}, u32[]{:S(2)}, u32[]{:S(2)}) collective-permute-start(bf16[5,17,8,256]{3,2,1,0:T(8,128)(2,1)} %get-tuple-element.302), channel_id=1, source_target_pairs={{0,4},{1,5},{2,6},{3,7},{4,0},{5,1},{6,2},{7,3},{8,12},{9,13},{10,... | collective-permute-start | bytes 1044488 | tf_op jit(solution)/shard_map/ppermute | solution.py:1660
  306.6 27.7 %collective-permute-start.21 = (bf16[5,17,8,256]{3,2,1,0:T(8,128)(2,1)}, bf16[5,17,8,256]{3,2,1,0:T(8,128)(2,1)S(1)}, u32[]{:S(2)}, u32[]{:S(2)}) collective-permute-start(bf16[5,17,8,256]{3,2,1,0:T(8,128)(2,1)} %get-tuple-element.303), channel_id=1, source_target_pairs={{0,6},{1,7},{2,4},{3,5},{4,2},{5,3},{6,0},{7,1},{8,14},{9,15},{10,... | collective-permute-start | bytes 1044488 | tf_op jit(solution)/shard_map/ppermute | solution.py:1660
  308.7 15.5 %copy-start.10 = (bf16[12,8,768]{2,1,0:T(8,128)(2,1)}, bf16[12,8,768]{2,1,0:T(8,128)(2,1)S(1)}, u32[]{:S(2)}) copy-start(bf16[12,8,768]{2,1,0:T(8,128)(2,1)S(1)} %collective-permute-done.15.refs_1_) | copy-start | bytes 442372
  308.7 13.2 %collective-permute-start.16 = (bf16[12,8,768]{2,1,0:T(8,128)(2,1)}, bf16[12,8,768]{2,1,0:T(8,128)(2,1)S(1)}, u32[]{:S(2)}, u32[]{:S(2)}) collective-permute-start(bf16[12,8,768]{2,1,0:T(8,128)(2,1)} %get-tuple-element.286), channel_id=1, source_target_pairs={{0,16},{1,17},{2,18},{3,19},{4,20},{5,21},{6,22},{7,23},{8,24},{9,... | collective-permute-start | bytes 442376 | tf_op jit(solution)/shard_map/ppermute | solution.py:1660
  312.2 2.0 copy-start.9
  312.2 11.9 %collective-permute-start.17 = (bf16[12,8,768]{2,1,0:T(8,128)(2,1)}, bf16[12,8,768]{2,1,0:T(8,128)(2,1)S(1)}, u32[]{:S(2)}, u32[]{:S(2)}) collective-permute-start(bf16[12,8,768]{2,1,0:T(8,128)(2,1)} %get-tuple-element.287), channel_id=1, source_target_pairs={{0,24},{1,25},{2,26},{3,27},{4,28},{5,29},{6,30},{7,31},{8,16},{9,... | collective-permute-start | bytes 442376 | tf_op jit(solution)/shard_map/ppermute | solution.py:1660
  321.9 2.2 copy-start.11
  321.9 22.2 %collective-permute-start.26 = (bf16[7,8,768]{2,1,0:T(8,128)(2,1)}, bf16[7,8,768]{2,1,0:T(8,128)(2,1)S(1)}, u32[]{:S(2)}, u32[]{:S(2)}) collective-permute-start(bf16[7,8,768]{2,1,0:T(8,128)(2,1)} %get-tuple-element.323), channel_id=1, source_target_pairs={{0,8},{1,9},{2,10},{3,11},{4,12},{5,13},{6,14},{7,15},{8,0},{9,1},... | collective-permute-start | bytes 258056 | tf_op jit(solution)/shard_map/ppermute | solution.py:1660
  324.2 0.7 copy-start.12
  328.8 13.2 %copy-start.22 = (bf16[7,8,768]{2,1,0:T(8,128)(2,1)S(1)}, bf16[7,8,768]{2,1,0:T(8,128)(2,1)}, u32[]{:S(2)}) copy-start(bf16[7,8,768]{2,1,0:T(8,128)(2,1)} %get-tuple-element.324) | copy-start | bytes 258052
  328.8 15.3 %copy-start.21 = (bf16[7,8,768]{2,1,0:T(8,128)(2,1)S(1)}, bf16[7,8,768]{2,1,0:T(8,128)(2,1)}, u32[]{:S(2)}) copy-start(bf16[7,8,768]{2,1,0:T(8,128)(2,1)} %get-tuple-element.325) | copy-start | bytes 258052
  334.2 0.7 copy-start.6
  334.2 0.9 copy-start.7
  334.2 1.0 copy-start.8
  337.3 19.8 %collective-permute-start.22 = (bf16[23,8,256]{2,1,0:T(8,128)(2,1)}, bf16[23,8,256]{2,1,0:T(8,128)(2,1)S(1)}, u32[]{:S(2)}, u32[]{:S(2)}) collective-permute-start(bf16[23,8,256]{2,1,0:T(8,128)(2,1)} %get-tuple-element.309), channel_id=1, source_target_pairs={{0,8},{1,9},{2,10},{3,11},{4,12},{5,13},{6,14},{7,15},{8,0},{9,1},... | collective-permute-start | bytes 282632 | tf_op jit(solution)/shard_map/ppermute | solution.py:1660
  339.2 18.0 %collective-permute-start.23 = (bf16[23,8,256]{2,1,0:T(8,128)(2,1)}, bf16[23,8,256]{2,1,0:T(8,128)(2,1)S(1)}, u32[]{:S(2)}, u32[]{:S(2)}) collective-permute-start(bf16[23,8,256]{2,1,0:T(8,128)(2,1)} %get-tuple-element.310), channel_id=1, source_target_pairs={{0,16},{1,17},{2,18},{3,19},{4,20},{5,21},{6,22},{7,23},{8,24},{9,... | collective-permute-start | bytes 282632 | tf_op jit(solution)/shard_map/ppermute | solution.py:1660
  340.6 16.5 %collective-permute-start.24 = (bf16[23,8,256]{2,1,0:T(8,128)(2,1)}, bf16[23,8,256]{2,1,0:T(8,128)(2,1)S(1)}, u32[]{:S(2)}, u32[]{:S(2)}) collective-permute-start(bf16[23,8,256]{2,1,0:T(8,128)(2,1)} %get-tuple-element.311), channel_id=1, source_target_pairs={{0,24},{1,25},{2,26},{3,27},{4,28},{5,29},{6,30},{7,31},{8,16},{9,... | collective-permute-start | bytes 282632 | tf_op jit(solution)/shard_map/ppermute | solution.py:1660
  342.0 12.7 %collective-permute-start.27 = (bf16[7,8,768]{2,1,0:T(8,128)(2,1)S(1)}, bf16[7,8,768]{2,1,0:T(8,128)(2,1)S(1)}, u32[]{:S(2)}, u32[]{:S(2)}) collective-permute-start(bf16[7,8,768]{2,1,0:T(8,128)(2,1)S(1)} %copy-done.22), channel_id=1, source_target_pairs={{0,16},{1,17},{2,18},{3,19},{4,20},{5,21},{6,22},{7,23},{8,24},{9,... | collective-permute-start | bytes 258056 | tf_op jit(solution)/shard_map/ppermute | solution.py:1660
  344.1 10.7 %copy-start.16 = (bf16[7,8,768]{2,1,0:T(8,128)(2,1)}, bf16[7,8,768]{2,1,0:T(8,128)(2,1)S(1)}, u32[]{:S(2)}) copy-start(bf16[7,8,768]{2,1,0:T(8,128)(2,1)S(1)} %collective-permute-done.26.refs_1_) | copy-start | bytes 258052
  344.1 10.7 %collective-permute-start.28 = (bf16[7,8,768]{2,1,0:T(8,128)(2,1)S(1)}, bf16[7,8,768]{2,1,0:T(8,128)(2,1)S(1)}, u32[]{:S(2)}, u32[]{:S(2)}) collective-permute-start(bf16[7,8,768]{2,1,0:T(8,128)(2,1)S(1)} %copy-done.21), channel_id=1, source_target_pairs={{0,24},{1,25},{2,26},{3,27},{4,28},{5,29},{6,30},{7,31},{8,16},{9,... | collective-permute-start | bytes 258056 | tf_op jit(solution)/shard_map/ppermute | solution.py:1660
  354.8 0.6 copy-start.17
  354.8 0.7 copy-start.18
  357.1 0.7 copy-start.13
  357.1 0.7 copy-start.14
  357.2 0.7 copy-start.15
Sparse Core Ops, SparseCore 0:
  199.9 58.0 all-gather.2

commit v4 on v3

--- a/solution.py
+++ b/solution.py
@@ -136,7 +136,7 @@
 
 
 PAIRS = 16
-VECTORS = 3
+VECTORS = 7
 
 
 def store_pairs(values, mine_ref, other_ref, core):
@@ -579,7 +579,6 @@
             grad = ref[0].astype(f32) * keep
             sent[image_rows(image), :] = grad.astype(bf16)
             sums = sums + fold(grad)
-            normed_turned[:, image_rows(image)] = normed_ref[image].T
         grad_shrink_bias_ref[...] = sums
         result[...] = jnp.zeros_like(result)
         grad_normed[...] = jnp.zeros_like(grad_normed)
@@ -605,7 +604,7 @@
             grad_normed[rows, :] += dot_nt(grad_low, expand_ref[...])
     grad_expand_bias_ref[...] = bias_sums
     shrink_total[...] = dot_tn(hidden[...], sent[...])
-    expand_total[...] = dot_nn(normed_turned[...], grad_pre[...])
+    expand_total[...] = dot_tn(normed_ref[...].reshape(images * cells, width), grad_pre[...])
     core = core_ref[0]
     store_pairs(shrink_total, shrink_mine_ref, shrink_other_ref, core)
     store_pairs(expand_total, expand_mine_ref, expand_other_ref, core)
@@ -844,16 +843,10 @@
     tokens_ref,
     mixed_ref,
     grad_resid_ref,
-    feed_expand_ref,
-    feed_shrink_ref,
-    mix_sums_ref,
-    attend_sums0_ref,
-    attend_sums1_ref,
     grad_tokens_ref,
     mine_ref,
     other_ref,
     sums_ref,
-    vectors_ref,
     grad_joint,
     weight_total,
     grad_normed,
@@ -877,14 +870,6 @@
         for copy in loads:
             copy.start()
         grad_normed[...] = jnp.zeros_like(grad_normed)
-        vectors_ref[...] = jnp.zeros_like(vectors_ref)
-        for k in range(feed_expand_ref.shape[1] // width):
-            vectors_ref[k : k + 1, :] = total(feed_expand_ref[:, k * width : (k + 1) * width])
-        vectors_ref[4:5, :] = total(feed_shrink_ref[...])
-        for k in range(3):
-            vectors_ref[5 + k : 6 + k, :] = total(mix_sums_ref[k])
-        for k in range(2):
-            vectors_ref[8 + k : 9 + k, :] = total(attend_sums0_ref[k] + attend_sums1_ref[k])
 
     @pl.when(step < last)
     def _():
@@ -924,11 +909,6 @@
     grad_joint1,
     gain1,
     joint,
-    sums_expand,
-    sums_shrink,
-    sums_mix,
-    sums_attend0,
-    sums_attend1,
 ):
     images, cells, width = tokens.shape
     size = width // (2 * PAIRS)
@@ -943,7 +923,6 @@
             jax.ShapeDtypeStruct(half, bf16),
             jax.ShapeDtypeStruct(half, bf16),
             jax.ShapeDtypeStruct((2, 8, width), f32),
-            jax.ShapeDtypeStruct((16, width), f32),
         ),
         grid_spec=pltpu.PrefetchScalarGridSpec(
             num_scalar_prefetch=1,
@@ -957,18 +936,12 @@
                 anywhere,
                 anywhere,
                 anywhere,
-                whole(sums_expand.shape),
-                whole(sums_shrink.shape),
-                whole(sums_mix.shape),
-                whole(sums_attend0.shape),
-                whole(sums_attend1.shape),
             ],
             out_specs=[
                 whole((images, cells, width)),
                 half_spec,
                 half_spec,
                 whole((2, 8, width)),
-                whole((16, width)),
             ],
             scratch_shapes=[
                 pltpu.VMEM((images * cells, width), bf16),
@@ -993,11 +966,6 @@
         tokens,
         mixed,
         grad_resid,
-        sums_expand,
-        sums_shrink,
-        sums_mix,
-        sums_attend0,
-        sums_attend1,
     )
 
 
@@ -1008,11 +976,9 @@
 
 def embed_weights_kernel(
     class_ref,
-    core_ref,
     grad_tokens_ref,
     stem_ref,
-    mine_ref,
-    other_ref,
+    blocks_ref,
     sums_ref,
     grad_masked,
     weight_total,
@@ -1038,33 +1004,28 @@
             block * position_rows : (block + 1) * position_rows, :
         ]
     weight_total[...] = dot_tn(stem_ref[...].reshape(images * cells, channels), grad_masked[...])
-    core = core_ref[0]
     size = channels // (2 * PAIRS)
-    for pair in range(PAIRS):
-        for ref, side in ((mine_ref, core), (other_ref, 1 - core)):
-            block = 2 * pair + side
-            at = pl.ds(pl.multiple_of(block * size, 8), size)
-            ref[pair, 0 : size // 8] = sections_of(weight_total[at, :])
-            ref[pair, size // 8 :] = sections_of(position_total[block])
-
-
-def embed_weights(image_class, core, grad_tokens, stem):
+    for block in range(2 * PAIRS):
+        blocks_ref[block, 0 : size // 8] = sections_of(weight_total[block * size : (block + 1) * size, :])
+        blocks_ref[block, size // 8 :] = sections_of(position_total[block])
+
+
+def embed_weights(image_class, grad_tokens, stem):
     images, cells, width = grad_tokens.shape
     channels = stem.shape[2]
     position_rows = -(-cells // (2 * PAIRS) // 8) * 8
-    half = (PAIRS, (channels // (2 * PAIRS) + position_rows) // 8, 8, width)
+    blocks = (2 * PAIRS, (channels // (2 * PAIRS) + position_rows) // 8, 8, width)
     return pl.pallas_call(
         embed_weights_kernel,
         out_shape=(
-            jax.ShapeDtypeStruct(half, bf16),
-            jax.ShapeDtypeStruct(half, bf16),
+            jax.ShapeDtypeStruct(blocks, bf16),
             jax.ShapeDtypeStruct((8, width), f32),
         ),
         grid_spec=pltpu.PrefetchScalarGridSpec(
-            num_scalar_prefetch=2,
+            num_scalar_prefetch=1,
             grid=(1,),
             in_specs=[whole(grad_tokens.shape), whole(stem.shape)],
-            out_specs=[whole(half), whole(half), whole((8, width))],
+            out_specs=[whole(blocks), whole((8, width))],
             scratch_shapes=[
                 pltpu.VMEM((images * cells, width), bf16),
                 pltpu.VMEM((channels, width), f32),
@@ -1074,7 +1035,7 @@
         compiler_params=pltpu.CompilerParams(vmem_limit_bytes=62 * MIB),
         cost_estimate=cost(8_000_000_000, 8 * MIB),
         name="embed_weights",
-    )(image_class, core, grad_tokens, stem)
+    )(image_class, grad_tokens, stem)
 
 
 def embed_backward_kernel(
@@ -1194,6 +1155,11 @@
     sums_embed_ref,
     sums3_ref,
     sums_attn_ref,
+    sums_expand_ref,
+    sums_shrink_ref,
+    sums_mix_ref,
+    sums_attend0_ref,
+    sums_attend1_ref,
     arrived_ref,
     grad_first_ref,
     mine_ref,
@@ -1311,6 +1277,13 @@
             total(sums2[1]),
             total(sums3_ref[0]),
             total(sums3_ref[1]),
+            total(sums_expand_ref[...]),
+            total(sums_shrink_ref[...]),
+            total(sums_mix_ref[0]),
+            total(sums_mix_ref[1]),
+            total(sums_mix_ref[2]),
+            total(sums_attend0_ref[0] + sums_attend1_ref[0]),
+            total(sums_attend0_ref[1] + sums_attend1_ref[1]),
         ):
             for start in range(0, item.shape[1], middle):
                 vectors[row : row + 1, :] = item[:, start : start + middle]
@@ -1335,6 +1308,7 @@
     sums_embed,
     sums3,
     sums_attn,
+    sums_block,
     arrived,
 ):
     images, cells, channels = x.shape
@@ -1377,6 +1351,7 @@
                 whole((8, width)),
                 whole((2, 8, channels)),
                 whole((2, 8, width)),
+                *[whole(item.shape) for item in sums_block],
                 slot_spec,
             ],
             out_specs=[
@@ -1418,6 +1393,7 @@
         sums_embed,
         sums3,
         sums_attn,
+        *sums_block,
         arrived,
     )
 
@@ -1530,25 +1506,77 @@
     )(bits, *flat)
 
 
-def split_depth_kernel(depth_ref, *refs):
-    outs = refs[-4:]
+def split_merged_kernel(bits_ref, *refs, bit):
+    outs = refs[-2:]
     start = 0
-    for k in range(len(refs) // 2 - 2):
+    for k in range(len(refs) // 2 - 1):
         left, right = refs[2 * k], refs[2 * k + 1]
         size = left.shape[1]
-        for q in range(4):
-            at = lax.bitwise_xor(depth_ref[0], q)
-            summed = left[at].astype(f32) + right[at].astype(f32)
-            outs[q][start : start + size] = summed.astype(bf16)
+        for at in range(left.shape[0] // 2):
+            for q in range(2):
+                here = 2 * at + lax.bitwise_xor(bits_ref[bit], q)
+                summed = left[here].astype(f32) + right[here].astype(f32)
+                outs[q][at, start : start + size] = summed.astype(bf16)
         start += size
 
 
-def split_depth(depth, pairs):
+def split_merged(bits, pairs, bit):
     flat = [item for pair in pairs for item in pair]
-    shape = (sum(pair[0].shape[1] for pair in pairs),) + flat[0].shape[2:]
+    shape = (flat[0].shape[0] // 2, sum(pair[0].shape[1] for pair in pairs)) + flat[0].shape[2:]
     size = sum(item.size for item in flat)
     return pl.pallas_call(
-        split_depth_kernel,
+        lambda *refs: split_merged_kernel(*refs, bit=bit),
+        out_shape=[jax.ShapeDtypeStruct(shape, bf16)] * 2,
+        grid_spec=pltpu.PrefetchScalarGridSpec(
+            num_scalar_prefetch=1,
+            grid=(1,),
+            in_specs=[whole(item.shape) for item in flat],
+            out_specs=[whole(shape)] * 2,
+        ),
+        compiler_params=pltpu.CompilerParams(vmem_limit_bytes=62 * MIB),
+        cost_estimate=cost(size, 3 * size),
+        name="split_merged",
+    )(bits, *flat)
+
+
+def four(values):
+    if len(values) == 1:
+        return values[0]
+    if len(values) == 2:
+        return values[0] + values[1]
+    return (values[0] + values[1]) + (values[2] + values[3])
+
+
+def combine_plane_kernel(depth_ref, *refs, extra, beside):
+    parts, outs = refs[:4], refs[4 + beside :]
+    size = parts[0].shape[1]
+    columns = parts[0].shape[3]
+    for q in range(4):
+        at = lax.bitwise_xor(depth_ref[0], q)
+        outs[q][0:size] = four([part[at].astype(f32) for part in parts]).astype(bf16)
+        if beside:
+            summed = refs[4][at].astype(f32) + refs[5][at].astype(f32)
+            start = size + 2 * VECTORS * extra
+            for section in range(summed.shape[0]):
+                for k in range(summed.shape[2] // columns):
+                    outs[q][start] = summed[section, :, k * columns : (k + 1) * columns].astype(bf16)
+                    start += 1
+    if extra:
+        vectors = four([load_split(part.at[PAIRS // 4], 0) for part in parts])
+        for out in outs:
+            store_split(out, size, vectors)
+
+
+def combine_plane(depth, parts, extra, beside=()):
+    columns = parts[0].shape[3]
+    sections = parts[0].shape[1] + 2 * VECTORS * extra
+    if beside:
+        sections += beside[0].shape[1] * (beside[0].shape[3] // columns)
+    shape = (sections,) + parts[0].shape[2:]
+    flat = list(parts) + list(beside)
+    size = sum(item.size for item in flat)
+    return pl.pallas_call(
+        lambda *refs: combine_plane_kernel(*refs, extra=extra, beside=len(beside)),
         out_shape=[jax.ShapeDtypeStruct(shape, bf16)] * 4,
         grid_spec=pltpu.PrefetchScalarGridSpec(
             num_scalar_prefetch=1,
@@ -1558,42 +1586,8 @@
         ),
         compiler_params=pltpu.CompilerParams(vmem_limit_bytes=62 * MIB),
         cost_estimate=cost(size, 3 * size),
-        name="split_depth",
+        name="combine_plane",
     )(depth, *flat)
-
-
-def four(values):
-    return (values[0] + values[1]) + (values[2] + values[3])
-
-
-def combine_plane_kernel(depth_ref, *refs, extra):
-    parts, outs = refs[:4], refs[4:]
-    size = parts[0].shape[1]
-    for q in range(4):
-        at = lax.bitwise_xor(depth_ref[0], q)
-        outs[q][0:size] = four([part[at].astype(f32) for part in parts]).astype(bf16)
-    if extra:
-        vectors = four([load_split(part.at[PAIRS // 4], 0) for part in parts])
-        for out in outs:
-            store_split(out, size, vectors)
-
-
-def combine_plane(depth, parts, extra):
-    shape = (parts[0].shape[1] + 2 * VECTORS * extra,) + parts[0].shape[2:]
-    size = 4 * parts[0].size
-    return pl.pallas_call(
-        lambda *refs: combine_plane_kernel(*refs, extra=extra),
-        out_shape=[jax.ShapeDtypeStruct(shape, bf16)] * 4,
-        grid_spec=pltpu.PrefetchScalarGridSpec(
-            num_scalar_prefetch=1,
-            grid=(1,),
-            in_specs=[whole(item.shape) for item in parts],
-            out_specs=[whole(shape)] * 4,
-        ),
-        compiler_params=pltpu.CompilerParams(vmem_limit_bytes=62 * MIB),
-        cost_estimate=cost(size, 3 * size),
-        name="combine_plane",
-    )(depth, *parts)
 
 
 def store_lines(outs, vectors, lines):
@@ -1607,53 +1601,49 @@
     return [jax.ShapeDtypeStruct((sum(size for _, size in pieces),), f32) for pieces in lines]
 
 
-def combine_depth_kernel(*refs, places, lines):
-    parts, outs = refs[:4], refs[4:]
-    count = len(places)
-    summed = four([part[0:count].astype(f32) for part in parts])
-    for section, (out, row, column, columns, rows) in enumerate(places):
-        stride = columns // LANES
-        for lane in range(summed.shape[2] // LANES):
-            start = row * stride + column // LANES + lane
-            outs[out][pl.ds(start, rows, stride=stride), :] = summed[
-                section, 0:rows, lane * LANES : (lane + 1) * LANES
-            ]
-    if lines:
-        vectors = four([load_split(part, count) for part in parts])
-        store_lines(outs[len(outs) - len(lines) :], vectors, lines)
-
-
-def combine_depth(parts, places, sizes, lines):
-    shapes = [jax.ShapeDtypeStruct((size // LANES, LANES), f32) for size in sizes] + line_shapes(lines)
-    size = 4 * parts[0].size
+def combine_depth_kernel(*refs, batches):
+    outs = refs[sum(count for count, _, _, _ in batches) :]
+    first = first_out = 0
+    for count, places, sizes, lines in batches:
+        parts = refs[first : first + count]
+        here = outs[first_out : first_out + sizes + len(lines)]
+        summed = four([part[...].astype(f32) for part in parts])
+        for section, place in enumerate(places):
+            if place is None:
+                continue
+            out, row, column, columns, rows = place
+            stride = columns // LANES
+            for lane in range(summed.shape[2] // LANES):
+                start = row * stride + column // LANES + lane
+                here[out][pl.ds(start, rows, stride=stride), :] = summed[
+                    section, 0:rows, lane * LANES : (lane + 1) * LANES
+                ]
+        if lines:
+            vectors = four([load_split(part, places.index(None)) for part in parts])
+            store_lines(here[sizes:], vectors, lines)
+        first += count
+        first_out += sizes + len(lines)
+
+
+def combine_depth(batches):
+    flat = [item for parts, _, _, _ in batches for item in parts]
+    shapes = []
+    for _, _, sizes, lines in batches:
+        shapes += [jax.ShapeDtypeStruct((size // LANES, LANES), f32) for size in sizes]
+        shapes += line_shapes(lines)
+    size = sum(item.size for item in flat)
+    known = [(len(parts), places, len(sizes), lines) for parts, places, sizes, lines in batches]
     outs = pl.pallas_call(
-        lambda *refs: combine_depth_kernel(*refs, places=places, lines=lines),
+        lambda *refs: combine_depth_kernel(*refs, batches=known),
         out_shape=shapes,
         grid=(1,),
-        in_specs=[whole(item.shape) for item in parts],
+        in_specs=[whole(item.shape) for item in flat],
         out_specs=[whole(item.shape) for item in shapes],
         compiler_params=pltpu.CompilerParams(vmem_limit_bytes=62 * MIB),
         cost_estimate=cost(size, 3 * size),
         name="combine_depth",
-    )(*parts)
-    return [item.reshape(-1) for item in outs[: len(sizes)]], list(outs[len(sizes) :])
-
-
-def sum_vectors_kernel(gathered_ref, *outs, lines):
-    store_lines(outs, jnp.sum(gathered_ref[...], axis=0), lines)
-
-
-def sum_vectors(gathered, lines):
-    shapes = line_shapes(lines)
-    return pl.pallas_call(
-        lambda *refs: sum_vectors_kernel(*refs, lines=lines),
-        out_shape=shapes,
-        grid=(1,),
-        in_specs=[whole(gathered.shape)],
-        out_specs=[whole(item.shape) for item in shapes],
-        compiler_params=pltpu.CompilerParams(vmem_limit_bytes=62 * MIB),
-        name="sum_vectors",
-    )(gathered)
+    )(*flat)
+    return [item.reshape(-1) for item in outs]
 
 
 def permuted(item, distance, devices):
@@ -1665,7 +1655,7 @@
         self.devices = devices
         self.plane = ((index // 2) % 4).astype(jnp.int32).reshape(1)
         self.depth = (index // 8).astype(jnp.int32).reshape(1)
-        self.bits = jnp.stack([index // 4 % 2, index // 2 % 2]).astype(jnp.int32)
+        self.bits = jnp.stack([index // unit % 2 for unit in (4, 2, 8, 16)]).astype(jnp.int32)
 
     def spread(self, parts, unit):
         return [parts[0]] + [permuted(parts[q], q * unit, self.devices) for q in (1, 2, 3)]
@@ -1686,8 +1676,12 @@
     def start_plane(self, parts):
         return self.spread(parts, 2)
 
-    def end_plane(self, started, extra=0):
-        return combine_plane(self.depth, started, extra)
+    def merged(self, pairs, bit, distance):
+        keep, send = split_merged(self.bits, pairs, bit)
+        return keep, permuted(send, distance, self.devices)
+
+    def end_plane(self, started, extra=0, beside=()):
+        return combine_plane(self.depth, started, extra, beside)
 
     def start_depth(self, parts):
         return self.spread(parts, 8)
@@ -1713,11 +1707,15 @@
 
 def scattered(mine, other, places, sizes, devices):
     blocks = jnp.stack([mine, other], axis=1).reshape((2 * PAIRS,) + mine.shape[1:])
+    return scattered_blocks(blocks, places, sizes, devices)
+
+
+def scattered_blocks(blocks, places, sizes, devices):
     results = []
     for out, size in sizes:
         chosen = [k for k, place in enumerate(places) if place[0] == out]
         columns = places[chosen[0]][3]
-        width = mine.shape[-1]
+        width = blocks.shape[-1]
         rows = size // columns
         groups = columns // width
         values = blocks[:, chosen[0] : chosen[-1] + 1]
@@ -1833,7 +1831,7 @@
     grad_joint1, sums_attend1 = attend_backward(
         1, image_class, query, key, value, log_total, grad_mixed
     )
-    grad_tokens, joint_mine, joint_other, sums_attn, vectors_block = joint_backward(
+    grad_tokens, joint_mine, joint_other, sums_attn = joint_backward(
         core,
         tokens,
         normed,
@@ -1843,29 +1841,24 @@
         grad_joint1,
         attn_gain,
         joint_weight,
-        sums_expand,
-        sums_shrink,
-        sums_mix,
-        sums_attend0,
-        sums_attend1,
     )
-    gathered = lax.all_gather(vectors_block, BOTH)
     if staged:
         feed_half, arrived, joint_other = ahead(grad_tokens, (feed_half, arrived, joint_other))
         joint_other = after(joint_other, *feed_half[0], *feed_half[1], arrived)
         joint_core = sums.start_core([joint_mine], [joint_other])
         feed_quarter = sums.halves(feed_half, ((1, 1), (1, 0)), (2, 4), 1)
         grad_tokens = after(grad_tokens, feed_quarter[0][0])
-    embed_mine, embed_other, sums_embed = embed_weights(image_class, core, grad_tokens, stem)
+    embed_blocks, sums_embed = embed_weights(image_class, grad_tokens, stem)
+    if staged:
+        embed_own = lax.psum_scatter(embed_blocks, BOTH, scatter_dimension=0, tiled=True)
     if staged:
         joint_core, feed_quarter, grad_tokens = ahead(
-            embed_mine, (joint_core, feed_quarter, grad_tokens)
+            embed_blocks, (joint_core, feed_quarter, grad_tokens)
         )
-        embed_core = sums.start_core([embed_mine], [embed_other])
         joint_parts = sums.end_core(joint_core)
         joint_plane = sums.start_plane(joint_parts)
-        feed_depth = split_depth(sums.depth, feed_quarter)
-        grad_tokens = after(grad_tokens, joint_plane[0], feed_depth[0])
+        feed_eighth = sums.merged(feed_quarter, 2, 8)
+        grad_tokens = after(grad_tokens, joint_plane[0], feed_eighth[0])
     grad_inner, grad_third, sums3 = embed_backward(
         image_class,
         grad_tokens,
@@ -1877,14 +1870,10 @@
         embed_weight,
     )
     if staged:
-        embed_core, joint_plane = ahead(grad_third, (embed_core, joint_plane))
-        feed_depth = after(feed_depth, *joint_plane)
-        feed_depth = sums.start_depth(feed_depth)
-        embed_half = sums.halves(
-            [(embed_core[0][0], embed_core[1][0])], ((2, 0),), (4,), 4
-        )
-        joint_parts = sums.end_plane(joint_plane)
-        grad_third = after(grad_third, joint_parts[0], embed_half[0][0])
+        joint_plane, feed_eighth = ahead(grad_third, (joint_plane, feed_eighth))
+        joint_depth = sums.start_depth(sums.end_plane(joint_plane))
+        feed_last = sums.merged([feed_eighth], 3, 16)
+        grad_third = after(grad_third, joint_depth[0], feed_last[0])
     grad_first, conv_mine, conv_other, block_output = convs_backward(
         image_class,
         core,
@@ -1900,16 +1889,14 @@
         sums_embed,
         sums3,
         sums_attn,
+        (sums_expand, sums_shrink, sums_mix, sums_attend0, sums_attend1),
         arrived,
     )
     block_output = block_output[None]
     if staged:
-        feed_depth, embed_half = ahead(grad_first, (feed_depth, embed_half))
-        conv_other = after(conv_other, *feed_depth, *embed_half[0])
+        feed_last, joint_depth = ahead(grad_first, (feed_last, joint_depth))
+        conv_other = after(conv_other, *feed_last, *joint_depth)
         conv_core = sums.start_core([conv_mine], [conv_other])
-        embed_quarter = sums.halves(embed_half, ((1, 1),), (2,), 1)
-        joint_depth = sums.start_depth(joint_parts)
-        grad_first = after(grad_first, embed_quarter[0][0])
     input_grad = input_backward(image_class, grad_inner, grad_first, std_in)
 
     parts = 2 * PAIRS
@@ -1930,30 +1917,29 @@
         9 * middle * middle // parts,
         middle * channels // parts,
     ]
-    block_lines = [[(row, width) for row in range(inner // width)]] + [
-        [(row, width)] for row in range(inner // width, inner // width + 6)
-    ]
     stem_lines = []
     row = 0
-    for size in [width] * 3 + [middle] * 4 + [channels] * 2:
+    for size in [width] * 3 + [middle] * 4 + [channels] * 2 + [inner] + [width] * 6:
         stem_lines.append([(row + k, middle) for k in range(size // middle)])
         row += size // middle
-    block_vectors = sum_vectors(gathered.reshape((-1,) + vectors_block.shape), block_lines)
     if staged:
         conv_plane = sums.start_plane(sums.end_core(conv_core, 1))
-        embed_depth = sums.start_depth(split_depth(sums.depth, embed_quarter))
-        (grad_shrink, grad_expand), _ = combine_depth(
-            feed_depth, shrink_places + expand_places, feed_sizes, []
+        grad_shrink, grad_expand, grad_joint, grad_mix = combine_depth(
+            [
+                ([item[0] for item in feed_last], shrink_places + expand_places, feed_sizes, []),
+                (joint_depth, joint_places, joint_sizes, []),
+            ]
         )
-        (grad_joint, grad_mix), _ = combine_depth(joint_depth, joint_places, joint_sizes, [])
-        conv_plane = ahead(
-            (input_grad, grad_shrink, grad_joint, block_vectors), conv_plane
+        conv_plane = ahead((input_grad, grad_shrink), conv_plane)
+        last_depth = sums.start_depth(sums.end_plane(conv_plane, 1))
+        grad_embed, grad_position, *grads = combine_depth(
+            [
+                ([embed_own[0]], embed_places, embed_sizes, []),
+                (last_depth, conv_places + [None] * (2 * VECTORS), conv_sizes, stem_lines),
+            ]
         )
-        conv_depth = sums.start_depth(sums.end_plane(conv_plane, 1))
-        (grad_embed, grad_position), _ = combine_depth(embed_depth, embed_places, embed_sizes, [])
-        (grad_in, grad_mid, grad_out), stem_vectors = combine_depth(
-            conv_depth, conv_places, conv_sizes, stem_lines
-        )
+        grad_in, grad_mid, grad_out = grads[:3]
+        stem_vectors = grads[3:]
     else:
         (grad_shrink,) = scattered(
             shrink_mine, shrink_other, shrink_places, [(0, feed_sizes[0])], devices
@@ -1964,8 +1950,8 @@
         grad_joint, grad_mix = scattered(
             joint_mine, joint_other, joint_places, list(enumerate(joint_sizes)), devices
         )
-        grad_embed, grad_position = scattered(
-            embed_mine, embed_other, embed_places, list(enumerate(embed_sizes)), devices
+        grad_embed, grad_position = scattered_blocks(
+            embed_blocks, embed_places, list(enumerate(embed_sizes)), devices
         )
         rows = conv_mine[PAIRS, :VECTORS].astype(f32) + conv_mine[PAIRS, VECTORS : 2 * VECTORS].astype(f32)
         rows = lax.psum(rows.reshape(-1, middle), BOTH)
@@ -1974,15 +1960,6 @@
         grad_in, grad_mid, grad_out = scattered(
             conv_mine, conv_other, conv_places, list(enumerate(conv_sizes)), devices
         )
-    (
-        grad_expand_bias,
-        grad_shrink_bias,
-        grad_mlp_gain,
-        grad_mlp_bias,
-        grad_mix_bias,
-        grad_query_bias,
-        grad_value_bias,
-    ) = block_vectors
     (
         grad_embed_bias,
         grad_attn_gain,
@@ -1993,6 +1970,13 @@
         grad_second_bias,
         grad_third_gain,
         grad_third_bias,
+        grad_expand_bias,
+        grad_shrink_bias,
+        grad_mlp_gain,
+        grad_mlp_bias,
+        grad_mix_bias,
+        grad_query_bias,
+        grad_value_bias,
     ) = stem_vectors
     return (
         block_output,

time: 374 us -> 356 us (0.952)
  Pallas kernels: 260 us -> 248 us
  starting transfers between devices: 45.9 us -> 36.7 us
  waiting for transfers between devices: 39.6 us -> 44.4 us
    ppermute x29 -> x22, starting transfers between devices: 36.4 us -> 27.2 us  [permuted(): return lax.ppermute(item, BOTH, [(k, k ^ distance) for k in range(devices)])]
    pallas_call x4 -> x2, Pallas kernels: 19.3 us -> 11.8 us  [split_two(): pl.pallas_call(lambda *refs: split_two_kernel(*refs, modes=modes), out_sh...]
    ppermute x29 -> x22, waiting for transfers between devices: 39.6 us -> 44.4 us  [permuted(): return lax.ppermute(item, BOTH, [(k, k ^ distance) for k in range(devices)])]
    pallas_call x10 -> x7, Pallas kernels: 25.9 us -> 22.2 us  [the longest x1 6.93 us: embed_weights(): pl.pallas_call(embed_weights_kernel, out_shape=(jax.ShapeDtypeStruct(bloc...]
  transfers between devices with their start and end apart: 32 -> 25, of which waited for: 7 -> 10; matrix products, arithmetic and copies ran while one was open for 0% -> 0% of each run, Pallas kernels for 55% -> 55%
where the time goes in v4:
time: 356 us; the launch traced here: 349 us
  Pallas kernels  248 us (70%)
  waiting for transfers between devices  44.4 us (12%)
  starting transfers between devices  36.7 us (10%)
  between operations  14.6 us (4%)
  local copies, waits for them, and re-layouts  4.75 us (1%)
    pallas_call x1, Pallas kernels, feed(): pl.pallas_call(feed_kernel, out_shape=(jax.ShapeDtypeStruct((slots, cells...  55.1 us
    ppermute x22, waiting for transfers between devices, permuted(): return lax.ppermute(item, BOTH, [(k, k ^ distance) for k in range(devices)])  44.4 us
    pallas_call x2, Pallas kernels, attend_backward(): pl.pallas_call(lambda *refs: attend_backward_kernel(*refs, image=image),...  34.2 us
    pallas_call x1, Pallas kernels, attend_forward(): pl.pallas_call(attend_forward_kernel, out_shape=(low, low, low, low, jax....  32.5 us
    ppermute x22, starting transfers between devices, permuted(): return lax.ppermute(item, BOTH, [(k, k ^ distance) for k in range(devices)])  27.2 us
    pallas_call x1, Pallas kernels, stem_forward(): pl.pallas_call(stem_forward_kernel, out_shape=(jax.ShapeDtypeStruct((chan...  24.7 us
    pallas_call x1, Pallas kernels, convs_backward(): pl.pallas_call(convs_backward_kernel, out_shape=(jax.ShapeDtypeStruct((im...  21.4 us
    pallas_call x1, Pallas kernels, joint_backward(): pl.pallas_call(joint_backward_kernel, out_shape=(jax.ShapeDtypeStruct((im...  18 us
  transfers between devices with their start and end apart: 25, of which 10 were waited for; matrix products, arithmetic and copies ran while one was open for 0% of the time, Pallas kernels for 55%

profile of v4, /device:TPU:0, one launch (start us, length us, event | category | flops | bytes accessed | tf_op | source)
XLA Modules:
  0.0 348.7 jit_solution(9607681697287615152)
XLA Ops:
  7.2 4.7 %all-to-all-start = ((bf16[4,576,768]{2,1,0:T(8,128)(2,1)}), bf16[4,576,768]{2,1,0:T(8,128)(2,1)}, u32[]{:S(2)}, u32[]{:S(2)}) async-start(bf16[4,576,768]{2,1,0:T(8,128)(2,1)} %bitcast.24), calls=%async_computation | async-start | bytes 7077888 | tf_op jit(solution)/shard_map/all_to_all | solution.py:1774
  12.0 0.1 reshape.98
  12.0 0.5 dynamic-slice_bitcast_fusion.mine_ref
  12.6 24.7 %stem_forward.1 = (bf16[1024,256]{1,0:T(8,128)(2,1)}, bf16[2304,256]{1,0:T(8,128)(2,1)}, bf16[256,1024]{1,0:T(8,128)(2,1)}, f32[2,576,256]{2,1,0:T(8,128)}, f32[...) custom-call(s32[2]{0:T(128)} %class_ref.13, ...), custom_call_target="tpu_custom_call" | custom-call | flops 24999999488 | bytes 31457280 | tf_op jit(solution)/shard_map/stem_forward/pallas_call | solution.py:302
  37.3 32.5 %attend_forward.1 = (bf16[2,576,768]{2,1,0:T(8,128)(2,1)}, bf16[2,576,768]{2,1,0:T(8,128)(2,1)}, bf16[2,576,768]{2,1,0:T(8,128)(2,1)}, bf16[2,576,768]{2,1,0:T(8...) custom-call(s32[2]{0:T(128)} %class_ref.13, ...), custom_call_target="tpu_custom_call" | custom-call | flops 35000000512 | bytes 31457280 | tf_op jit(solution)/shard_map/attend_forward/pallas_call | solution.py:462
  69.8 55.1 %feed.1 = (bf16[4,576,768]{2,1,0:T(8,128)(2,1)}, f32[2,576,768]{2,1,0:T(8,128)}, bf16[2,576,768]{2,1,0:T(8,128)(2,1)}, bf16[16,12,8,768]{3,2,1,0:T(8,128)(2,1)},...) custom-call(s32[2]{0:T(128)} %class_ref.13, ...), custom_call_target="tpu_custom_call" | custom-call | flops 38050725888 | bytes 41943040 | tf_op jit(solution)/shard_map/feed/pallas_call | solution.py:676
  124.9 0.5 collective-permute-start
  125.5 0.1 collective-permute-start.1
  125.5 0.6 pad_add_fusion.refs_0_
  126.1 4.7 %all-to-all-start.1 = ((bf16[4,576,768]{2,1,0:T(8,128)(2,1)}), bf16[4,576,768]{2,1,0:T(8,128)(2,1)}, u32[]{:S(2)}, u32[]{:S(2)}) async-start(bf16[4,576,768]{2,1,0:T(8,128)(2,1)} %get-tuple-element.192), calls=%async_computation.1 | async-start | bytes 7077888 | tf_op jit(solution)/shard_map/all_to_all | solution.py:1821
  130.8 0.0 reduce-scatter.2.cloned.1.call-start
  130.9 17.2 %attend_backward.2 = (bf16[1,576,2304]{2,1,0:T(8,128)(2,1)}, f32[2,8,768]{2,1,0:T(8,128)}) custom-call(s32[2]{0:T(128)} %class_ref.13, bf16[2,576,768]{2,1,0:T(8,128)(2,1)} %get-tuple-element.167.refs_1_, bf16[2,576,768]{2,1,0:T(8,128)(2,1)} %get-tuple-element.168.refs_2_, bf16[2,576,768]{2,1,0:T(8,128)(2,1)} %get-tuple-element.169.refs_3_, ...), custom_call_target="tpu_custom_call" | custom-call | flops 10192158720 | bytes 6291456 | tf_op jit(solution)/shard_map/attend_backward/pallas_call | solution.py:818
  148.1 6.9 %split_two.2 = (bf16[8,12,8,768]{3,2,1,0:T(8,128)(2,1)}, bf16[8,12,8,768]{3,2,1,0:T(8,128)(2,1)}, bf16[8,12,8,768]{3,2,1,0:T(8,128)(2,1)}, bf16[8,12,8,768]{3,2,1,0:T(8,128)(2,1)}) custom-call(s32[4]{0:T(128)} %pad_add_fusion.refs_0_, bf16[16,12,8,768]{3,2,1,0:T(8,128)(2,1)} %get-tuple-element.179.refs_1_, ...), custom_call_target="tpu_custom_call" | custom-call | flops 4718592 | bytes 14155776 | tf_op jit(solution)/shard_map/split_two/pallas_call | solution.py:1494
  155.0 2.9 collective-permute-start.2
  157.9 1.9 collective-permute-start.3
  159.9 17.0 %attend_backward.3 = (bf16[1,576,2304]{2,1,0:T(8,128)(2,1)}, f32[2,8,768]{2,1,0:T(8,128)}) custom-call(s32[2]{0:T(128)} %class_ref.13, bf16[2,576,768]{2,1,0:T(8,128)(2,1)} %get-tuple-element.167.refs_1_, bf16[2,576,768]{2,1,0:T(8,128)(2,1)} %get-tuple-element.168.refs_2_, bf16[2,576,768]{2,1,0:T(8,128)(2,1)} %get-tuple-element.169.refs_3_, ...), custom_call_target="tpu_custom_call" | custom-call | flops 10192158720 | bytes 6291456 | tf_op jit(solution)/shard_map/attend_backward/pallas_call | solution.py:818
  176.9 18.0 %joint_backward.1 = (bf16[2,576,768]{2,1,0:T(8,128)(2,1)}, bf16[16,12,8,768]{3,2,1,0:T(8,128)(2,1)}, bf16[16,12,8,768]{3,2,1,0:T(8,128)(2,1)}, f32[2,8,768]{2,1,0:T(8,128)}) custom-call(s32[1]{0:T(128)} %bitcast.core_ref, bf16[2,576,768]{2,1,0:T(8,128)(2,1)} %get-tuple-element.166.normed_ref, bf16[1,576,2304]{2,1,0:T(8,128)(2,1)} %get-tuple-element.174.grad_joint0_ref, ...), custom_call_target="tpu_custom_call" | custom-call | flops 9512681472 | bytes 26214400 | tf_op jit(solution)/shard_map/joint_backward/pallas_call | solution.py:919
  194.9 0.0 copy-start.1
  194.9 3.3 collective-permute-done.3.refs_4_
  198.2 4.9 %split_two.3 = (bf16[4,12,8,768]{3,2,1,0:T(8,128)(2,1)}, bf16[4,12,8,768]{3,2,1,0:T(8,128)(2,1)}, bf16[4,12,8,768]{3,2,1,0:T(8,128)(2,1)}, bf16[4,12,8,768]{3,2,1,0:T(8,128)(2,1)}) custom-call(s32[4]{0:T(128)} %pad_add_fusion.refs_0_, bf16[8,12,8,768]{3,2,1,0:T(8,128)(2,1)} %get-tuple-element.194.refs_1_, bf16[8,12,8,768]{3,2,1,0:T(8,128)(2,1)} %copy-done.1, ...), custom_call_target="tpu_custom_call" | custom-call | flops 2359296 | bytes 7077888 | tf_op jit(solution)/shard_map/split_two/pallas_call | solution.py:1494
  203.1 2.4 collective-permute-start.6
  205.5 6.9 %embed_weights.1 = (bf16[32,7,8,768]{3,2,1,0:T(8,128)(2,1)}, f32[8,768]{1,0:T(8,128)}) custom-call(s32[2]{0:T(128)} %class_ref.13, bf16[2,576,768]{2,1,0:T(8,128)(2,1)} %get-tuple-element.218.grad_tokens_ref, bf16[2,576,1024]{2,1,0:T(8,128)(2,1)} %get-tuple-element.200.stem_ref), custom_call_target="tpu_custom_call" | custom-call | flops 8000000000 | bytes 8388608 | tf_op jit(solution)/shard_map/embed_weights/pallas_call | solution.py:1018
  212.4 0.0 reduce-scatter.2.cloned.1.call-update
  212.4 6.6 %collective-permute-done.5.refs_2_ = bf16[4,12,8,768]{3,2,1,0:T(8,128)(2,1)S(1)} collective-permute-done((bf16[4,12,8,768]{3,2,1,0:T(8,128)(2,1)}, bf16[4,12,8,768]{3,2,1,0:T(8,128)(2,1)S(1)}, u32[]{:S(2)}, u32[]{:S(2)}) %collective-permute-start.5) | collective-permute-done | bytes 589856 | tf_op jit(solution)/shard_map/ppermute | solution.py:1650
  219.1 0.3 collective-permute-done.6.refs_4_
  219.4 0.5 copy-done.4
  219.9 0.3 copy-done.5
  220.2 3.6 %split_merged.2 = (bf16[2,24,8,768]{3,2,1,0:T(8,128)(2,1)}, bf16[2,24,8,768]{3,2,1,0:T(8,128)(2,1)}) custom-call(s32[4]{0:T(128)} %pad_add_fusion.refs_0_, bf16[4,12,8,768]{3,2,1,0:T(8,128)(2,1)} %get-tuple-element.213.refs_1_, bf16[4,12,8,768]{3,2,1,0:T(8,128)(2,1)} %copy-done.4, bf16[4,12,8,768]{3,2,1,0:T(8,128)(2,1)} %get-tuple-element.215.refs_3_, ...), custom_call_target="tpu_custom_call" | custom-call | flops 1179648 | bytes 3538944 | tf_op jit(solution)/shard_map/split_merged/pallas_call | solution.py:1527
  223.8 1.9 collective-permute-start.10
  225.8 4.4 %combine_core.2 = (bf16[4,12,8,768]{3,2,1,0:T(8,128)(2,1)}, bf16[4,12,8,768]{3,2,1,0:T(8,128)(2,1)}, bf16[4,12,8,768]{3,2,1,0:T(8,128)(2,1)}, bf16[4,12,8,768]{3,2,1,0:T(8,128)(2,1)}) custom-call(s32[1]{0:T(128)} %bitcast.8.refs_0_, bf16[16,12,8,768]{3,2,1,0:T(8,128)(2,1)} %get-tuple-element.210.refs_1_, bf16[16,12,8,768]{3,2,1,0:T(8,128)(2,1)} %collective-permute-done.4.refs_2_), custom_call_target="tpu_custom_call" | custom-call | flops 1179648 | bytes 7077888 | tf_op jit(solution)/shard_map/combine_core/pallas_call | solution.py:1458
  230.1 1.6 collective-permute-start.7
  231.7 1.5 collective-permute-start.8
  233.2 0.4 collective-permute-start.9
  233.6 15.3 %embed_backward.1 = (f32[2,576,1024]{2,1,0:T(8,128)}, bf16[2,576,1024]{2,1,0:T(8,128)(2,1)}, f32[2,8,1024]{2,1,0:T(8,128)}) custom-call(s32[2]{0:T(128)} %class_ref.13, bf16[2,576,768]{2,1,0:T(8,128)(2,1)} %get-tuple-element.218.grad_tokens_ref, f32[2,576,1024]{2,1,0:T(8,128)} %x_ref.5, f32[2,576,1024]{2,1,0:T(8,128)} %get-tuple-element.219.third_ref, ...), custom_call_target="tpu_custom_call" | custom-call | flops 20000000000 | bytes 31457280 | tf_op jit(solution)/shard_map/embed_backward/pallas_call | solution.py:1102
  248.9 0.0 copy-start.2
  249.0 9.9 %collective-permute-done.9.refs_4_ = bf16[4,12,8,768]{3,2,1,0:T(8,128)(2,1)S(1)} collective-permute-done((bf16[4,12,8,768]{3,2,1,0:T(8,128)(2,1)}, bf16[4,12,8,768]{3,2,1,0:T(8,128)(2,1)S(1)}, u32[]{:S(2)}, u32[]{:S(2)}) %collective-permute-start.9) | collective-permute-done | bytes 589856 | tf_op jit(solution)/shard_map/ppermute | solution.py:1650
  258.8 0.8 copy-done.6
  259.7 2.6 combine_plane.2
  262.3 0.3 collective-permute-start.12
  262.6 2.7 collective-permute-start.13
  265.3 1.4 collective-permute-start.14
  266.7 2.8 split_merged.3
  269.5 1.7 collective-permute-start.11
  271.1 21.4 %convs_backward.1 = (bf16[2,576,256]{2,1,0:T(8,128)(2,1)}, bf16[17,17,8,256]{3,2,1,0:T(8,128)(2,1)}, bf16[17,17,8,256]{3,2,1,0:T(8,128)(2,1)}, bf16[4,576,768]{2,1,0:T(8,128)(2,1)}) custom-call(s32[2]{0:T(128)} %class_ref.13, s32[1]{0:T(128)} %bitcast.core_ref, bf16[2,576,1024]{2,1,0:T(8,128)(2,1)} %get-tuple-element.234.grad_third_ref, ...), custom_call_target="tpu_custom_call" | custom-call | flops 20000000000 | bytes 20971520 | tf_op jit(solution)/shard_map/convs_backward/pallas_call | solution.py:1323
  292.6 4.5 %collective-permute-done.11 = bf16[1,24,8,768]{3,2,1,0:T(8,128)(2,1)S(1)} collective-permute-done((bf16[1,24,8,768]{3,2,1,0:T(8,128)(2,1)}, bf16[1,24,8,768]{3,2,1,0:T(8,128)(2,1)S(1)}, u32[]{:S(2)}, u32[]{:S(2)}) %collective-permute-start.11) | collective-permute-done | bytes 294944 | tf_op jit(solution)/shard_map/ppermute | solution.py:1650
  297.1 3.1 collective-permute-done.15.refs_2_
  300.1 1.0 copy-done
  301.2 2.9 combine_core.3
  304.1 1.3 collective-permute-start.16
  305.5 1.1 collective-permute-start.17
  306.6 1.1 collective-permute-start.18
  307.6 5.2 %input_backward.1 = f32[2,576,1024]{2,1,0:T(8,128)} custom-call(s32[2]{0:T(128)} %class_ref.13, f32[2,576,1024]{2,1,0:T(8,128)} %get-tuple-element.251.grad_inner_ref, bf16[2,576,256]{2,1,0:T(8,128)(2,1)} %get-tuple-element.252.grad_first_ref, bf16[1024,256]{1,0:T(8,128)(2,1)} %get-tuple-element.239.std_in_ref), custom_call_target="tpu_custom_call" | custom-call | flops 603979776 | bytes 12582912 | tf_op jit(solution)/shard_map/input_backward/pallas_call | solution.py:1411
  312.9 2.2 combine_depth.2
  315.1 2.2 collective-permute-done.17.refs_3_
  317.3 6.5 %collective-permute-done.18.refs_4_ = bf16[5,17,8,256]{3,2,1,0:T(8,128)(2,1)S(1)} collective-permute-done((bf16[5,17,8,256]{3,2,1,0:T(8,128)(2,1)}, bf16[5,17,8,256]{3,2,1,0:T(8,128)(2,1)S(1)}, u32[]{:S(2)}, u32[]{:S(2)}) %collective-permute-start.18) | collective-permute-done | bytes 348192 | tf_op jit(solution)/shard_map/ppermute | solution.py:1650
  323.8 0.7 copy-done.9
  324.6 2.2 combine_plane.3
  326.8 2.0 collective-permute-start.20
  328.7 2.4 collective-permute-start.21
  331.1 2.0 collective-permute-done.19.refs_2_
  333.2 5.8 %collective-permute-done.20.refs_3_ = bf16[31,8,256]{2,1,0:T(8,128)(2,1)S(1)} collective-permute-done((bf16[31,8,256]{2,1,0:T(8,128)(2,1)}, bf16[31,8,256]{2,1,0:T(8,128)(2,1)S(1)}, u32[]{:S(2)}, u32[]{:S(2)}) %collective-permute-start.20) | collective-permute-done | bytes 127008 | tf_op jit(solution)/shard_map/ppermute | solution.py:1650
  339.1 0.6 copy-done.15
  339.7 0.0 copy-done.16
  339.7 1.9 combine_depth.3
  (46 shorter events, 0.1 us)
Async XLA Ops:
  7.2 4.8 %copy-start.17 = (s32[8]{0:T(128)S(1)}, s32[8]{0:T(128)}, u32[]{:S(2)}) copy-start(s32[8]{0:T(128)} %param.31) | copy-start | bytes 100
  7.2 62.6 %all-to-all-start = ((bf16[4,576,768]{2,1,0:T(8,128)(2,1)}), bf16[4,576,768]{2,1,0:T(8,128)(2,1)}, u32[]{:S(2)}, u32[]{:S(2)}) async-start(bf16[4,576,768]{2,1,0:T(8,128)(2,1)} %bitcast.24), calls=%async_computation | async-start | bytes 7077888 | tf_op jit(solution)/shard_map/all_to_all | solution.py:1774
  124.9 23.2 %collective-permute-start = (bf16[16,12,8,768]{3,2,1,0:T(8,128)(2,1)}, bf16[16,12,8,768]{3,2,1,0:T(8,128)(2,1)}, u32[]{:S(2)}, u32[]{:S(2)}) collective-permute-start(bf16[16,12,8,768]{3,2,1,0:T(8,128)(2,1)} %get-tuple-element.177), channel_id=1, source_target_pairs={{0,1},{1,0},{2,3},{3,2},{4,5},{5,4},{6,7},{7,6},{8,9},{9,8},{10,11... | collective-permute-start | bytes 7077896 | tf_op jit(solution)/shard_map/ppermute | solution.py:1650
  125.5 22.7 %collective-permute-start.1 = (bf16[16,12,8,768]{3,2,1,0:T(8,128)(2,1)}, bf16[16,12,8,768]{3,2,1,0:T(8,128)(2,1)}, u32[]{:S(2)}, u32[]{:S(2)}) collective-permute-start(bf16[16,12,8,768]{3,2,1,0:T(8,128)(2,1)} %get-tuple-element.178), channel_id=1, source_target_pairs={{0,1},{1,0},{2,3},{3,2},{4,5},{5,4},{6,7},{7,6},{8,9},{9,8},{10,11... | collective-permute-start | bytes 7077896 | tf_op jit(solution)/shard_map/ppermute | solution.py:1650
  126.1 68.7 %all-to-all-start.1 = ((bf16[4,576,768]{2,1,0:T(8,128)(2,1)}), bf16[4,576,768]{2,1,0:T(8,128)(2,1)}, u32[]{:S(2)}, u32[]{:S(2)}) async-start(bf16[4,576,768]{2,1,0:T(8,128)(2,1)} %get-tuple-element.192), calls=%async_computation.1 | async-start | bytes 7077888 | tf_op jit(solution)/shard_map/all_to_all | solution.py:1821
  130.8 200.3 %reduce-scatter.2.cloned.1.call-start = ((), (), s32[]{:S(2)}) async-start(), calls=%async_computation.3 | async-start | bytes 2838528 | tf_op jit(solution)/shard_map/reduce_scatter | solution.py:1853
  155.0 39.8 %collective-permute-start.2 = (bf16[8,12,8,768]{3,2,1,0:T(8,128)(2,1)}, bf16[8,12,8,768]{3,2,1,0:T(8,128)(2,1)S(1)}, u32[]{:S(2)}, u32[]{:S(2)}) collective-permute-start(bf16[8,12,8,768]{3,2,1,0:T(8,128)(2,1)} %get-tuple-element.189), channel_id=1, source_target_pairs={{0,4},{1,5},{2,6},{3,7},{4,0},{5,1},{6,2},{7,3},{8,12},{9,13},{10,... | collective-permute-start | bytes 3538952 | tf_op jit(solution)/shard_map/ppermute | solution.py:1650
  157.9 40.3 %collective-permute-start.3 = (bf16[8,12,8,768]{3,2,1,0:T(8,128)(2,1)}, bf16[8,12,8,768]{3,2,1,0:T(8,128)(2,1)}, u32[]{:S(2)}, u32[]{:S(2)}) collective-permute-start(bf16[8,12,8,768]{3,2,1,0:T(8,128)(2,1)} %get-tuple-element.191), channel_id=1, source_target_pairs={{0,2},{1,3},{2,0},{3,1},{4,6},{5,7},{6,4},{7,5},{8,10},{9,11},{10,... | collective-permute-start | bytes 3538952 | tf_op jit(solution)/shard_map/ppermute | solution.py:1650
  194.9 3.4 copy-start.1
  198.2 21.2 %collective-permute-start.4 = (bf16[16,12,8,768]{3,2,1,0:T(8,128)(2,1)}, bf16[16,12,8,768]{3,2,1,0:T(8,128)(2,1)}, u32[]{:S(2)}, u32[]{:S(2)}) collective-permute-start(bf16[16,12,8,768]{3,2,1,0:T(8,128)(2,1)} %get-tuple-element.205), channel_id=1, source_target_pairs={{0,1},{1,0},{2,3},{3,2},{4,5},{5,4},{6,7},{7,6},{8,9},{9,8},{10,11... | collective-permute-start | bytes 7077896 | tf_op jit(solution)/shard_map/ppermute | solution.py:1650
  203.1 15.9 %collective-permute-start.5 = (bf16[4,12,8,768]{3,2,1,0:T(8,128)(2,1)}, bf16[4,12,8,768]{3,2,1,0:T(8,128)(2,1)S(1)}, u32[]{:S(2)}, u32[]{:S(2)}) collective-permute-start(bf16[4,12,8,768]{3,2,1,0:T(8,128)(2,1)} %get-tuple-element.206), channel_id=1, source_target_pairs={{0,2},{1,3},{2,0},{3,1},{4,6},{5,7},{6,4},{7,5},{8,10},{9,11},{10,... | collective-permute-start | bytes 1769480 | tf_op jit(solution)/shard_map/ppermute | solution.py:1650
  203.1 16.3 %collective-permute-start.6 = (bf16[4,12,8,768]{3,2,1,0:T(8,128)(2,1)}, bf16[4,12,8,768]{3,2,1,0:T(8,128)(2,1)S(1)}, u32[]{:S(2)}, u32[]{:S(2)}) collective-permute-start(bf16[4,12,8,768]{3,2,1,0:T(8,128)(2,1)} %get-tuple-element.208), channel_id=1, source_target_pairs={{0,4},{1,5},{2,6},{3,7},{4,0},{5,1},{6,2},{7,3},{8,12},{9,13},{10,... | collective-permute-start | bytes 1769480 | tf_op jit(solution)/shard_map/ppermute | solution.py:1650
  219.1 0.8 copy-start.4
  219.4 0.8 copy-start.5
  223.8 25.1 %collective-permute-start.10 = (bf16[2,24,8,768]{3,2,1,0:T(8,128)(2,1)}, bf16[2,24,8,768]{3,2,1,0:T(8,128)(2,1)}, u32[]{:S(2)}, u32[]{:S(2)}) collective-permute-start(bf16[2,24,8,768]{3,2,1,0:T(8,128)(2,1)} %get-tuple-element.225), channel_id=1, source_target_pairs={{0,8},{1,9},{2,10},{3,11},{4,12},{5,13},{6,14},{7,15},{8,0},{9,1},... | collective-permute-start | bytes 1769480 | tf_op jit(solution)/shard_map/ppermute | solution.py:1650
  230.1 18.8 %collective-permute-start.7 = (bf16[4,12,8,768]{3,2,1,0:T(8,128)(2,1)}, bf16[4,12,8,768]{3,2,1,0:T(8,128)(2,1)S(1)}, u32[]{:S(2)}, u32[]{:S(2)}) collective-permute-start(bf16[4,12,8,768]{3,2,1,0:T(8,128)(2,1)} %get-tuple-element.222), channel_id=1, source_target_pairs={{0,2},{1,3},{2,0},{3,1},{4,6},{5,7},{6,4},{7,5},{8,10},{9,11},{10,... | collective-permute-start | bytes 1769480 | tf_op jit(solution)/shard_map/ppermute | solution.py:1650
  231.7 17.3 %collective-permute-start.8 = (bf16[4,12,8,768]{3,2,1,0:T(8,128)(2,1)}, bf16[4,12,8,768]{3,2,1,0:T(8,128)(2,1)S(1)}, u32[]{:S(2)}, u32[]{:S(2)}) collective-permute-start(bf16[4,12,8,768]{3,2,1,0:T(8,128)(2,1)} %get-tuple-element.223), channel_id=1, source_target_pairs={{0,4},{1,5},{2,6},{3,7},{4,0},{5,1},{6,2},{7,3},{8,12},{9,13},{10,... | collective-permute-start | bytes 1769480 | tf_op jit(solution)/shard_map/ppermute | solution.py:1650
  233.2 25.7 %collective-permute-start.9 = (bf16[4,12,8,768]{3,2,1,0:T(8,128)(2,1)}, bf16[4,12,8,768]{3,2,1,0:T(8,128)(2,1)S(1)}, u32[]{:S(2)}, u32[]{:S(2)}) collective-permute-start(bf16[4,12,8,768]{3,2,1,0:T(8,128)(2,1)} %get-tuple-element.224), channel_id=1, source_target_pairs={{0,6},{1,7},{2,4},{3,5},{4,2},{5,3},{6,0},{7,1},{8,14},{9,15},{10,... | collective-permute-start | bytes 1769480 | tf_op jit(solution)/shard_map/ppermute | solution.py:1650
  248.9 9.9 %copy-start.2 = (bf16[4,12,8,768]{3,2,1,0:T(8,128)(2,1)}, bf16[4,12,8,768]{3,2,1,0:T(8,128)(2,1)S(1)}, u32[]{:S(2)}) copy-start(bf16[4,12,8,768]{3,2,1,0:T(8,128)(2,1)S(1)} %collective-permute-done.7.refs_2_) | copy-start | bytes 1769476
  249.0 9.9 %copy-start.3 = (bf16[4,12,8,768]{3,2,1,0:T(8,128)(2,1)}, bf16[4,12,8,768]{3,2,1,0:T(8,128)(2,1)S(1)}, u32[]{:S(2)}) copy-start(bf16[4,12,8,768]{3,2,1,0:T(8,128)(2,1)S(1)} %collective-permute-done.8.refs_3_) | copy-start | bytes 1769476
  258.8 0.8 copy-start.6
  262.3 30.2 %collective-permute-start.12 = (bf16[12,8,768]{2,1,0:T(8,128)(2,1)}, bf16[12,8,768]{2,1,0:T(8,128)(2,1)S(1)}, u32[]{:S(2)}, u32[]{:S(2)}) collective-permute-start(bf16[12,8,768]{2,1,0:T(8,128)(2,1)} %get-tuple-element.254), channel_id=1, source_target_pairs={{0,8},{1,9},{2,10},{3,11},{4,12},{5,13},{6,14},{7,15},{8,0},{9,1},... | collective-permute-start | bytes 442376 | tf_op jit(solution)/shard_map/ppermute | solution.py:1650
  262.6 30.0 %collective-permute-start.13 = (bf16[12,8,768]{2,1,0:T(8,128)(2,1)}, bf16[12,8,768]{2,1,0:T(8,128)(2,1)S(1)}, u32[]{:S(2)}, u32[]{:S(2)}) collective-permute-start(bf16[12,8,768]{2,1,0:T(8,128)(2,1)} %get-tuple-element.255), channel_id=1, source_target_pairs={{0,16},{1,17},{2,18},{3,19},{4,20},{5,21},{6,22},{7,23},{8,24},{9,... | collective-permute-start | bytes 442376 | tf_op jit(solution)/shard_map/ppermute | solution.py:1650
  265.3 27.3 %collective-permute-start.14 = (bf16[12,8,768]{2,1,0:T(8,128)(2,1)}, bf16[12,8,768]{2,1,0:T(8,128)(2,1)S(1)}, u32[]{:S(2)}, u32[]{:S(2)}) collective-permute-start(bf16[12,8,768]{2,1,0:T(8,128)(2,1)} %get-tuple-element.256), channel_id=1, source_target_pairs={{0,24},{1,25},{2,26},{3,27},{4,28},{5,29},{6,30},{7,31},{8,16},{9,... | collective-permute-start | bytes 442376 | tf_op jit(solution)/shard_map/ppermute | solution.py:1650
  269.5 27.6 %collective-permute-start.11 = (bf16[1,24,8,768]{3,2,1,0:T(8,128)(2,1)}, bf16[1,24,8,768]{3,2,1,0:T(8,128)(2,1)S(1)}, u32[]{:S(2)}, u32[]{:S(2)}) collective-permute-start(bf16[1,24,8,768]{3,2,1,0:T(8,128)(2,1)} %get-tuple-element.253), channel_id=1, source_target_pairs={{0,16},{1,17},{2,18},{3,19},{4,20},{5,21},{6,22},{7,23},{8,24},{9,... | collective-permute-start | bytes 884744 | tf_op jit(solution)/shard_map/ppermute | solution.py:1650
  292.5 20.4 %copy-start.11 = (bf16[12,8,768]{2,1,0:T(8,128)(2,1)}, bf16[12,8,768]{2,1,0:T(8,128)(2,1)S(1)}, u32[]{:S(2)}) copy-start(bf16[12,8,768]{2,1,0:T(8,128)(2,1)S(1)} %collective-permute-done.12.refs_3_) | copy-start | bytes 442372
  292.5 20.3 %copy-start.12 = (bf16[12,8,768]{2,1,0:T(8,128)(2,1)}, bf16[12,8,768]{2,1,0:T(8,128)(2,1)S(1)}, u32[]{:S(2)}) copy-start(bf16[12,8,768]{2,1,0:T(8,128)(2,1)S(1)} %collective-permute-done.13.refs_4_) | copy-start | bytes 442372
  292.6 20.3 %copy-start.13 = (bf16[12,8,768]{2,1,0:T(8,128)(2,1)}, bf16[12,8,768]{2,1,0:T(8,128)(2,1)S(1)}, u32[]{:S(2)}) copy-start(bf16[12,8,768]{2,1,0:T(8,128)(2,1)S(1)} %collective-permute-done.14.refs_5_) | copy-start | bytes 442372
  297.1 15.8 %copy-start.10 = (bf16[1,24,8,768]{3,2,1,0:T(8,128)(2,1)}, bf16[1,24,8,768]{3,2,1,0:T(8,128)(2,1)S(1)}, u32[]{:S(2)}) copy-start(bf16[1,24,8,768]{3,2,1,0:T(8,128)(2,1)S(1)} %collective-permute-done.11) | copy-start | bytes 884740
  297.1 3.1 collective-permute-start.15
  300.1 1.0 copy-start
  304.1 11.0 %collective-permute-start.16 = (bf16[5,17,8,256]{3,2,1,0:T(8,128)(2,1)}, bf16[5,17,8,256]{3,2,1,0:T(8,128)(2,1)S(1)}, u32[]{:S(2)}, u32[]{:S(2)}) collective-permute-start(bf16[5,17,8,256]{3,2,1,0:T(8,128)(2,1)} %get-tuple-element.268), channel_id=1, source_target_pairs={{0,2},{1,3},{2,0},{3,1},{4,6},{5,7},{6,4},{7,5},{8,10},{9,11},{10,... | collective-permute-start | bytes 1044488 | tf_op jit(solution)/shard_map/ppermute | solution.py:1650
  305.5 11.9 %collective-permute-start.17 = (bf16[5,17,8,256]{3,2,1,0:T(8,128)(2,1)}, bf16[5,17,8,256]{3,2,1,0:T(8,128)(2,1)S(1)}, u32[]{:S(2)}, u32[]{:S(2)}) collective-permute-start(bf16[5,17,8,256]{3,2,1,0:T(8,128)(2,1)} %get-tuple-element.269), channel_id=1, source_target_pairs={{0,4},{1,5},{2,6},{3,7},{4,0},{5,1},{6,2},{7,3},{8,12},{9,13},{10,... | collective-permute-start | bytes 1044488 | tf_op jit(solution)/shard_map/ppermute | solution.py:1650
  306.6 17.3 %collective-permute-start.18 = (bf16[5,17,8,256]{3,2,1,0:T(8,128)(2,1)}, bf16[5,17,8,256]{3,2,1,0:T(8,128)(2,1)S(1)}, u32[]{:S(2)}, u32[]{:S(2)}) collective-permute-start(bf16[5,17,8,256]{3,2,1,0:T(8,128)(2,1)} %get-tuple-element.270), channel_id=1, source_target_pairs={{0,6},{1,7},{2,4},{3,5},{4,2},{5,3},{6,0},{7,1},{8,14},{9,15},{10,... | collective-permute-start | bytes 1044488 | tf_op jit(solution)/shard_map/ppermute | solution.py:1650
  315.1 8.7 %copy-start.7 = (bf16[5,17,8,256]{3,2,1,0:T(8,128)(2,1)}, bf16[5,17,8,256]{3,2,1,0:T(8,128)(2,1)S(1)}, u32[]{:S(2)}) copy-start(bf16[5,17,8,256]{3,2,1,0:T(8,128)(2,1)S(1)} %collective-permute-done.16.refs_2_) | copy-start | bytes 1044484
  317.3 6.5 %copy-start.8 = (bf16[5,17,8,256]{3,2,1,0:T(8,128)(2,1)}, bf16[5,17,8,256]{3,2,1,0:T(8,128)(2,1)S(1)}, u32[]{:S(2)}) copy-start(bf16[5,17,8,256]{3,2,1,0:T(8,128)(2,1)S(1)} %collective-permute-done.17.refs_3_) | copy-start | bytes 1044484
  323.8 0.7 copy-start.9
  326.8 6.4 %collective-permute-start.19 = (bf16[31,8,256]{2,1,0:T(8,128)(2,1)}, bf16[31,8,256]{2,1,0:T(8,128)(2,1)S(1)}, u32[]{:S(2)}, u32[]{:S(2)}) collective-permute-start(bf16[31,8,256]{2,1,0:T(8,128)(2,1)} %get-tuple-element.276), channel_id=1, source_target_pairs={{0,8},{1,9},{2,10},{3,11},{4,12},{5,13},{6,14},{7,15},{8,0},{9,1},... | collective-permute-start | bytes 380936 | tf_op jit(solution)/shard_map/ppermute | solution.py:1650
  326.8 12.3 %collective-permute-start.20 = (bf16[31,8,256]{2,1,0:T(8,128)(2,1)}, bf16[31,8,256]{2,1,0:T(8,128)(2,1)S(1)}, u32[]{:S(2)}, u32[]{:S(2)}) collective-permute-start(bf16[31,8,256]{2,1,0:T(8,128)(2,1)} %get-tuple-element.277), channel_id=1, source_target_pairs={{0,16},{1,17},{2,18},{3,19},{4,20},{5,21},{6,22},{7,23},{8,24},{9,... | collective-permute-start | bytes 380936 | tf_op jit(solution)/shard_map/ppermute | solution.py:1650
  328.7 10.3 %collective-permute-start.21 = (bf16[31,8,256]{2,1,0:T(8,128)(2,1)}, bf16[31,8,256]{2,1,0:T(8,128)(2,1)S(1)}, u32[]{:S(2)}, u32[]{:S(2)}) collective-permute-start(bf16[31,8,256]{2,1,0:T(8,128)(2,1)} %get-tuple-element.278), channel_id=1, source_target_pairs={{0,24},{1,25},{2,26},{3,27},{4,28},{5,29},{6,30},{7,31},{8,16},{9,... | collective-permute-start | bytes 380936 | tf_op jit(solution)/shard_map/ppermute | solution.py:1650
  333.2 5.9 %copy-start.14 = (bf16[31,8,256]{2,1,0:T(8,128)(2,1)}, bf16[31,8,256]{2,1,0:T(8,128)(2,1)S(1)}, u32[]{:S(2)}) copy-start(bf16[31,8,256]{2,1,0:T(8,128)(2,1)S(1)} %collective-permute-done.19.refs_2_) | copy-start | bytes 380932
  339.0 0.7 copy-start.15
  339.0 0.7 copy-start.16
Sparse Core Ops, SparseCore 0:
  212.6 113.1 reduce-scatter.1
